TPU v7x, 32 devices: a whole 2x2x4 slice. The times are simulated.
32 devices in a mesh: seq: 16 (over z, x, core), head: 2 (over y).
Axes of the slice: x: 2, y: 2, z: 4, core: 2. Of those that a mesh axis runs over, the one named last changes fastest.
Arguments:
- loaded: bfloat16 [2048, 2048], P('seq', 'head'), may hold values from -6 to 6
- out_grad: bfloat16 [2048, 512], P('seq', 'head'), may hold values from -6 to 6
- w_query: bfloat16 [2048, 512], P(None, 'head'), may hold values from -0.125 to 0.125
- w_key: bfloat16 [2048, 512], P(None, 'head'), may hold values from -0.125 to 0.125
- w_value: bfloat16 [2048, 512], P(None, 'head'), may hold values from -0.125 to 0.125
- w_beta: bfloat16 [2048, 4], P(None, 'head'), may hold values from -0.125 to 0.125
- beta_max: float32 [4], P('head'), may hold values from 0.0625 to 1
- out_gain: float32 [128], replicated, may hold values from 0.1 to 1.9
- clip_lengths: int32 [16], replicated, may hold values from 1 to 512, 2048 in all
- delay_offsets: int32 [4], replicated, may hold values from 0 to 3, each once
- block_order: int32 [16, 16], P('seq'), may hold values from 0 to 15, each once within a row
Outputs:
- head_out: bfloat16 [2048, 512], P('seq', 'head')
- input_grad: bfloat16 [2048, 2048], P('seq', 'head')
Inputs may be any that keep to these rules, and one draw needn't show every extreme that they name: `clip_lengths`: the clip lengths sum to 2048; the longest is exactly 512. `delay_offsets`: each codebook has a different delay. `block_order`: each row is a permutation of 0 to 15.
All inputs are finite; a program needn't handle non-finite values.
Results may differ from a plain program's by a relative error of at most 0.022.
Values may be sent and summed in bfloat16 or wider, within the bound.
No kernel may reach another device: no remote copies, remote signals or barrier semaphores. Data moves between devices by JAX's collectives and lax.ppermute only.
A program may use at most 128 MiB of HBM per device.

v0:
```python
import jax
import jax.numpy as jnp
from jax import lax
from jax.sharding import PartitionSpec as P

SPAN = 128


EPSILON = 1e-06
HIGHEST = lax.Precision.HIGHEST


def from_behind(x, axis, by):
    count = lax.axis_size(axis)
    pairs = [(i, i + by) for i in range(count) if 0 <= i + by < count]
    return lax.ppermute(x, axis, pairs)


def prefix(x, axis, join, neutral):
    place = lax.axis_index(axis)
    gathered = jax.tree.map(
        lambda a, kind: lax.all_gather(a.astype(kind), axis), x, (jnp.bfloat16, jnp.bfloat16)
    )
    state = jax.tree.map(lambda a, e: jnp.zeros_like(a) + jnp.asarray(e, a.dtype), x, neutral)

    def one(turn, state):
        return join(
            state,
            jax.tree.map(
                lambda a, own: lax.dynamic_index_in_dim(a, turn, 0, False).astype(own.dtype),
                gathered,
                x,
            ),
        )

    return lax.fori_loop(0, place, one, state)


def prefix_2(x, axis, combine, identity):
    count, here = (lax.axis_size(axis), lax.axis_index(axis))
    everything = jax.tree.map(
        lambda part, kind: lax.all_gather(part.astype(kind), axis),
        x,
        jax.tree.map(lambda a: jnp.bfloat16 if a.dtype == jnp.float32 else a.dtype, x),
    )
    start = jax.tree.map(
        lambda part, zero: jnp.broadcast_to(jnp.asarray(zero, part.dtype), part.shape), x, identity
    )

    def turn(k, before):
        at = count - 1 - k
        reached = at > here
        new = combine(
            before, jax.tree.map(lambda part, own: part[at].astype(own.dtype), everything, x)
        )
        return jax.tree.map(lambda a, b: jnp.where(reached, a, b), new, before)

    return lax.fori_loop(0, count, turn, start)


def clip_start(clip_lengths, positions):
    clip_ends = jnp.cumsum(clip_lengths)
    finished = clip_ends[None, :] <= positions[:, None]
    return jnp.sum(jnp.where(finished, clip_lengths[None, :], 0), axis=1)


def column_delays(delay_offsets, columns, group_width):
    codebook = columns // group_width
    matches = codebook[:, None] == jnp.arange(delay_offsets.shape[0], dtype=jnp.int32)[None, :]
    return jnp.sum(jnp.where(matches, delay_offsets[None, :], 0), axis=1)


def prepare(q_raw, k_raw, logit, rate_cap):
    query_rows = q_raw / jnp.sqrt(jnp.sum(q_raw * q_raw, axis=-1, keepdims=True) + EPSILON)
    key_rows = k_raw / jnp.sqrt(jnp.sum(k_raw * k_raw, axis=-1, keepdims=True) + EPSILON)
    beta_rate = rate_cap * jax.nn.sigmoid(logit[:, 0])
    return (query_rows, key_rows, beta_rate)


def span_terms(key_rows, value_rows, beta_rate, clip_begin, span_first):
    span_len = key_rows.shape[0]
    key_width = key_rows.shape[1]
    same_clip = (clip_begin[:, None] == clip_begin[None, :]).astype(jnp.float32)
    gram = beta_rate[:, None] * jnp.dot(key_rows, key_rows.T, precision=HIGHEST) * same_clip
    system = jnp.eye(span_len, dtype=jnp.float32) + jnp.tril(gram, -1)
    stacked = beta_rate[:, None] * jnp.concatenate([key_rows, value_rows], axis=1)
    solved = jax.scipy.linalg.solve_triangular(system, stacked, lower=True, unit_diagonal=True)
    carried = (clip_begin < span_first).astype(jnp.float32)
    final_mask = (clip_begin == clip_begin[-1]).astype(jnp.float32)
    return (solved[:, :key_width], solved[:, key_width:], carried, final_mask, same_clip)


def span_output(state_in, pieces):
    query_rows, key_rows, value_rows, beta_rate, clip_begin, span_first = pieces
    key_part, value_part, carried, final_mask, same_clip = span_terms(
        key_rows, value_rows, beta_rate, clip_begin, span_first
    )
    refreshed = value_part - carried[:, None] * jnp.dot(key_part, state_in, precision=HIGHEST)
    scores = jnp.tril(jnp.dot(query_rows, key_rows.T, precision=HIGHEST)) * same_clip
    outputs = carried[:, None] * jnp.dot(query_rows, state_in, precision=HIGHEST) + jnp.dot(
        scores, refreshed, precision=HIGHEST
    )
    state_out = carried[-1] * state_in + jnp.dot(
        key_rows.T, final_mask[:, None] * refreshed, precision=HIGHEST
    )
    return (state_out, outputs)


def affine_step(affine, pieces):
    key_rows, value_rows, beta_rate, clip_begin, span_first = pieces
    key_part, value_part, carried, final_mask, same_clip = span_terms(
        key_rows, value_rows, beta_rate, clip_begin, span_first
    )
    widened = jnp.concatenate(
        [jnp.zeros((key_rows.shape[0], key_rows.shape[1]), jnp.float32), value_part], axis=1
    )
    refreshed = widened - carried[:, None] * jnp.dot(key_part, affine, precision=HIGHEST)
    return (
        carried[-1] * affine
        + jnp.dot(key_rows.T, final_mask[:, None] * refreshed, precision=HIGHEST),
        None,
    )


def run_head(q_raw, k_raw, v_raw, logit, rate_cap, out_gain, clip_begin, positions, state_in):
    query_rows, key_rows, beta_rate = prepare(q_raw, k_raw, logit, rate_cap)
    span_count = q_raw.shape[0] // SPAN
    pieces = (
        query_rows.reshape(span_count, SPAN, -1),
        key_rows.reshape(span_count, SPAN, -1),
        v_raw.reshape(span_count, SPAN, -1),
        beta_rate.reshape(span_count, SPAN),
        clip_begin.reshape(span_count, SPAN),
        positions.reshape(span_count, SPAN)[:, 0],
    )
    state_out, outputs = lax.scan(span_output, state_in, pieces)
    raw_out = outputs.reshape(-1, outputs.shape[-1])
    normed = (
        raw_out
        / jnp.sqrt(jnp.mean(raw_out * raw_out, axis=-1, keepdims=True) + EPSILON)
        * out_gain[None, :]
    )
    return (normed, state_out)


def compose(before_map, after_map):
    return (
        jnp.matmul(after_map[0], before_map[0], precision=HIGHEST),
        jnp.matmul(after_map[0], before_map[1], precision=HIGHEST) + after_map[1],
    )


def back_product(gradient, weight):
    return lax.dot_general(
        gradient, weight, (((1,), (1,)), ((), ())), preferred_element_type=jnp.float32
    )


def split_heads(matrix, heads_local):
    return matrix.reshape(matrix.shape[0], heads_local, -1).transpose(1, 0, 2)


def join_heads(stacked):
    return stacked.transpose(1, 0, 2).reshape(stacked.shape[1], -1)


def on_device(
    loaded,
    out_grad,
    w_query,
    w_key,
    w_value,
    w_beta,
    beta_max,
    out_gain,
    clip_lengths,
    delay_offsets,
    block_order,
):
    sources = lax.axis_size("seq")
    frames = loaded.shape[0]
    local_width = loaded.shape[1]
    block_rows = frames // sources
    received = lax.all_to_all(
        loaded.reshape(sources, block_rows, local_width),
        "seq",
        split_axis=0,
        concat_axis=0,
        tiled=True,
    )
    inverse = jnp.argsort(block_order[0])
    arranged = jnp.take(received, inverse, axis=0).reshape(frames, local_width)
    positions = lax.axis_index("seq") * frames + jnp.arange(frames, dtype=jnp.int32)
    clip_begin = clip_start(clip_lengths, positions)
    codebooks = delay_offsets.shape[0]
    delay_reach = codebooks - 1
    full_width = local_width * lax.axis_size("head")
    columns = lax.axis_index("head") * local_width + jnp.arange(local_width, dtype=jnp.int32)
    col_delay = column_delays(delay_offsets, columns, full_width // codebooks)
    earlier = from_behind(arranged[frames - delay_reach :], "seq", 1)
    extended = jnp.concatenate([earlier, arranged], axis=0)
    delayed = jnp.zeros((frames, local_width), jnp.bfloat16)
    for shift_by in range(codebooks):
        shifted = extended[delay_reach - shift_by : delay_reach - shift_by + frames]
        inside = positions - shift_by >= clip_begin
        delayed = jnp.where((col_delay[None, :] == shift_by) & inside[:, None], shifted, delayed)
    heads_local = w_beta.shape[1]
    key_width = w_query.shape[1] // heads_local
    value_width = w_value.shape[1] // heads_local
    empty = (
        jnp.zeros((frames, w_query.shape[1]), jnp.float32),
        jnp.zeros((frames, w_key.shape[1]), jnp.float32),
        jnp.zeros((frames, w_value.shape[1]), jnp.float32),
        jnp.zeros((frames, heads_local), jnp.float32),
    )
    feature_part = lax.all_gather(delayed, "head", axis=1, tiled=True)
    results = []
    for running, weight in zip(empty, (w_query, w_key, w_value, w_beta)):
        results.append(jnp.dot(feature_part, weight, preferred_element_type=jnp.float32))
    q_flat, k_flat, v_flat, logit_flat = tuple(results)
    q_heads = split_heads(q_flat, heads_local)
    k_heads = split_heads(k_flat, heads_local)
    v_heads = split_heads(v_flat, heads_local)
    logit_heads = split_heads(logit_flat, heads_local)
    span_count = frames // SPAN
    start_affine = jnp.concatenate(
        [jnp.eye(key_width, dtype=jnp.float32), jnp.zeros((key_width, value_width), jnp.float32)],
        axis=1,
    )

    def head_affine(q_one, k_one, v_one, logit_one, rate_cap):
        query_rows, key_rows, beta_rate = prepare(q_one, k_one, logit_one, rate_cap)
        map_pieces = (
            key_rows.reshape(span_count, SPAN, -1),
            v_one.reshape(span_count, SPAN, -1),
            beta_rate.reshape(span_count, SPAN),
            clip_begin.reshape(span_count, SPAN),
            positions.reshape(span_count, SPAN)[:, 0],
        )
        affine, _ = lax.scan(affine_step, start_affine, map_pieces)
        return affine

    affine = jax.vmap(head_affine)(q_heads, k_heads, v_heads, logit_heads, beta_max)
    transition = affine[:, :, :key_width]
    offset_map = affine[:, :, key_width:]
    identity = (
        jnp.broadcast_to(
            jnp.eye(key_width, dtype=jnp.float32), (heads_local, key_width, key_width)
        ),
        jnp.zeros((heads_local, key_width, value_width), jnp.float32),
    )
    _, state_in = prefix((transition, offset_map), "seq", compose, identity)

    def forward(query_in, key_in, value_in, logit_in, state_start):

        def one_head(q_one, k_one, v_one, logit_one, rate_cap, state_one):
            return run_head(
                q_one, k_one, v_one, logit_one, rate_cap, out_gain, clip_begin, positions, state_one
            )

        return jax.vmap(one_head)(query_in, key_in, value_in, logit_in, beta_max, state_start)

    (normed, state_out), pullback = jax.vjp(
        forward, q_heads, k_heads, v_heads, logit_heads, state_in
    )
    head_out = join_heads(normed).astype(jnp.bfloat16)
    cotangent = split_heads(out_grad, heads_local).astype(jnp.float32)
    first_pass = pullback((cotangent, jnp.zeros_like(state_out)))
    _, state_grad = prefix_2(
        (jnp.swapaxes(transition, 1, 2), first_pass[4]), "seq", compose, identity
    )
    second_pass = pullback((jnp.zeros_like(normed), state_grad))
    gradients = [
        join_heads(first_pass[index] + second_pass[index]).astype(jnp.bfloat16)
        for index in range(4)
    ]
    partial_sum = back_product(gradients[0], w_query) + back_product(gradients[1], w_key)
    partial_sum = (
        partial_sum + back_product(gradients[2], w_value) + back_product(gradients[3], w_beta)
    )
    summed = lax.psum_scatter(
        partial_sum.astype(jnp.bfloat16), "head", scatter_dimension=1, tiled=True
    )
    following = from_behind(summed[:delay_reach], "seq", -1)
    extended_grad = jnp.concatenate([summed, following], axis=0)
    input_grad = jnp.zeros((frames, local_width), jnp.bfloat16)
    for shift_by in range(codebooks):
        ahead = extended_grad[shift_by : shift_by + frames]
        inside = clip_start(clip_lengths, positions + shift_by) <= positions
        input_grad = jnp.where(
            (col_delay[None, :] == shift_by) & inside[:, None], ahead, input_grad
        )
    return (head_out, input_grad)


def solution(mesh):
    return jax.shard_map(
        on_device,
        mesh=mesh,
        in_specs=(
            P("seq", "head"),
            P("seq", "head"),
            P(None, "head"),
            P(None, "head"),
            P(None, "head"),
            P(None, "head"),
            P("head"),
            P(),
            P(),
            P(),
            P("seq", None),
        ),
        out_specs=(P("seq", "head"), P("seq", "head")),
        check_vma=False,
    )
```

profile of v0, /device:TPU:0, one launch (start us, length us, event | category | flops | bytes accessed | tf_op | source)
XLA Modules:
  0.0 285.4 jit_solution(18326170858271973493)
XLA Ops:
  7.2 7.5 %all-to-all-start = ((bf16[16,8,1024]{2,1,0:T(8,128)(2,1)}), bf16[16,8,1024]{2,1,0:T(8,128)(2,1)S(1)}, u32[]{:S(2)}, u32[]{:S(2)}) async-start(bf16[16,8,1024]{2,1,0:T(8,128)(2,1)} %bitcast.208), calls=%async_computation | async-start | bytes 524288 | tf_op jit(solution)/shard_map/all_to_all | solution.py:184
  15.4 1.2 sort.17
  19.6 1.9 fusion.109
  22.7 1.3 broadcast_multiply_fusion.2
  25.4 2.1 collective-permute-start
  27.5 0.8 collective-permute-done
  28.9 9.3 %all_gather.27 = bf16[128,2048]{1,0:T(8,128)(2,1)S(1)} all-gather(bf16[128,1024]{1,0:T(8,128)(2,1)S(1)} %and_select_fusion.7), channel_id=1, replica_groups=mesh['seq'=16,'head'=2] {'head'}, dimensions={1}, use_global_device_ids=true | all-gather | bytes 786432 | tf_op jit(solution)/shard_map/all_gather | solution.py:216
  40.6 0.8 bitcast_multiply_fusion.1
  42.1 19.7 %custom-call.10 = f32[2,1,128,128]{2,3,1,0:T(8,128)S(1)} custom-call(f32[2,1,128,128]{3,2,1,0:T(8,128)S(1)} %add_bitcast_fusion), custom_call_target="InvertDiagBlocksLowerTriangular" | custom-call | tf_op jit(solution)/shard_map/vmap()/while/body/eval_jaxpr/jit(_solve_triangular)/triangular_solve/custom-call.1 | solution.py:87
  61.8 1.7 fusion.116
  64.7 0.9 copy-done.17
  68.6 0.8 copy.146
  73.8 1.0 convolution_multiply_fusion.2
  76.0 31.0 %all-gather.9.cloned.1.call-done = bf16[32,128,128]{2,1,0:T(8,128)(2,1)} async-done(((bf16[2,128,128]{2,1,0:T(8,128)(2,1)}), bf16[32,128,128]{2,1,0:T(8,128)(2,1)}) %all-gather.9.cloned.1.call-update) | async-done | bytes 1048592 | tf_op jit(solution)/shard_map/all_gather | solution.py:22
  107.0 39.6 %all-gather.11.cloned.1.call-done = bf16[32,128,128]{2,1,0:T(8,128)(2,1)} async-done(((bf16[2,128,128]{2,1,0:T(8,128)(2,1)}), bf16[32,128,128]{2,1,0:T(8,128)(2,1)}) %all-gather.11.cloned.1.call-update) | async-done | bytes 1048592 | tf_op jit(solution)/shard_map/all_gather | solution.py:22
  150.9 1.2 fusion.55
  152.5 1.1 fusion.26
  153.6 1.9 fusion.23
  155.5 1.1 fusion.22
  157.0 1.1 fusion.68
  160.9 1.1 fusion.65
  162.5 1.1 fusion.34
  164.2 1.5 fusion.117
  165.7 20.0 %all-gather.13.cloned.1.call-done = bf16[32,128,128]{2,1,0:T(8,128)(2,1)} async-done(((bf16[2,128,128]{2,1,0:T(8,128)(2,1)}), bf16[32,128,128]{2,1,0:T(8,128)(2,1)}) %all-gather.13.cloned.1.call-update) | async-done | bytes 1048592 | tf_op jit(solution)/shard_map/all_gather | solution.py:42
  185.7 39.5 %all-gather.15.cloned.1.call-done = bf16[32,128,128]{2,1,0:T(8,128)(2,1)} async-done(((bf16[2,128,128]{2,1,0:T(8,128)(2,1)}), bf16[32,128,128]{2,1,0:T(8,128)(2,1)}) %all-gather.15.cloned.1.call-update) | async-done | bytes 1048592 | tf_op jit(solution)/shard_map/all_gather | solution.py:42
  225.2 18.3 %while.26 = (s32[]{:T(128)}, f32[2,128,128]{2,1,0:T(8,128)S(1)}, s32[]{:T(128)}, bf16[16,2,128,128]{3,2,1,0:T(8,128)(2,1)}, bf16[16,2,128,128]{3,2,1,0:T(8,128)(...) while((s32[]{:T(128)}, f32[2,128,128]{2,1,0:T(8,128)S(1)}, s32[]{:T(128)}, ...), condition=%wide.region_16.19_spmd.clone, body=%wide.region_15.18_spmd.clone.sunk | while | flops 50495496 | bytes 789149 | solution.py:58
  225.2 1.1 fusion.168
  226.3 1.1 fusion.168
  227.5 1.1 fusion.168
  228.6 1.1 fusion.168
  229.8 1.1 fusion.168
  230.9 1.1 fusion.168
  232.1 1.1 fusion.168
  233.2 1.1 fusion.168
  234.4 1.1 fusion.168
  235.5 1.1 fusion.168
  236.7 1.1 fusion.168
  237.8 1.1 fusion.168
  239.0 1.1 fusion.168
  240.1 1.1 fusion.168
  241.3 1.1 fusion.168
  242.4 1.1 fusion.168
  249.4 0.8 copy-done.13
  258.2 1.2 fusion.11
  263.1 10.0 %reduce-scatter.2.cloned.1.call-done = bf16[128,1024]{1,0:T(8,128)(2,1)} async-done(((bf16[128,2048]{1,0:T(8,128)(2,1)}), bf16[128,1024]{1,0:T(8,128)(2,1)}) %reduce-scatter.2.cloned.1.call-update) | async-done | bytes 262160 | tf_op jit(solution)/shard_map/reduce_scatter | solution.py:281
  273.8 1.4 collective-permute-start.1
  275.3 1.0 constant_dynamic-update-slice_fusion.1
  277.7 1.2 and_select_fusion.3
  (299 shorter events, 46.9 us)
Async XLA Ops:
  7.2 64.8 %copy-start = (bf16[2048,256]{1,0:T(8,128)(2,1)S(1)}, bf16[2048,256]{1,0:T(8,128)(2,1)}, u32[]{:S(2)}) copy-start(bf16[2048,256]{1,0:T(8,128)(2,1)} %param.23) | copy-start | bytes 3145732
  7.2 17.6 %all-to-all-start = ((bf16[16,8,1024]{2,1,0:T(8,128)(2,1)}), bf16[16,8,1024]{2,1,0:T(8,128)(2,1)S(1)}, u32[]{:S(2)}, u32[]{:S(2)}) async-start(bf16[16,8,1024]{2,1,0:T(8,128)(2,1)} %bitcast.208), calls=%async_computation | async-start | bytes 524288 | tf_op jit(solution)/shard_map/all_to_all | solution.py:184
  14.7 92.3 %all-gather.9.cloned.1.call-start = ((), (), s32[]{:S(2)}) async-start(), calls=%async_computation.3 | async-start | bytes 1114112 | tf_op jit(solution)/shard_map/all_gather | solution.py:22
  24.2 4.1 %copy-start.48 = (pred[1024]{0:T(1024)(128)(4,1)}, pred[1024]{0:T(1024)(128)(4,1)S(1)}, u32[]{:S(2)}) copy-start(pred[1024]{0:T(1024)(128)(4,1)S(1)} %get-tuple-element.986) | copy-start | bytes 3076
  24.2 4.1 %copy-start.50 = (pred[1024]{0:T(1024)(128)(4,1)}, pred[1024]{0:T(1024)(128)(4,1)S(1)}, u32[]{:S(2)}) copy-start(pred[1024]{0:T(1024)(128)(4,1)S(1)} %get-tuple-element.987) | copy-start | bytes 3076
  24.2 4.1 %copy-start.52 = (pred[1024]{0:T(1024)(128)(4,1)}, pred[1024]{0:T(1024)(128)(4,1)S(1)}, u32[]{:S(2)}) copy-start(pred[1024]{0:T(1024)(128)(4,1)S(1)} %get-tuple-element.988) | copy-start | bytes 3076
  24.2 4.1 %copy-start.54 = (pred[1024]{0:T(1024)(128)(4,1)}, pred[1024]{0:T(1024)(128)(4,1)S(1)}, u32[]{:S(2)}) copy-start(pred[1024]{0:T(1024)(128)(4,1)S(1)} %get-tuple-element.989) | copy-start | bytes 3076
  24.3 50.6 %copy-start.4 = (f32[128,128]{1,0:T(8,128)}, f32[128,128]{1,0:T(8,128)S(1)}, u32[]{:S(2)}) copy-start(f32[128,128]{1,0:T(8,128)S(1)} %compare_convert_fusion) | copy-start | bytes 196612
  25.3 12.8 %copy-start.1 = (bf16[2048,256]{1,0:T(8,128)(2,1)S(1)}, bf16[2048,256]{1,0:T(8,128)(2,1)}, u32[]{:S(2)}) copy-start(bf16[2048,256]{1,0:T(8,128)(2,1)} %param.24) | copy-start | bytes 3145732
  25.4 2.9 %collective-permute-start = (bf16[3,1024]{1,0:T(4,128)(2,1)S(1)}, bf16[3,1024]{1,0:T(4,128)(2,1)S(1)}, u32[]{:S(2)}, u32[]{:S(2)}) collective-permute-start(bf16[3,1024]{1,0:T(4,128)(2,1)S(1)} %slice.106), channel_id=1, source_target_pairs={{0,2},{2,4},{4,6},{6,8},{8,10},{10,12},{12,14},{14,16},{16,18},{18... | collective-permute-start | bytes 18440 | tf_op jit(solution)/shard_map/ppermute | solution.py:16
  39.8 1.6 copy-start.22
  40.5 23.0 %copy-start.7 = (f32[2,128,128]{1,2,0:T(8,128)}, f32[2,128,128]{1,2,0:T(8,128)S(1)}, u32[]{:S(2)}) copy-start(f32[2,128,128]{1,2,0:T(8,128)S(1)} %bitcast_divide_fusion.4) | copy-start | bytes 393220
  63.5 1.1 copy-start.10
  67.7 78.9 %all-gather.11.cloned.1.call-start = ((), (), s32[]{:S(2)}) async-start(), calls=%async_computation.4 | async-start | bytes 1114112 | tf_op jit(solution)/shard_map/all_gather | solution.py:22
  68.4 117.2 %all-gather.13.cloned.1.call-start = ((), (), s32[]{:S(2)}) async-start(), calls=%async_computation.5 | async-start | bytes 1114112 | tf_op jit(solution)/shard_map/all_gather | solution.py:42
  68.6 2.7 copy-start.15
  73.1 74.4 %copy-start.45 = (f32[2,128]{1,0:T(2,128)}, f32[2,128]{1,0:T(2,128)S(1)}, u32[]{:S(2)}) copy-start(f32[2,128]{1,0:T(2,128)S(1)} %get-tuple-element.996) | copy-start | bytes 3076
  74.9 150.3 %all-gather.15.cloned.1.call-start = ((), (), s32[]{:S(2)}) async-start(), calls=%async_computation.6 | async-start | bytes 1114112 | tf_op jit(solution)/shard_map/all_gather | solution.py:42
  76.0 71.9 %copy-start.24 = (f32[2,128,128]{2,1,0:T(8,128)}, f32[2,128,128]{2,1,0:T(8,128)S(1)}, u32[]{:S(2)}) copy-start(f32[2,128,128]{2,1,0:T(8,128)S(1)} %fusion.25) | copy-start | bytes 393220
  147.9 0.9 copy-start.9
  149.9 1.0 copy-start.69
  149.9 1.0 copy-start.79
  150.9 1.2 copy-start.25
  150.9 1.2 copy-start.27
  153.5 2.0 copy-start.5
  153.5 2.0 copy-start.31
  153.5 2.0 copy-start.70
  153.6 2.0 copy-start.80
  153.6 2.0 copy-start.85
  156.7 116.4 %reduce-scatter.2.cloned.1.call-start = ((), (), s32[]{:S(2)}) async-start(), calls=%async_computation.2 | async-start | bytes 786432 | tf_op jit(solution)/shard_map/reduce_scatter | solution.py:281
  156.9 1.1 copy-start.19
  156.9 1.1 copy-start.28
  156.9 1.1 copy-start.35
  160.9 1.1 copy-start.40
  244.2 0.9 copy-start.81
  244.2 0.9 copy-start.86
  247.2 1.0 copy-start.11
  247.2 1.0 copy-start.44
  249.4 1.0 copy-start.18
  249.4 1.0 copy-start.47
  251.2 1.0 copy-start.23
  253.2 2.6 copy-start.2
  255.8 1.2 copy-start.3
  273.8 3.2 %copy-start.14 = (bf16[128,1024]{1,0:T(8,128)(2,1)S(1)}, bf16[128,1024]{1,0:T(8,128)(2,1)}, u32[]{:S(2)}) copy-start(bf16[128,1024]{1,0:T(8,128)(2,1)} %reduce-scatter.2.cloned.1.call-done) | copy-start | bytes 786436
  273.8 3.2 %collective-permute-start.1 = (bf16[3,1024]{1,0:T(4,128)(2,1)S(1)}, bf16[3,1024]{1,0:T(4,128)(2,1)S(1)}, u32[]{:S(2)}, u32[]{:S(2)}) collective-permute-start(bf16[3,1024]{1,0:T(4,128)(2,1)S(1)} %slice.115), channel_id=1, source_target_pairs={{2,0},{4,2},{6,4},{8,6},{10,8},{12,10},{14,12},{16,14},{18,16},{20... | collective-permute-start | bytes 18440 | tf_op jit(solution)/shard_map/ppermute | solution.py:16
  275.3 1.8 copy-start.51
  275.3 1.8 copy-start.53
  275.3 1.8 copy-start.55
  (52 other events, 36.9 us)
Sparse Core Ops, SparseCore 0:
  67.8 39.1 all-gather.8
  109.7 36.8 all-gather.10
  148.8 36.8 all-gather.12
  188.2 36.8 all-gather.14
  259.6 13.4 reduce-scatter.1
where the time goes:
time: 289 us; the launch traced here: 285 us
  waiting for transfers between devices  143 us (49%)
  matrix products  45.9 us (16%)
  other arithmetic  30.8 us (11%)
  local copies, waits for them, and re-layouts  29.1 us (10%)
  between operations  15.5 us (5%)
  starting transfers between devices  11.4 us (4%)
  blocking collectives  9.28 us (3%)
    all_gather x2, waiting for transfers between devices, prefix(): lax.all_gather(a.astype(kind), axis)  70.6 us
    all_gather x2, waiting for transfers between devices, prefix_2(): lax.all_gather(part.astype(kind), axis)  59.5 us
    unnamed x187, local copies, waits for them, and re-layouts  23.3 us
    another operation x5, other arithmetic, span_terms(): jax.scipy.linalg.solve_triangular(system, stacked, lower=True, unit_diago...  19.9 us
    dot_general x16, matrix products, compose(): jnp.matmul(after_map[0], before_map[1], precision=HIGHEST) + after_map[1]  17.5 us
    reduce_scatter x1, waiting for transfers between devices, on_device(): lax.psum_scatter(partial_sum.astype(jnp.bfloat16), 'head', scatter_dimens...  10 us
    all_gather x1, blocking collectives, on_device(): feature_part = lax.all_gather(delayed, 'head', axis=1, tiled=True)  9.28 us
    all_to_all x1, starting transfers between devices, on_device(): lax.all_to_all(loaded.reshape(sources, block_rows, local_width), 'seq', s...  7.5 us
  transfers between devices with their start and end apart: 8, of which 8 were waited for; matrix products, arithmetic and copies ran while one was open for 10% of the time, Pallas kernels for 0%

commit v1 on v0

v1 whole, which is shorter than its diff:
```python
import functools

import jax
import jax.numpy as jnp
from jax import lax
from jax.experimental import pallas as pl
from jax.experimental.pallas import tpu as pltpu
from jax.sharding import PartitionSpec as P

EPSILON = 1e-06
F32 = jnp.float32
BF16 = jnp.bfloat16
HALO = 8
REACH = 16
LANES = 128
VMEM_LIMIT = 16 * 1024 * 1024


def halves(x):
    high = x.astype(BF16)
    return high, (x - high.astype(F32)).astype(BF16)


def dot(a, b):
    return jnp.dot(a, b, preferred_element_type=F32)


def dot_nt(a, b):
    return lax.dot_general(a, b, (((1,), (1,)), ((), ())), preferred_element_type=F32)


def mm(a, b):
    width = b.shape[1]
    b_high, b_low = halves(b)
    right = jnp.concatenate([b_high, b_low], axis=1)
    if a.dtype == BF16:
        both = dot(a, right)
    else:
        left = jnp.concatenate(halves(a), axis=1)
        both = dot(left, jnp.concatenate([right, right], axis=0))
    return both[:, :width] + both[:, width:]


def mm_nt(a, b):
    width = b.shape[0]
    left = jnp.concatenate(halves(a), axis=1)
    right = jnp.concatenate(halves(b), axis=0)
    both = dot_nt(left, jnp.concatenate([right, right], axis=1))
    return both[:, :width] + both[:, width:]


def begins(clips_ref, position):
    end = 0
    total = jnp.zeros_like(position)
    for clip in range(clips_ref.shape[0]):
        length = clips_ref[clip]
        end = end + length
        total = total + jnp.where(end <= position, length, 0)
    return total


def here():
    return lax.axis_index("seq"), lax.axis_index("head")


def solve_unit(low, right):
    size = low[0].shape[0]
    row = lax.broadcasted_iota(jnp.int32, (size, size), 0)
    col = lax.broadcasted_iota(jnp.int32, (size, size), 1)
    eye = jnp.where(row == col, 1.0, 0.0).astype(F32)

    def within(width):
        return (row // width) == (col // width)

    def wide_products(lefts, *rights):
        results = []
        for left, *several in zip(lefts, *rights):
            both, at, parts = mm(left, jnp.concatenate(several, axis=1)), 0, []
            for one in several:
                parts.append(both[:, at : at + one.shape[1]])
                at += one.shape[1]
            results.append(parts)
        return [list(part) for part in zip(*results)]

    block = 2
    inverse = [eye - jnp.where(within(block), x, 0.0) for x in low]
    while block < size:
        wide = min(8 * block, size)
        ring = within(wide) & jnp.logical_not(within(block))
        rest = [jnp.where(ring, n, 0.0) for n in low]
        if wide < size:
            (step,) = wide_products(inverse, rest)
            start = inverse
        else:
            step, solved = wide_products(inverse, rest, right)
            start = [jnp.concatenate(both, axis=1) for both in zip(inverse, solved)]
        square, moved = wide_products(step, step, start)
        start = [x - m for x, m in zip(start, moved)]
        fourth, moved = wide_products(square, square, start)
        start = [x + m for x, m in zip(start, moved)]
        inverse = [x + mm(f, x) for f, x in zip(fourth, start)]
        block = wide
    return [x[:, :size] for x in inverse], [x[:, size:] for x in inverse]


def prepare_kernel(kinds, local, order_ref, clips_ref, delays_ref, cap_ref, pick_ref, edge_ref, last_ref,
                   back_pick_ref, back_edge_ref, mask_ref, caps_ref):
    seq, head = here()
    frames = pick_ref.shape[1]
    parts = pick_ref.shape[0] // kinds
    width = local // parts
    group = (local * kinds) // delays_ref.shape[0]
    sources = order_ref.shape[1]
    rows_each = frames // sources
    base = seq * frames
    row = lax.broadcasted_iota(jnp.int32, (frames, frames), 0)
    col = lax.broadcasted_iota(jnp.int32, (frames, frames), 1)
    row_begin = begins(clips_ref, base + row) - base
    col_begin = begins(clips_ref, base + col[:1]) - base
    last_begin = begins(clips_ref, base + frames - 1) - base
    same = row_begin == col_begin
    carried_last = jnp.where(last_begin < 0, 1.0, 0.0)
    mask_ref[0] = jnp.where((row > col) & same, 1.0, 0.0).astype(F32)
    mask_ref[1] = jnp.where((row >= col) & same, 1.0, 0.0).astype(F32)
    mask_ref[2] = jnp.where(row_begin < 0, 1.0, 0.0).astype(F32)
    mask_ref[3] = jnp.where(row_begin == last_begin, 1.0, 0.0).astype(F32)
    mask_ref[4] = jnp.where(row == col, carried_last, 0.0).astype(F32)
    for index in range(caps_ref.shape[0]):
        caps_ref[index] = jnp.full(caps_ref.shape[1:], cap_ref[index], F32)
    lane = col[:1]
    landing = jnp.zeros((1, frames), jnp.int32)
    for source in range(sources):
        at = order_ref[0, source] * rows_each + (lane - source * rows_each)
        landing = jnp.where(lane // rows_each == source, at, landing)
    edge_row = row[:, :HALO]
    edge_col = lax.broadcasted_iota(jnp.int32, (frames, HALO), 1)
    last_ref[...] = jnp.where(landing == row[:HALO] + (frames - HALO), 1.0, 0.0).astype(BF16)
    for kind in range(kinds):
        owner = lax.rem(head + kinds - kind, kinds)
        for part in range(parts):
            source_row = row - delays_ref[(owner * local + part * width) // group]
            inside = source_row >= row_begin
            pick = jnp.where((landing == source_row) & inside, 1.0, 0.0).astype(BF16)
            pick_ref[kind * parts + part] = pick
            edge = (edge_col - HALO == source_row[:, :HALO]) & inside[:, :HALO]
            edge_ref[kind * parts + part] = jnp.where(edge, 1.0, 0.0).astype(BF16)
    edge_begin = begins(clips_ref, base + frames + edge_col[:1]) - base
    for part in range(parts):
        delay = delays_ref[(head * local + part * width) // group]
        pick = jnp.where((col == row + delay) & (col_begin <= row), 1.0, 0.0).astype(BF16)
        back_pick_ref[part] = pick
        edge = (edge_col + frames == edge_row + delay) & (edge_begin <= edge_row)
        back_edge_ref[part] = jnp.where(edge, 1.0, 0.0).astype(BF16)


def flip_kernel(*refs):
    for ref, out_ref in zip(refs[:4], refs[4:]):
        out_ref[...] = ref[...].T


def add_products(sums, kind, kinds, piece_ref, halo_ref, pick_ref, edge_ref, weights):
    local = halo_ref.shape[1] if piece_ref is None else piece_ref.shape[1]
    parts = pick_ref.shape[0] // kinds
    width = local // parts
    owner = lax.rem(here()[1] + kinds - kind, kinds)
    for part in range(parts):
        span = slice(part * width, (part + 1) * width)
        index = kind * parts + part
        if piece_ref is None:
            delayed = dot(edge_ref[index, :REACH], halo_ref[:, span])
        else:
            delayed = dot(pick_ref[index], piece_ref[:, span])
            if halo_ref is not None:
                delayed = delayed + dot(edge_ref[index], halo_ref[:, span])
        at = pl.ds(pl.multiple_of(owner * local + part * width, width), width)
        delayed = delayed.astype(BF16)
        new = [dot(delayed, weight[at, :]) for weight in weights]
        sums = new if sums is None else [a + b for a, b in zip(sums, new)]
    return sums


def own_kernel(kinds, piece_ref, pick_ref, edge_ref, *refs):
    sums = add_products(None, 0, kinds, piece_ref, None, pick_ref, edge_ref, refs[:4])
    for ref, part in zip(refs[4:], sums):
        ref[...] = part


def own_halo_kernel(kinds, halo_ref, edge_ref, *refs):
    sums = add_products(None, 0, kinds, None, halo_ref, edge_ref, edge_ref, refs[:4])
    for ref, part in zip(refs[4:], sums):
        ref[...] = part


def project_kernel(heads, kinds, mask_ref, cap_ref, *refs):
    sums, first, refs = [ref[...] for ref in refs[:4]], [ref[...] for ref in refs[4:8]], refs[8:]
    pieces, halos = refs[: kinds - 1], refs[kinds - 1 : 2 * kinds - 2]
    pick_ref, edge_ref = refs[2 * kinds - 2 : 2 * kinds]
    weights = refs[2 * kinds : 2 * kinds + 4]
    map_ref, q_ref, k_ref, v_ref, solve_ref, w_ref, aux_ref = refs[2 * kinds + 4 :]
    frames = sums[0].shape[0]
    strict, carried, final, eye = mask_ref[0], mask_ref[2], mask_ref[3], mask_ref[4]
    sums = [jnp.concatenate([x[:REACH] + a, x[REACH:]], axis=0) for x, a in zip(sums, first)]
    for kind in range(1, kinds):
        sums = add_products(
            sums, kind, kinds, pieces[kind - 1], halos[kind - 1], pick_ref, edge_ref, weights
        )
    q_all, k_all, v_all, logit_all = sums
    dk = q_all.shape[1] // heads
    dv = v_all.shape[1] // heads
    keys, rights, lows = [], [], []
    aux = jnp.zeros((frames, LANES), F32)
    aux_lane = lax.broadcasted_iota(jnp.int32, (frames, LANES), 1)
    for head in range(heads):
        q_raw = q_all[:, head * dk : (head + 1) * dk]
        k_raw = k_all[:, head * dk : (head + 1) * dk]
        value = v_all[:, head * dv : (head + 1) * dv]
        q_scale = lax.rsqrt(jnp.sum(q_raw * q_raw, axis=1, keepdims=True) + EPSILON)
        k_scale = lax.rsqrt(jnp.sum(k_raw * k_raw, axis=1, keepdims=True) + EPSILON)
        gate = 1.0 / (1.0 + jnp.exp(-logit_all[:, head : head + 1]))
        rate = cap_ref[head, :, :1] * gate
        key = k_raw * k_scale
        q_ref[head] = q_raw * q_scale
        k_ref[head] = key
        v_ref[head] = value
        for index, item in enumerate((q_scale, k_scale, rate, rate * (1.0 - gate))):
            aux = jnp.where(aux_lane == 4 * head + index, item, aux)
        gram = mm_nt(key, key)
        lows.append(strict * (rate * gram))
        keys.append(key)
        rights.append(rate * jnp.concatenate([key, value], axis=1))
    aux_ref[...] = aux
    solves, solutions = solve_unit(lows, rights)
    for head in range(heads):
        solved = solutions[head]
        solve_ref[head] = solves[head]
        w_ref[head] = solved
        ended = jnp.concatenate(
            [-(final * carried) * solved[:, :dk], final * solved[:, dk:]], axis=1
        )
        affine = mm(keys[head].T, ended)
        map_ref[head, :, :dk] = (affine[:, :dk] + eye).astype(BF16)
        map_ref[head, :, dk:] = affine[:, dk:].astype(BF16)


def local_kernel(heads, mask_ref, q_ref, k_ref, w_ref, solve_ref, early_ref, suffix_ref, prefix_ref,
                 gain_ref, grad_ref, score_t_ref, reach_ref, reach_t_ref, local_ref, solve_t_ref,
                 gram_ref, spread_ref, early_t_ref, suffix_t_ref, weighted_ref, gains_ref):
    frames, dk = q_ref.shape[1:]
    lower, carried, final = mask_ref[1], mask_ref[2], mask_ref[3]
    gains_ref[...] = gain_ref[...]
    for head in range(heads):
        query, key, solved = q_ref[head], k_ref[head], w_ref[head]
        scores = lower * mm_nt(query, key)
        both = mm(scores, solved)
        reach = carried * (query - both[:, :dk])
        score_t_ref[head] = scores.T
        prefix = prefix_ref[head]
        reach_t_ref[head] = reach.T
        grown = mm(reach, prefix.astype(F32))
        reach_ref[head] = grown[:, :dk]
        local_ref[head] = both[:, dk:] + grown[:, dk:]
        solve_t = solve_ref[head].T
        solve_t_ref[head] = solve_t
        gram_ref[head] = mm_nt(key, key)
        spread_ref[head] = mm(solve_t, final * key)
        early_t_ref[head] = early_ref[head].astype(F32).T
        suffix_t_ref[head] = suffix_ref[head].astype(F32).T
        dv = local_ref.shape[2]
        weighted_ref[head] = grad_ref[:, head * dv : (head + 1) * dv].astype(F32) * gain_ref[...]


def is_upper():
    return lax.rem(here()[0], 2) == 1


def join_kernel(heads, chips, own_ref, other_ref, *refs):
    joined_ref, prefix_ref, suffix_ref, early_ref = refs[:4]
    dk = own_ref.shape[1]
    upper = is_upper()
    row = lax.broadcasted_iota(jnp.int32, (dk, dk), 0)
    col = lax.broadcasted_iota(jnp.int32, (dk, dk), 1)
    eye = jnp.where(row == col, 1.0, 0.0)
    for head in range(heads):
        own, other = own_ref[head].astype(F32), other_ref[head].astype(F32)
        early = jnp.where(upper, other, own)
        late = jnp.where(upper, own, other)
        both = dot(late[:, :dk].astype(BF16), early.astype(BF16))
        offset = (both[:, dk:] + late[:, dk:]).astype(BF16)
        if chips > 1:
            joined_ref[head, :, :dk] = both[:, :dk].astype(BF16)
            joined_ref[head, :, dk:] = offset
            refs[4][head] = offset
        else:
            joined_ref[head] = offset
        early_ref[head] = early[:, :dk].astype(BF16)
        prefix_ref[head, :, :dk] = jnp.where(upper, other[:, :dk], eye).astype(BF16)
        prefix_ref[head, :, dk:] = jnp.where(upper, other[:, dk:], 0.0).astype(BF16)
        suffix_ref[head] = jnp.where(upper, eye, other[:, :dk]).astype(BF16)


def give_kernel(heads, even_ref, odd_ref, give_ref):
    upper = is_upper()
    width = odd_ref.shape[2]
    for head in range(heads):
        odd = odd_ref[head].astype(F32)
        even = even_ref[head].astype(F32)
        give_ref[head, :, -width:] = jnp.where(upper, odd, even[:, -width:]).astype(BF16)
        if width < even.shape[1]:
            give_ref[head, :, :-width] = even_ref[head, :, :-width]


def output_kernel(heads, chips, *refs):
    rows, swapped, refs = refs[:chips], refs[chips : chips + chips // 2], refs[chips + chips // 2 :]
    maps = []
    upper = is_upper()
    for index, row in enumerate(rows):
        other = swapped[index // 2]
        width = row.shape[2]
        mine = upper if index % 2 else jnp.logical_not(upper)
        maps.append([
            jnp.where(mine, row[head].astype(F32), other[head, :, -width:].astype(F32))
            for head in range(heads)
        ])
    (prefix_ref, reach_ref, reach_t_ref, local_ref, weighted_ref,
     state_ref, unit_ref, dout_ref, back_ref, send_ref) = refs[:10]
    flipped = refs[10:]
    seq = here()[0]
    dk = reach_ref.shape[2]
    for head in range(heads):
        state = jnp.where(seq >= 2 * chips, maps[-1][head], 0.0)
        for index in range(chips - 2, -1, -1):
            earlier = maps[index][head]
            state = earlier[:, dk:] + mm(earlier[:, :dk].astype(BF16), state)
            state = jnp.where(seq >= 2 * index + 2, state, 0.0)
        raw = local_ref[head] + mm(reach_ref[head], state)
        state_ref[head] = prefix_ref[head, :, dk:].astype(F32) + mm(prefix_ref[head, :, :dk], state)
        scale = lax.rsqrt(jnp.mean(raw * raw, axis=1, keepdims=True) + EPSILON)
        unit = raw * scale
        unit_ref[head] = unit
        weighted = weighted_ref[head]
        dout = scale * (weighted - unit * jnp.mean(unit * weighted, axis=1, keepdims=True))
        dout_ref[head] = dout
        back = mm(reach_t_ref[head], dout)
        back_ref[head] = back
        send_ref[head] = back.astype(BF16)
        product = None
        for earlier, flip_ref in zip(maps, flipped):
            move = earlier[head][:, :dk]
            product = move if product is None else mm(product, move)
            flip_ref[head] = product.T


def join_back_kernel(heads, chips, own_ref, other_ref, early_t_ref, *refs):
    flipped, later_ref, sends = refs[: chips - 1], refs[chips - 1], refs[chips:]
    upper = is_upper()
    for head in range(heads):
        own, other = own_ref[head], other_ref[head].astype(F32)
        late = jnp.where(upper, own, other)
        joined = jnp.where(upper, other, own) + mm(early_t_ref[head], late)
        later_ref[head] = jnp.where(upper, 0.0, other)
        sends[0][head] = joined.astype(BF16)
        for flip_ref, send in zip(flipped, sends[1:]):
            send[head] = mm(flip_ref[head], joined).astype(BF16)


def query_kernel(heads, mask_ref, dout_ref, state_ref, w_ref, score_t_ref, q_ref, k_ref, solve_t_ref,
                 aux_ref, unit_ref, gain_ref, spread_ref, suffix_t_ref, later_ref,
                 out_ref, gq_ref, u_ref, y_ref, dk_ref, reach_ref):
    frames, dk = q_ref.shape[1:]
    lower, carried, final = mask_ref[1], mask_ref[2], mask_ref[3]
    for head in range(heads):
        dv = unit_ref.shape[2]
        out_ref[:, head * dv : (head + 1) * dv] = (unit_ref[head] * gain_ref[...]).astype(BF16)
        dout, state, solved = dout_ref[head], state_ref[head], w_ref[head]
        query, key = q_ref[head], k_ref[head]
        fresh = solved[:, dk:] - carried * mm(solved[:, :dk], state)
        u_ref[head] = fresh
        later, suffix_t = later_ref[head], suffix_t_ref[head]
        ended = final * fresh
        reach = mm(spread_ref[head], jnp.concatenate([later, suffix_t], axis=1))
        reach_ref[head] = reach[:, dv:]
        y_ref[head] = mm(solve_t_ref[head], mm(score_t_ref[head], dout)) + reach[:, :dv]
        flow = lower * mm_nt(dout, fresh)
        dquery = carried * mm_nt(dout, state) + mm(flow, key)
        dk_ref[head] = mm(flow.T, query) + mm_nt(ended, later)
        scale = aux_ref[:, 4 * head : 4 * head + 1]
        along = jnp.sum(query * dquery, axis=1, keepdims=True)
        gq_ref[:, head * dk : (head + 1) * dk] = (scale * (dquery - query * along)).astype(BF16)


def key_kernel(heads, kinds, chips, count, mask_ref, *refs):
    arrived, refs = refs[:chips], refs[chips:]
    (suffix_t_ref, reach_ref, gq_ref, u_ref, y_ref, dk0_ref, state_ref, k_ref, v_ref, gram_ref,
     aux_ref), refs = refs[:11], refs[11:]
    seq = here()[0]
    weights, refs = refs[:4], refs[4:]
    outs, grads_ref = refs[:-1], refs[-1]
    frames, dk = k_ref.shape[1:]
    strict, carried, final = mask_ref[0], mask_ref[2], mask_ref[3]
    key_grads, value_grads = [], []
    lane = lax.broadcasted_iota(jnp.int32, (frames, LANES), 1)
    logit_grad = jnp.zeros((frames, LANES), F32)
    for head in range(heads):
        after = sum(
            jnp.where(seq + 2 * index + 2 < count, ref[head].astype(F32), 0.0)
            for index, ref in enumerate(arrived)
        )
        key, fresh = k_ref[head], u_ref[head]
        k_scale = aux_ref[:, 4 * head + 1 : 4 * head + 2]
        rate = aux_ref[:, 4 * head + 2 : 4 * head + 3]
        slope = aux_ref[:, 4 * head + 3 : 4 * head + 4]
        y = y_ref[head] + mm(reach_ref[head], after)
        both = mm_nt(y, jnp.concatenate([state_ref[head], fresh], axis=0))
        from_state = -carried * both[:, :dk]
        system = strict * -both[:, dk:]
        scaled = rate * system
        dkey = dk0_ref[head] + mm_nt(mm_nt(final * fresh, after), suffix_t_ref[head])
        dkey = dkey + mm(scaled + scaled.T, key) + rate * from_state
        drate = jnp.sum(
            system * gram_ref[head] + from_state * key + y * v_ref[head], axis=1, keepdims=True
        )
        logit_grad = jnp.where(lane == head, drate * slope, logit_grad)
        along = jnp.sum(key * dkey, axis=1, keepdims=True)
        key_grads.append((k_scale * (dkey - key * along)).astype(BF16))
        value_grads.append((rate * y).astype(BF16))
    grads_ref[...] = jnp.concatenate(
        [gq_ref[...]] + key_grads + value_grads + [logit_grad.astype(BF16)], axis=1
    )
    others, halos = outs[: kinds - 1], outs[kinds - 1 :]
    for turn in range(1, kinds):
        back_products(grads_ref, weights, turn, kinds, others[turn - 1], halos[turn - 1])


def back_products(grads_ref, weights, turn, kinds, sum_ref, halo_ref):
    local = sum_ref.shape[1]
    width = min(512, local)
    for part in range(local // width):
        first = lax.rem(here()[1] + turn, kinds) * local + part * width
        at = pl.ds(pl.multiple_of(first, width), width)
        row, total = 0, 0.0
        for weight in weights:
            total = total + dot(grads_ref[:, row : row + weight.shape[0]], weight[:, at])
            row += weight.shape[0]
        span = slice(part * width, (part + 1) * width)
        halo_ref[:, span] = total[:HALO].astype(BF16)
        sum_ref[:, span] = total.astype(sum_ref.dtype)


def own_back_kernel(kinds, grads_ref, *refs):
    back_products(grads_ref, refs[:4], 0, kinds, *refs[4:])


def finish_kernel(kinds, pick_ref, edge_ref, mine_ref, *refs):
    others, halos = refs[: kinds - 1], refs[kinds - 1 : 2 * kinds - 1]
    out_ref, held_ref, semaphores = refs[-3:]
    parts = pick_ref.shape[0]
    copies = []
    width = mine_ref.shape[1] // parts
    for part in range(parts):
        span = slice(part * width, (part + 1) * width)
        total = mine_ref[:, span]
        for other in others:
            total = total + other[:, span].astype(F32)
        edge = halos[0][:, span].astype(F32)
        for halo in halos[1:]:
            edge = edge + halo[:, span].astype(F32)
        moved = dot(pick_ref[part], total.astype(BF16)) + dot(edge_ref[part], edge.astype(BF16))
        held_ref[:, span] = moved.astype(BF16)
        copies.append(
            pltpu.make_async_copy(held_ref.at[:, span], out_ref.at[:, span], semaphores.at[part])
        )
        copies[-1].start()
    for copy in copies:
        copy.wait()


SMEM = pl.BlockSpec(memory_space=pltpu.SMEM)
VMEM = pl.BlockSpec(memory_space=pltpu.VMEM)


def call(body, name, scalars, arrays, outs, flops=0, out_space=VMEM, scratch=()):
    moved = sum(a.size * a.dtype.itemsize for a in arrays)
    moved += sum(o.size * o.dtype.itemsize for o in outs)
    return pl.pallas_call(
        body,
        name=name,
        out_shape=tuple(outs),
        in_specs=[SMEM] * len(scalars) + [VMEM] * len(arrays),
        out_specs=tuple([out_space] * len(outs)),
        scratch_shapes=list(scratch),
        cost_estimate=pl.CostEstimate(flops=flops, bytes_accessed=moved, transcendentals=0),
        compiler_params=pltpu.CompilerParams(vmem_limit_bytes=VMEM_LIMIT),
    )(*scalars, *arrays)


def shape(dims, kind=F32):
    return jax.ShapeDtypeStruct(tuple(dims), kind)


def row_shift(x, by, rising, count):
    chips = count // 2
    pairs = []
    for chip in range(chips):
        up, down = chip + by, chip - by
        pairs.append((2 * chip + rising, 2 * up + rising if up < chips else 2 * chip + 1 - rising))
        pairs.append((2 * chip + 1 - rising, 2 * down + 1 - rising if down >= 0 else 2 * chip + rising))
    return lax.ppermute(x, "seq", pairs)


def seq_shift(x, by, count):
    return lax.ppermute(x, "seq", [(i, (i + by) % count) for i in range(count)])


def core_swap(x, count):
    return lax.ppermute(x, "seq", [(i, i ^ 1) for i in range(count)])


def corner_shift(x, by, turn, count, kinds):
    pairs = []
    for i in range(count):
        for h in range(kinds):
            pairs.append((i * kinds + h, (i + by) % count * kinds + (h + turn) % kinds))
    return lax.ppermute(x, ("seq", "head"), pairs)


def head_turn(x, turn, kinds):
    return lax.ppermute(x, "head", [(h, (h + turn) % kinds) for h in range(kinds)])


def on_device(loaded, out_grad, w_query, w_key, w_value, w_beta, beta_max, out_gain, clip_lengths,
              delay_offsets, block_order):
    count = lax.axis_size("seq")
    kinds = lax.axis_size("head")
    frames, local = loaded.shape
    rows_each = frames // count
    heads = w_beta.shape[1]
    dk = w_query.shape[1] // heads
    dv = w_value.shape[1] // heads
    chips = count // 8
    group = (local * kinds) // delay_offsets.shape[0]
    parts = local // min(group, local)
    columns = heads * (2 * dk + dv) + LANES
    wb = jnp.pad(w_beta, ((0, 0), (0, LANES - heads)))
    gain = out_gain.reshape(1, dv)

    received = lax.all_to_all(
        loaded.reshape(count, rows_each, local), "seq", split_axis=0, concat_axis=0, tiled=True
    ).reshape(frames, local)
    prepared = call(
        functools.partial(prepare_kernel, kinds, local),
        "prepare",
        [block_order, clip_lengths, delay_offsets, beta_max],
        [],
        [
            shape((kinds * parts, frames, frames), BF16),
            shape((kinds * parts, frames, HALO), BF16),
            shape((HALO, frames), BF16),
            shape((parts, frames, frames), BF16),
            shape((parts, frames, HALO), BF16),
            shape((5, frames, frames)),
            shape((heads, 1, LANES)),
        ],
    )
    received, wb, *prepared = lax.optimization_barrier((received, wb, *prepared))
    pick, edge, last, back_pick, back_edge, masks, caps = prepared
    tail = jnp.dot(last, received, preferred_element_type=F32).astype(BF16)
    pieces = [head_turn(received, turn, kinds) for turn in range(1, kinds)]
    halos = [corner_shift(tail, 1, turn, count, kinds) for turn in range(kinds)]
    weights = [w_query, w_key, w_value, wb]
    sums = call(
        functools.partial(own_kernel, kinds),
        "project_own",
        [],
        [received, pick, edge] + weights,
        [shape((frames, weight.shape[1])) for weight in weights],
        flops=2 * frames * local * columns,
    )
    first = call(
        functools.partial(own_halo_kernel, kinds),
        "project_halo",
        [],
        [halos[0], edge] + weights,
        [shape((REACH, weight.shape[1])) for weight in weights],
        flops=2 * REACH * local * columns,
    )
    flipped = call(
        flip_kernel, "flip", [], weights, [shape(w.shape[::-1], BF16) for w in weights]
    )
    sums, first, flipped = lax.optimization_barrier((sums, first, flipped))

    square = shape((heads, frames, dk))
    values = shape((heads, frames, dv))
    times = shape((heads, frames, frames))
    maps = shape((heads, dk, dk + dv), BF16)
    moves = shape((heads, dk, dk))
    states = shape((heads, dk, dv))
    offsets = shape((heads, dk, dv), BF16)
    affine, q, k, v, solve, solved, aux = call(
        functools.partial(project_kernel, heads, kinds),
        "project",
        [],
        [masks, caps] + list(sums) + list(first) + pieces + halos[1:] + [pick, edge] + weights,
        [maps, square, square, values, times, shape((heads, frames, dk + dv)),
         shape((frames, LANES))],
        flops=2 * frames * local * columns,
    )
    results = call(
        functools.partial(join_kernel, heads, chips),
        "join",
        [],
        [affine, core_swap(affine, count)],
        [maps if chips > 1 else offsets, maps, shape(moves.shape, BF16), shape(moves.shape, BF16)]
        + [offsets] * (chips > 1),
        flops=10**7,
    )
    joined, prefix, suffix, early = results[:4]
    arrived = [row_shift(joined, by, (by - 1) % 2, count) for by in range(1, chips)]
    arrived.append(row_shift(results[-1], chips, (chips - 1) % 2, count))
    local_terms = call(
        functools.partial(local_kernel, heads),
        "local_terms",
        [],
        [masks, q, k, solved, solve, early, suffix, prefix, gain, out_grad],
        [times, square, shape((heads, dk, frames)), values, times, times, square, moves, moves,
         values, shape((1, dv))],
        flops=2 * 10**8,
    )
    arrived, local_terms = lax.optimization_barrier((arrived, local_terms))
    (score_t, reach, reach_t, local_out, solve_t, gram, spread, early_t, suffix_t, weighted,
     gains) = local_terms
    swapped = []
    for at in range(0, chips, 2):
        (give,) = call(
            functools.partial(give_kernel, heads), "give", [], arrived[at : at + 2], [maps],
        )
        swapped.append(core_swap(give, count))
    results = call(
        functools.partial(output_kernel, heads, chips),
        "outputs",
        [],
        arrived + swapped + [prefix, reach, reach_t, local_out, weighted],
        [states, values, values, states, offsets] + [moves] * (chips - 1),
        flops=2 * 10**8,
    )
    state, unit, dout, back, send = results[:5]
    results = call(
        functools.partial(join_back_kernel, heads, chips),
        "join_back",
        [],
        [back, core_swap(send, count), early_t] + list(results[5:]),
        [states] + [offsets] * chips,
        flops=10**7,
    )
    later = results[0]
    arrived = [seq_shift(x, -2 * by, count) for by, x in enumerate(results[1:], 1)]
    query_terms = call(
        functools.partial(query_kernel, heads),
        "query_grad",
        [],
        [masks, dout, state, solved, score_t, q, k, solve_t, aux, unit, gains, spread, suffix_t,
         later],
        [shape((frames, heads * dv), BF16), shape((frames, heads * dk), BF16), values, values,
         square, square],
        flops=2 * 10**8,
    )
    head_out, gq, fresh, y, dkey, reach = query_terms
    results = call(
        functools.partial(key_kernel, heads, kinds, chips, count),
        "key_grad",
        [],
        [masks] + arrived + [suffix_t, reach, gq, fresh, y, dkey, state, k, v, gram, aux] + list(flipped),
        [shape((frames, local), BF16)] * (kinds - 1)
        + [shape((HALO, local), BF16)] * (kinds - 1)
        + [shape((frames, columns), BF16)],
        flops=2 * 10**8,
    )
    others, edges, grads = results[: kinds - 1], results[kinds - 1 : -1], results[-1]
    mine, edge = call(
        functools.partial(own_back_kernel, kinds),
        "own_back",
        [],
        [grads] + list(flipped),
        [shape((frames, local)), shape((HALO, local), BF16)],
        flops=2 * frames * local * columns,
    )
    others = [head_turn(x, turn, kinds) for turn, x in enumerate(others, 1)]
    edges = [corner_shift(x, -1, turn, count, kinds) for turn, x in enumerate([edge] + list(edges))]
    (input_grad,) = call(
        functools.partial(finish_kernel, kinds),
        "finish",
        [],
        [back_pick, back_edge, mine] + others + edges,
        [shape((frames, local), BF16)],
        flops=10**8,
        out_space=pl.BlockSpec(memory_space=pl.ANY),
        scratch=[pltpu.VMEM((frames, local), BF16), pltpu.SemaphoreType.DMA((parts,))],
    )
    return head_out, input_grad


def solution(mesh):
    return jax.shard_map(
        on_device,
        mesh=mesh,
        in_specs=(
            P("seq", "head"),
            P("seq", "head"),
            P(None, "head"),
            P(None, "head"),
            P(None, "head"),
            P(None, "head"),
            P("head"),
            P(),
            P(),
            P(),
            P("seq", None),
        ),
        out_specs=(P("seq", "head"), P("seq", "head")),
        check_vma=False,
    )
```

time: 289 us -> 57.6 us (0.20); the launches traced: 285 us -> 57.3 us
  waiting for transfers between devices: 143 us -> 18.5 us
  matrix products: 45.9 us -> 0.15 us
  other arithmetic: 30.8 us -> 0 us
  local copies, waits for them, and re-layouts: 29.1 us -> 5.73 us
  between operations: 15.5 us -> 0.85 us
  Pallas kernels: 0 us -> 13 us
  blocking collectives: 9.28 us -> 0 us
  starting transfers between devices: 11.4 us -> 19 us
    all_gather x4 -> x0, waiting for transfers between devices: 130 us -> none  [the longest x2 70.6 us: prefix(): lax.all_gather(a.astype(kind), axis)]
    dot_general x52 -> x1, matrix products: 40.5 us -> 0.15 us  [on_device(): tail = jnp.dot(last, received, preferred_element_type=F32).astype(BF16)]
    another operation x8 -> x0, other arithmetic: 20.6 us -> none  [the longest x5 19.9 us: span_terms(): jax.scipy.linalg.solve_triangular(system, stacked, lower=True, unit_diago...]
    unnamed x187 -> x25, local copies, waits for them, and re-layouts: 23.3 us -> 4.54 us
    pallas_call x0 -> x14, Pallas kernels: none -> 13 us  [call(): pl.pallas_call(body, name=name, out_shape=tuple(outs), in_specs=[SMEM] *...]
    ppermute x2 -> x13, waiting for transfers between devices: 1.56 us -> 13.1 us  [the longest x4 4.94 us: corner_shift(): return lax.ppermute(x, ('seq', 'head'), pairs)]
    reduce_scatter x1 -> x0, waiting for transfers between devices: 10 us -> none  [on_device(): lax.psum_scatter(partial_sum.astype(jnp.bfloat16), 'head', scatter_dimens...]
    all_gather x1 -> x0, blocking collectives: 9.28 us -> none  [on_device(): feature_part = lax.all_gather(delayed, 'head', axis=1, tiled=True)]
  transfers between devices with their start and end apart: 8 -> 14, of which waited for: 8 -> 10; matrix products, arithmetic and copies ran while one was open for 10% -> 6% of each run, Pallas kernels for 0% -> 10%
where the time goes in v1:
time: 57.6 us; the launch traced here: 57.3 us
  starting transfers between devices  19 us (33%)
  waiting for transfers between devices  18.5 us (32%)
  Pallas kernels  13 us (23%)
  local copies, waits for them, and re-layouts  5.73 us (10%)
  between operations  0.85 us (1%)
    pallas_call x14, Pallas kernels, call(): pl.pallas_call(body, name=name, out_shape=tuple(outs), in_specs=[SMEM] *...  13 us
    all_to_all x1, starting transfers between devices, on_device(): lax.all_to_all(loaded.reshape(count, rows_each, local), 'seq', split_axis...  7.5 us
    all_to_all x1, waiting for transfers between devices, on_device(): lax.all_to_all(loaded.reshape(count, rows_each, local), 'seq', split_axis...  5.43 us
    ppermute x4, waiting for transfers between devices, corner_shift(): return lax.ppermute(x, ('seq', 'head'), pairs)  4.94 us
    unnamed x25, local copies, waits for them, and re-layouts  4.54 us
    ppermute x2, starting transfers between devices, seq_shift(): return lax.ppermute(x, 'seq', [(i, (i + by) % count) for i in range(count)])  4.01 us
    ppermute x3, waiting for transfers between devices, core_swap(): return lax.ppermute(x, 'seq', [(i, i ^ 1) for i in range(count)])  3.78 us
    ppermute x4, starting transfers between devices, corner_shift(): return lax.ppermute(x, ('seq', 'head'), pairs)  3.45 us
  transfers between devices with their start and end apart: 14, of which 10 were waited for; matrix products, arithmetic and copies ran while one was open for 6% of the time, Pallas kernels for 10%

profile of v1, /device:TPU:0, one launch (start us, length us, event | category | flops | bytes accessed | tf_op | source)
XLA Modules:
  0.0 57.3 jit_solution(16626893155519305265)
XLA Ops:
  0.6 7.5 %all-to-all-start = ((bf16[16,8,1024]{2,1,0:T(8,128)(2,1)}), bf16[16,8,1024]{2,1,0:T(8,128)(2,1)S(1)}, u32[]{:S(2)}, u32[]{:S(2)}) async-start(bf16[16,8,1024]{2,1,0:T(8,128)(2,1)} %bitcast.9), calls=%async_computation | async-start | bytes 524288 | tf_op jit(solution)/shard_map/all_to_all | solution.py:546
  8.1 0.0 copy-start
  8.2 1.8 %copy.13 = bf16[2048,2]{1,0:T(8,128)(2,1)} copy(bf16[2048,2]{0,1:T(2,128)(2,1)} %param.16) | data formatting | bytes 16384 | tf_op args[5]
  10.0 1.2 %pad.4.refs_3_.refs_15_ = bf16[2048,128]{1,0:T(8,128)(2,1)S(1)} pad(bf16[2048,2]{1,0:T(8,128)(2,1)} %copy.13, bf16[]{:T(256)} %constant.2.clone.1), padding=0_0x0_126 | pad | bytes 532482 | tf_op jit(solution)/shard_map/jit(_pad)/pad | solution.py:543
  11.3 0.9 %prepare.1 = (bf16[4,128,128]{2,1,0:T(8,128)(2,1)S(1)}, bf16[4,128,8]{2,1,0:T(8,128)(2,1)S(1)}, bf16[8,128]{1,0:T(8,128)(2,1)S(1)}, bf16[2,128,128]{2,1,0:T(8,12...) custom-call(s32[1,16]{1,0:T(1,128)S(1)} %copy-done.8, ...), custom_call_target="tpu_custom_call" | custom-call | bytes 539648 | tf_op jit(solution)/shard_map/prepare/pallas_call | solution.py:484
  12.1 0.0 copy-start.5
  12.1 0.6 %copy-done.5 = bf16[2,128,8]{2,1,0:T(8,128)(2,1)} copy-done((bf16[2,128,8]{2,1,0:T(8,128)(2,1)}, bf16[2,128,8]{2,1,0:T(8,128)(2,1)S(1)}, u32[]{:S(2)}) %copy-start.5) | copy-done | bytes 4120
  12.8 5.4 %all-to-all-done = bf16[16,8,1024]{2,1,0:T(8,128)(2,1)S(1)} async-done(((bf16[16,8,1024]{2,1,0:T(8,128)(2,1)}), bf16[16,8,1024]{2,1,0:T(8,128)(2,1)S(1)}, u32[]{:S(2)}, u32[]{:S(2)}) %all-to-all-start) | async-done | bytes 262176 | tf_op jit(solution)/shard_map/all_to_all | solution.py:546
  18.2 1.5 %collective-permute-start.1 = (bf16[128,1024]{1,0:T(8,128)(2,1)S(1)}, bf16[128,1024]{1,0:T(8,128)(2,1)S(1)}, u32[]{:S(2)}, u32[]{:S(2)}) collective-permute-start(bf16[128,1024]{1,0:T(8,128)(2,1)S(1)} %bitcast.5), channel_id=1, source_target_pairs={{0,1},{1,0},{2,3},{3,2},{4,5},{5,4},{6,7},{7,6},{8,9},{9,8},{10,11... | collective-permute-start | bytes 786440 | tf_op jit(solution)/shard_map/ppermute | solution.py:527
  19.7 0.1 convolution_convert_fusion
  19.9 0.0 collective-permute-start
  19.9 0.0 copy-start.2
  19.9 1.2 %copy-done.2 = bf16[2048,256]{1,0:T(8,128)(2,1)S(1)} copy-done((bf16[2048,256]{1,0:T(8,128)(2,1)S(1)}, bf16[2048,256]{1,0:T(8,128)(2,1)}, u32[]{:S(2)}) %copy-start.2) | copy-done | bytes 1048600
  21.2 1.1 %flip.1 = (bf16[256,2048]{1,0:T(8,128)(2,1)S(1)}, bf16[256,2048]{1,0:T(8,128)(2,1)S(1)}, bf16[256,2048]{1,0:T(8,128)(2,1)S(1)}, bf16[128,2048]{1,0:T(8,128)(2,1)S(1)}) custom-call(bf16[2048,256]{1,0:T(8,128)(2,1)S(1)} %copy-done, bf16[2048,256]{1,0:T(8,128)(2,1)S(1)} %copy-done.1, bf16[2048,256]{1,0:T(8,128)(2,1)S(1)} %copy-done.2, ...), custom_call_target="tpu_custom_call" | custom-call | bytes 7340032 | tf_op jit(solution)/shard_map/flip/pallas_call | solution.py:484
  22.2 0.2 copy-done.3
  22.4 0.6 %project_own.1 = (f32[128,256]{1,0:T(8,128)S(1)}, f32[128,256]{1,0:T(8,128)S(1)}, f32[128,256]{1,0:T(8,128)S(1)}, f32[128,128]{1,0:T(8,128)S(1)}) custom-call(bf16[128,1024]{1,0:T(8,128)(2,1)S(1)} %bitcast.7, bf16[4,128,128]{2,1,0:T(8,128)(2,1)S(1)} %get-tuple-element.108.pick_ref.refs_10_, bf16[4,128,8]{2,1,0:T(8,128)(2,1)S(1)} %get-tuple-element.109.edge_ref.refs_11_, ...), custom_call_target="tpu_custom_call" | custom-call | flops 234881024 | bytes 4530176 | tf_op jit(solution)/shard_map/project_own/pallas_call | solution.py:484
  23.0 2.8 %collective-permute-done.halo_ref = bf16[8,1024]{1,0:T(8,128)(2,1)S(1)} collective-permute-done((bf16[8,1024]{1,0:T(8,128)(2,1)S(1)}, bf16[8,1024]{1,0:T(8,128)(2,1)S(1)}, u32[]{:S(2)}, u32[]{:S(2)}) %collective-permute-start) | collective-permute-done | bytes 16416 | tf_op jit(solution)/shard_map/ppermute | solution.py:523
  25.8 0.4 project_halo.1
  26.3 0.3 collective-permute-done.2.refs_9_
  26.6 0.0 collective-permute-done.1.refs_8_
  26.6 2.9 %project.1 = (bf16[2,128,256]{2,1,0:T(8,128)(2,1)S(1)}, f32[2,128,128]{2,1,0:T(8,128)S(1)}, f32[2,128,128]{2,1,0:T(8,128)S(1)}, f32[2,128,128]{2,1,0:T(8,128)S(1...) custom-call(f32[5,128,128]{2,1,0:T(8,128)S(1)} %get-tuple-element.105.mask_ref, ...), custom_call_target="tpu_custom_call" | custom-call | flops 234881024 | bytes 5915648 | tf_op jit(solution)/shard_map/project/pallas_call | solution.py:484
  29.5 0.0 copy-start.4
  29.5 0.1 collective-permute-start.3
  29.6 1.3 %collective-permute-done.3.other_ref = bf16[2,128,256]{2,1,0:T(8,128)(2,1)S(1)} collective-permute-done((bf16[2,128,256]{2,1,0:T(8,128)(2,1)S(1)}, bf16[2,128,256]{2,1,0:T(8,128)(2,1)S(1)}, u32[]{:S(2)}, u32[]{:S(2)}) %collective-permute-start.3) | collective-permute-done | bytes 131104 | tf_op jit(solution)/shard_map/ppermute | solution.py:515
  30.9 0.2 join.1
  31.2 0.3 collective-permute-start.4
  31.4 0.3 collective-permute-start.5
  31.7 0.7 %copy-done.7 = f32[128]{0:T(128)S(1)} copy-done((f32[128]{0:T(128)S(1)}, f32[128]{0:T(128)}, u32[]{:S(2)}) %copy-start.7) | copy-done | bytes 536
  32.4 0.9 %local_terms.1 = (f32[2,128,128]{2,1,0:T(8,128)S(1)}, f32[2,128,128]{2,1,0:T(8,128)S(1)}, f32[2,128,128]{2,1,0:T(8,128)S(1)}, f32[2,128,128]{2,1,0:T(8,128)S(1)}...) custom-call(f32[5,128,128]{2,1,0:T(8,128)S(1)} %get-tuple-element.10, ...), custom_call_target="tpu_custom_call" | custom-call | flops 200000000 | bytes 2622464 | tf_op jit(solution)/shard_map/local_terms/pallas_call | solution.py:484
  33.3 2.5 %collective-permute-done.5.odd_ref.refs_1_ = bf16[2,128,128]{2,1,0:T(8,128)(2,1)S(1)} collective-permute-done((bf16[2,128,128]{2,1,0:T(8,128)(2,1)S(1)}, bf16[2,128,128]{2,1,0:T(8,128)(2,1)S(1)}, u32[]{:S(2)}, u32[]{:S(2)}) %collective-permute-start.5) | collective-permute-done | bytes 65568 | tf_op jit(solution)/shard_map/ppermute | solution.py:507
  35.8 0.1 collective-permute-start.6
  35.9 1.3 %collective-permute-done.6.refs_2_ = bf16[2,128,256]{2,1,0:T(8,128)(2,1)S(1)} collective-permute-done((bf16[2,128,256]{2,1,0:T(8,128)(2,1)S(1)}, bf16[2,128,256]{2,1,0:T(8,128)(2,1)S(1)}, u32[]{:S(2)}, u32[]{:S(2)}) %collective-permute-start.6) | collective-permute-done | bytes 131104 | tf_op jit(solution)/shard_map/ppermute | solution.py:515
  37.2 1.1 %outputs.1 = (f32[2,128,128]{2,1,0:T(8,128)S(1)}, f32[2,128,128]{2,1,0:T(8,128)S(1)}, f32[2,128,128]{2,1,0:T(8,128)S(1)}, f32[2,128,128]{2,1,0:T(8,128)S(1)}, bf...) custom-call(bf16[2,128,256]{2,1,0:T(8,128)(2,1)S(1)} %collective-permute-done.4.even_ref.refs_0_, ...), custom_call_target="tpu_custom_call" | custom-call | flops 200000000 | bytes 1703936 | tf_op jit(solution)/shard_map/outputs/pallas_call | solution.py:484
  38.3 0.2 collective-permute-start.7
  38.5 1.1 %collective-permute-done.7.other_ref = bf16[2,128,128]{2,1,0:T(8,128)(2,1)S(1)} collective-permute-done((bf16[2,128,128]{2,1,0:T(8,128)(2,1)S(1)}, bf16[2,128,128]{2,1,0:T(8,128)(2,1)S(1)}, u32[]{:S(2)}, u32[]{:S(2)}) %collective-permute-start.7) | collective-permute-done | bytes 65568 | tf_op jit(solution)/shard_map/ppermute | solution.py:515
  39.6 0.4 join_back.1
  40.0 2.2 %collective-permute-start.8 = (bf16[2,128,128]{2,1,0:T(8,128)(2,1)S(1)}, bf16[2,128,128]{2,1,0:T(8,128)(2,1)S(1)}, u32[]{:S(2)}, u32[]{:S(2)}) collective-permute-start(bf16[2,128,128]{2,1,0:T(8,128)(2,1)S(1)} %get-tuple-element.176), channel_id=1, source_target_pairs={{0,28},{2,30},{4,0},{6,2},{8,4},{10,6},{12,8},{14,10},{16,12},{18,... | collective-permute-start | bytes 196616 | tf_op jit(solution)/shard_map/ppermute | solution.py:511
  42.2 1.8 %collective-permute-start.9 = (bf16[2,128,128]{2,1,0:T(8,128)(2,1)S(1)}, bf16[2,128,128]{2,1,0:T(8,128)(2,1)S(1)}, u32[]{:S(2)}, u32[]{:S(2)}) collective-permute-start(bf16[2,128,128]{2,1,0:T(8,128)(2,1)S(1)} %get-tuple-element.177), channel_id=1, source_target_pairs={{0,24},{2,26},{4,28},{6,30},{8,0},{10,2},{12,4},{14,6},{16,8},{18,... | collective-permute-start | bytes 196616 | tf_op jit(solution)/shard_map/ppermute | solution.py:511
  44.0 1.6 %query_grad.1 = (bf16[128,256]{1,0:T(8,128)(2,1)}, bf16[128,256]{1,0:T(8,128)(2,1)S(1)}, f32[2,128,128]{2,1,0:T(8,128)S(1)}, f32[2,128,128]{2,1,0:T(8,128)S(1)},...) custom-call(f32[5,128,128]{2,1,0:T(8,128)S(1)} %get-tuple-element.105.mask_ref, ...), custom_call_target="tpu_custom_call" | custom-call | flops 200000000 | bytes 2621952 | tf_op jit(solution)/shard_map/query_grad/pallas_call | solution.py:484
  45.7 1.4 %collective-permute-done.9.refs_1_ = bf16[2,128,128]{2,1,0:T(8,128)(2,1)S(1)} collective-permute-done((bf16[2,128,128]{2,1,0:T(8,128)(2,1)S(1)}, bf16[2,128,128]{2,1,0:T(8,128)(2,1)S(1)}, u32[]{:S(2)}, u32[]{:S(2)}) %collective-permute-start.9) | collective-permute-done | bytes 65568 | tf_op jit(solution)/shard_map/ppermute | solution.py:511
  47.1 1.6 %key_grad.1 = (bf16[128,1024]{1,0:T(8,128)(2,1)S(1)}, bf16[8,1024]{1,0:T(8,128)(2,1)S(1)}, bf16[128,896]{1,0:T(8,128)(2,1)S(1)}) custom-call(f32[5,128,128]{2,1,0:T(8,128)S(1)} %get-tuple-element.105.mask_ref, bf16[2,128,128]{2,1,0:T(8,128)(2,1)S(1)} %collective-permute-done.8.refs_0_, bf16[2,128,128]{2,1,0:T(8,128)(2,1)S(1)} %collective-permute-done.9.refs_1_, ...), custom_call_target="tpu_custom_call" | custom-call | flops 200000000 | bytes 5947392 | tf_op jit(solution)/shard_map/key_grad/pallas_call | solution.py:484
  48.6 1.6 %collective-permute-start.10 = (bf16[128,1024]{1,0:T(8,128)(2,1)S(1)}, bf16[128,1024]{1,0:T(8,128)(2,1)S(1)}, u32[]{:S(2)}, u32[]{:S(2)}) collective-permute-start(bf16[128,1024]{1,0:T(8,128)(2,1)S(1)} %get-tuple-element.191), channel_id=1, source_target_pairs={{0,1},{1,0},{2,3},{3,2},{4,5},{5,4},{6,7},{7,6},{8,9},{9,8},{10,11... | collective-permute-start | bytes 786440 | tf_op jit(solution)/shard_map/ppermute | solution.py:527
  50.2 0.4 own_back.1
  50.7 1.6 %collective-permute-start.11 = (bf16[8,1024]{1,0:T(8,128)(2,1)S(1)}, bf16[8,1024]{1,0:T(8,128)(2,1)S(1)}, u32[]{:S(2)}, u32[]{:S(2)}) collective-permute-start(bf16[8,1024]{1,0:T(8,128)(2,1)S(1)} %get-tuple-element.192), channel_id=1, source_target_pairs={{0,30},{1,31},{2,0},{3,1},{4,2},{5,3},{6,4},{7,5},{8,6},{9,7},{10,... | collective-permute-start | bytes 49160 | tf_op jit(solution)/shard_map/ppermute | solution.py:523
  52.3 1.8 %collective-permute-start.12 = (bf16[8,1024]{1,0:T(8,128)(2,1)S(1)}, bf16[8,1024]{1,0:T(8,128)(2,1)S(1)}, u32[]{:S(2)}, u32[]{:S(2)}) collective-permute-start(bf16[8,1024]{1,0:T(8,128)(2,1)S(1)} %get-tuple-element.193), channel_id=1, source_target_pairs={{0,31},{1,30},{2,1},{3,0},{4,3},{5,2},{6,5},{7,4},{8,7},{9,6},{10,... | collective-permute-start | bytes 49160 | tf_op jit(solution)/shard_map/ppermute | solution.py:523
  54.1 1.7 %collective-permute-done.12.refs_2_ = bf16[8,1024]{1,0:T(8,128)(2,1)S(1)} collective-permute-done((bf16[8,1024]{1,0:T(8,128)(2,1)S(1)}, bf16[8,1024]{1,0:T(8,128)(2,1)S(1)}, u32[]{:S(2)}, u32[]{:S(2)}) %collective-permute-start.12) | collective-permute-done | bytes 16416 | tf_op jit(solution)/shard_map/ppermute | solution.py:523
  55.8 0.5 collective-permute-done.10.refs_0_
  56.3 1.0 %finish.1 = bf16[128,1024]{1,0:T(8,128)(2,1)} custom-call(bf16[2,128,128]{2,1,0:T(8,128)(2,1)S(1)} %get-tuple-element.174.pick_ref, bf16[2,128,8]{2,1,0:T(8,128)(2,1)S(1)} %copy-done.6, f32[128,1024]{1,0:T(8,128)S(1)} %get-tuple-element.190.mine_ref, bf16[128,1024]{1,0:T(8,128)(2,1)S(1)} %collective-permute-done.10.refs_0_, ...), custom_call_target="tpu_custom_call" | custom-call | flops 100000000 | bytes 1150976 | tf_op jit(solution)/shard_map/finish/pallas_call | solution.py:484
  (21 shorter events, 0.1 us)
Async XLA Ops:
  0.6 19.3 %copy-start.1 = (bf16[2048,256]{1,0:T(8,128)(2,1)S(1)}, bf16[2048,256]{1,0:T(8,128)(2,1)}, u32[]{:S(2)}) copy-start(bf16[2048,256]{1,0:T(8,128)(2,1)} %refs_13_.1) | copy-start | bytes 3145732
  0.6 17.6 %all-to-all-start = ((bf16[16,8,1024]{2,1,0:T(8,128)(2,1)}), bf16[16,8,1024]{2,1,0:T(8,128)(2,1)S(1)}, u32[]{:S(2)}, u32[]{:S(2)}) async-start(bf16[16,8,1024]{2,1,0:T(8,128)(2,1)} %bitcast.9), calls=%async_computation | async-start | bytes 524288 | tf_op jit(solution)/shard_map/all_to_all | solution.py:546
  8.1 11.8 %copy-start = (bf16[2048,256]{1,0:T(8,128)(2,1)S(1)}, bf16[2048,256]{1,0:T(8,128)(2,1)}, u32[]{:S(2)}) copy-start(bf16[2048,256]{1,0:T(8,128)(2,1)} %refs_12_.1) | copy-start | bytes 3145732
  10.0 1.2 %copy-start.8 = (s32[1,16]{1,0:T(1,128)S(1)}, s32[1,16]{1,0:T(1,128)}, u32[]{:S(2)}) copy-start(s32[1,16]{1,0:T(1,128)} %order_ref.1) | copy-start | bytes 196
  10.0 1.2 %copy-start.9 = (s32[16]{0:T(128)S(1)}, s32[16]{0:T(128)}, u32[]{:S(2)}) copy-start(s32[16]{0:T(128)} %clips_ref.1) | copy-start | bytes 196
  10.0 1.2 %copy-start.10 = (s32[4]{0:T(128)S(1)}, s32[4]{0:T(128)}, u32[]{:S(2)}) copy-start(s32[4]{0:T(128)} %delays_ref.1) | copy-start | bytes 52
  10.0 1.2 %copy-start.11 = (f32[2]{0:T(128)S(1)}, f32[2]{0:T(128)}, u32[]{:S(2)}) copy-start(f32[2]{0:T(128)} %cap_ref.1) | copy-start | bytes 28
  12.1 0.6 %copy-start.5 = (bf16[2,128,8]{2,1,0:T(8,128)(2,1)}, bf16[2,128,8]{2,1,0:T(8,128)(2,1)S(1)}, u32[]{:S(2)}) copy-start(bf16[2,128,8]{2,1,0:T(8,128)(2,1)S(1)} %get-tuple-element.175.edge_ref) | copy-start | bytes 12292
  18.2 8.4 %collective-permute-start.1 = (bf16[128,1024]{1,0:T(8,128)(2,1)S(1)}, bf16[128,1024]{1,0:T(8,128)(2,1)S(1)}, u32[]{:S(2)}, u32[]{:S(2)}) collective-permute-start(bf16[128,1024]{1,0:T(8,128)(2,1)S(1)} %bitcast.5), channel_id=1, source_target_pairs={{0,1},{1,0},{2,3},{3,2},{4,5},{5,4},{6,7},{7,6},{8,9},{9,8},{10,11... | collective-permute-start | bytes 786440 | tf_op jit(solution)/shard_map/ppermute | solution.py:527
  19.9 6.8 %collective-permute-start.2 = (bf16[8,1024]{1,0:T(8,128)(2,1)S(1)}, bf16[8,1024]{1,0:T(8,128)(2,1)S(1)}, u32[]{:S(2)}, u32[]{:S(2)}) collective-permute-start(bf16[8,1024]{1,0:T(8,128)(2,1)S(1)} %convolution_convert_fusion), channel_id=1, source_target_pairs={{0,3},{1,2},{2,5},{3,4},{4,7},{5,6},{6,9},{7,8},{8,11},{9,10},{10,... | collective-permute-start | bytes 49160 | tf_op jit(solution)/shard_map/ppermute | solution.py:523
  19.9 6.0 %collective-permute-start = (bf16[8,1024]{1,0:T(8,128)(2,1)S(1)}, bf16[8,1024]{1,0:T(8,128)(2,1)S(1)}, u32[]{:S(2)}, u32[]{:S(2)}) collective-permute-start(bf16[8,1024]{1,0:T(8,128)(2,1)S(1)} %convolution_convert_fusion), channel_id=1, source_target_pairs={{0,2},{1,3},{2,4},{3,5},{4,6},{5,7},{6,8},{7,9},{8,10},{9,11},{10,... | collective-permute-start | bytes 49160 | tf_op jit(solution)/shard_map/ppermute | solution.py:523
  19.9 1.2 %copy-start.2 = (bf16[2048,256]{1,0:T(8,128)(2,1)S(1)}, bf16[2048,256]{1,0:T(8,128)(2,1)}, u32[]{:S(2)}) copy-start(bf16[2048,256]{1,0:T(8,128)(2,1)} %refs_14_.1) | copy-start | bytes 3145732
  21.2 1.2 %copy-start.3 = (bf16[2048,256]{1,0:T(8,128)(2,1)S(1)}, bf16[2048,256]{1,0:T(8,128)(2,1)}, u32[]{:S(2)}) copy-start(bf16[2048,256]{1,0:T(8,128)(2,1)} %refs_14_.1) | copy-start | bytes 3145732
  29.5 2.2 %copy-start.4 = (bf16[128,256]{1,0:T(8,128)(2,1)S(1)}, bf16[128,256]{1,0:T(8,128)(2,1)}, u32[]{:S(2)}) copy-start(bf16[128,256]{1,0:T(8,128)(2,1)} %grad_ref.1) | copy-start | bytes 196612
  29.5 1.4 %collective-permute-start.3 = (bf16[2,128,256]{2,1,0:T(8,128)(2,1)S(1)}, bf16[2,128,256]{2,1,0:T(8,128)(2,1)S(1)}, u32[]{:S(2)}, u32[]{:S(2)}) collective-permute-start(bf16[2,128,256]{2,1,0:T(8,128)(2,1)S(1)} %get-tuple-element.132.own_ref), channel_id=1, source_target_pairs={{0,2},{2,0},{4,6},{6,4},{8,10},{10,8},{12,14},{14,12},{16,18},{18,... | collective-permute-start | bytes 393224 | tf_op jit(solution)/shard_map/ppermute | solution.py:515
  31.2 4.6 %collective-permute-start.4 = (bf16[2,128,256]{2,1,0:T(8,128)(2,1)S(1)}, bf16[2,128,256]{2,1,0:T(8,128)(2,1)S(1)}, u32[]{:S(2)}, u32[]{:S(2)}) collective-permute-start(bf16[2,128,256]{2,1,0:T(8,128)(2,1)S(1)} %get-tuple-element.133), channel_id=1, source_target_pairs={{0,4},{2,0},{4,8},{6,2},{8,12},{10,6},{12,16},{14,10},{16,20},{18,... | collective-permute-start | bytes 393224 | tf_op jit(solution)/shard_map/ppermute | solution.py:507
  31.4 4.3 %collective-permute-start.5 = (bf16[2,128,128]{2,1,0:T(8,128)(2,1)S(1)}, bf16[2,128,128]{2,1,0:T(8,128)(2,1)S(1)}, u32[]{:S(2)}, u32[]{:S(2)}) collective-permute-start(bf16[2,128,128]{2,1,0:T(8,128)(2,1)S(1)} %get-tuple-element.134), channel_id=1, source_target_pairs={{2,10},{0,2},{6,14},{4,6},{10,18},{8,0},{14,22},{12,4},{18,26},{16... | collective-permute-start | bytes 196616 | tf_op jit(solution)/shard_map/ppermute | solution.py:507
  31.7 0.7 %copy-start.7 = (f32[128]{0:T(128)S(1)}, f32[128]{0:T(128)}, u32[]{:S(2)}) copy-start(f32[128]{0:T(128)} %param.18) | copy-start | bytes 1540
  35.8 1.4 %collective-permute-start.6 = (bf16[2,128,256]{2,1,0:T(8,128)(2,1)S(1)}, bf16[2,128,256]{2,1,0:T(8,128)(2,1)S(1)}, u32[]{:S(2)}, u32[]{:S(2)}) collective-permute-start(bf16[2,128,256]{2,1,0:T(8,128)(2,1)S(1)} %give.1), channel_id=1, source_target_pairs={{0,2},{2,0},{4,6},{6,4},{8,10},{10,8},{12,14},{14,12},{16,18},{18,... | collective-permute-start | bytes 393224 | tf_op jit(solution)/shard_map/ppermute | solution.py:515
  38.3 1.3 %collective-permute-start.7 = (bf16[2,128,128]{2,1,0:T(8,128)(2,1)S(1)}, bf16[2,128,128]{2,1,0:T(8,128)(2,1)S(1)}, u32[]{:S(2)}, u32[]{:S(2)}) collective-permute-start(bf16[2,128,128]{2,1,0:T(8,128)(2,1)S(1)} %get-tuple-element.169), channel_id=1, source_target_pairs={{0,2},{2,0},{4,6},{6,4},{8,10},{10,8},{12,14},{14,12},{16,18},{18,... | collective-permute-start | bytes 196616 | tf_op jit(solution)/shard_map/ppermute | solution.py:515
  40.0 5.7 %collective-permute-start.8 = (bf16[2,128,128]{2,1,0:T(8,128)(2,1)S(1)}, bf16[2,128,128]{2,1,0:T(8,128)(2,1)S(1)}, u32[]{:S(2)}, u32[]{:S(2)}) collective-permute-start(bf16[2,128,128]{2,1,0:T(8,128)(2,1)S(1)} %get-tuple-element.176), channel_id=1, source_target_pairs={{0,28},{2,30},{4,0},{6,2},{8,4},{10,6},{12,8},{14,10},{16,12},{18,... | collective-permute-start | bytes 196616 | tf_op jit(solution)/shard_map/ppermute | solution.py:511
  42.2 4.9 %collective-permute-start.9 = (bf16[2,128,128]{2,1,0:T(8,128)(2,1)S(1)}, bf16[2,128,128]{2,1,0:T(8,128)(2,1)S(1)}, u32[]{:S(2)}, u32[]{:S(2)}) collective-permute-start(bf16[2,128,128]{2,1,0:T(8,128)(2,1)S(1)} %get-tuple-element.177), channel_id=1, source_target_pairs={{0,24},{2,26},{4,28},{6,30},{8,0},{10,2},{12,4},{14,6},{16,8},{18,... | collective-permute-start | bytes 196616 | tf_op jit(solution)/shard_map/ppermute | solution.py:511
  48.6 7.6 %collective-permute-start.10 = (bf16[128,1024]{1,0:T(8,128)(2,1)S(1)}, bf16[128,1024]{1,0:T(8,128)(2,1)S(1)}, u32[]{:S(2)}, u32[]{:S(2)}) collective-permute-start(bf16[128,1024]{1,0:T(8,128)(2,1)S(1)} %get-tuple-element.191), channel_id=1, source_target_pairs={{0,1},{1,0},{2,3},{3,2},{4,5},{5,4},{6,7},{7,6},{8,9},{9,8},{10,11... | collective-permute-start | bytes 786440 | tf_op jit(solution)/shard_map/ppermute | solution.py:527
  50.2 6.1 %copy-start.6 = (bf16[2,128,8]{2,1,0:T(8,128)(2,1)S(1)}, bf16[2,128,8]{2,1,0:T(8,128)(2,1)}, u32[]{:S(2)}) copy-start(bf16[2,128,8]{2,1,0:T(8,128)(2,1)} %copy-done.5) | copy-start | bytes 12292
  50.7 3.4 %collective-permute-start.11 = (bf16[8,1024]{1,0:T(8,128)(2,1)S(1)}, bf16[8,1024]{1,0:T(8,128)(2,1)S(1)}, u32[]{:S(2)}, u32[]{:S(2)}) collective-permute-start(bf16[8,1024]{1,0:T(8,128)(2,1)S(1)} %get-tuple-element.192), channel_id=1, source_target_pairs={{0,30},{1,31},{2,0},{3,1},{4,2},{5,3},{6,4},{7,5},{8,6},{9,7},{10,... | collective-permute-start | bytes 49160 | tf_op jit(solution)/shard_map/ppermute | solution.py:523
  52.3 3.6 %collective-permute-start.12 = (bf16[8,1024]{1,0:T(8,128)(2,1)S(1)}, bf16[8,1024]{1,0:T(8,128)(2,1)S(1)}, u32[]{:S(2)}, u32[]{:S(2)}) collective-permute-start(bf16[8,1024]{1,0:T(8,128)(2,1)S(1)} %get-tuple-element.193), channel_id=1, source_target_pairs={{0,31},{1,30},{2,1},{3,0},{4,3},{5,2},{6,5},{7,4},{8,7},{9,6},{10,... | collective-permute-start | bytes 49160 | tf_op jit(solution)/shard_map/ppermute | solution.py:523

commit v2 on v1

--- a/solution.py
+++ b/solution.py
@@ -389,7 +389,7 @@
 
 
 def key_kernel(heads, kinds, chips, count, mask_ref, *refs):
-    arrived, refs = refs[:chips], refs[chips:]
+    arrived, row_ref, shared_ref, refs = refs[: chips - 1], refs[chips - 1], refs[chips], refs[chips + 1 :]
     (suffix_t_ref, reach_ref, gq_ref, u_ref, y_ref, dk0_ref, state_ref, k_ref, v_ref, gram_ref,
      aux_ref), refs = refs[:11], refs[11:]
     seq = here()[0]
@@ -405,6 +405,8 @@
             jnp.where(seq + 2 * index + 2 < count, ref[head].astype(F32), 0.0)
             for index, ref in enumerate(arrived)
         )
+        farthest = jnp.where(is_upper(), row_ref[head], shared_ref[head])
+        after = after + jnp.where(seq + 2 * chips < count, farthest.astype(F32), 0.0)
         key, fresh = k_ref[head], u_ref[head]
         k_scale = aux_ref[:, 4 * head + 1 : 4 * head + 2]
         rate = aux_ref[:, 4 * head + 2 : 4 * head + 3]
@@ -652,7 +654,8 @@
         flops=10**7,
     )
     later = results[0]
-    arrived = [seq_shift(x, -2 * by, count) for by, x in enumerate(results[1:], 1)]
+    arrived = [seq_shift(x, -2 * by, count) for by, x in enumerate(results[1:-1], 1)]
+    farthest = row_shift(results[-1], chips, 0, count)
     query_terms = call(
         functools.partial(query_kernel, heads),
         "query_grad",
@@ -663,7 +666,9 @@
          square, square],
         flops=2 * 10**8,
     )
+    farthest, query_terms = lax.optimization_barrier((farthest, query_terms))
     head_out, gq, fresh, y, dkey, reach = query_terms
+    arrived += [farthest, core_swap(farthest, count)]
     results = call(
         functools.partial(key_kernel, heads, kinds, chips, count),
         "key_grad",

time: 57.6 us -> 58.1 us (level)
    ppermute x2 -> x1, starting transfers between devices: 4.01 us -> 0.14 us  [seq_shift(): return lax.ppermute(x, 'seq', [(i, (i + by) % count) for i in range(count)])]
    ppermute x2 -> x3, starting transfers between devices: 0.57 us -> 2.74 us  [row_shift(): return lax.ppermute(x, 'seq', pairs)]
    ppermute x3 -> x4, starting transfers between devices: 0.36 us -> 1.51 us  [core_swap(): return lax.ppermute(x, 'seq', [(i, i ^ 1) for i in range(count)])]
    ppermute x4, starting transfers between devices: 3.45 us -> 4.26 us  [corner_shift(): return lax.ppermute(x, ('seq', 'head'), pairs)]
    ppermute x4, waiting for transfers between devices: 4.94 us -> 5.69 us  [corner_shift(): return lax.ppermute(x, ('seq', 'head'), pairs)]
    ppermute x2 -> x1, waiting for transfers between devices: 1.42 us -> 1.21 us  [seq_shift(): return lax.ppermute(x, 'seq', [(i, (i + by) % count) for i in range(count)])]
    ppermute x2 -> x3, waiting for transfers between devices: 2.48 us -> 2.6 us  [row_shift(): return lax.ppermute(x, 'seq', pairs)]
    ppermute x3 -> x4, waiting for transfers between devices: 3.78 us -> 3.78 us  [core_swap(): return lax.ppermute(x, 'seq', [(i, i ^ 1) for i in range(count)])]
  transfers between devices with their start and end apart: 14 -> 15, of which waited for: 10 -> 11; matrix products, arithmetic and copies ran while one was open for 6% -> 6% of each run, Pallas kernels for 10% -> 10%
where the time goes in v2:
time: 58.1 us; the launch traced here: 57.7 us
  starting transfers between devices  19.3 us (33%)
  waiting for transfers between devices  18.7 us (32%)
  Pallas kernels  13 us (22%)
  local copies, waits for them, and re-layouts  5.73 us (10%)
  between operations  0.85 us (1%)
    pallas_call x14, Pallas kernels, call(): pl.pallas_call(body, name=name, out_shape=tuple(outs), in_specs=[SMEM] *...  13 us
    all_to_all x1, starting transfers between devices, on_device(): lax.all_to_all(loaded.reshape(count, rows_each, local), 'seq', split_axis...  7.5 us
    ppermute x4, waiting for transfers between devices, corner_shift(): return lax.ppermute(x, ('seq', 'head'), pairs)  5.69 us
    all_to_all x1, waiting for transfers between devices, on_device(): lax.all_to_all(loaded.reshape(count, rows_each, local), 'seq', split_axis...  5.43 us
    unnamed x25, local copies, waits for them, and re-layouts  4.53 us
    ppermute x4, starting transfers between devices, corner_shift(): return lax.ppermute(x, ('seq', 'head'), pairs)  4.26 us
    ppermute x4, waiting for transfers between devices, core_swap(): return lax.ppermute(x, 'seq', [(i, i ^ 1) for i in range(count)])  3.78 us
    ppermute x2, starting transfers between devices, head_turn(): lax.ppermute(x, 'head', [(h, (h + turn) % kinds) for h in range(kinds)])  3.1 us
  transfers between devices with their start and end apart: 15, of which 11 were waited for; matrix products, arithmetic and copies ran while one was open for 6% of the time, Pallas kernels for 10%

profile of v2, /device:TPU:0, one launch (start us, length us, event | category | flops | bytes accessed | tf_op | source)
XLA Modules:
  0.0 57.7 jit_solution(323849386790493375)
XLA Ops:
  0.6 7.5 %all-to-all-start = ((bf16[16,8,1024]{2,1,0:T(8,128)(2,1)}), bf16[16,8,1024]{2,1,0:T(8,128)(2,1)S(1)}, u32[]{:S(2)}, u32[]{:S(2)}) async-start(bf16[16,8,1024]{2,1,0:T(8,128)(2,1)} %bitcast.9), calls=%async_computation | async-start | bytes 524288 | tf_op jit(solution)/shard_map/all_to_all | solution.py:548
  8.1 0.0 copy-start
  8.2 1.8 %copy.13 = bf16[2048,2]{1,0:T(8,128)(2,1)} copy(bf16[2048,2]{0,1:T(2,128)(2,1)} %param.16) | data formatting | bytes 16384 | tf_op args[5]
  10.0 1.2 %pad.4.refs_3_.refs_15_ = bf16[2048,128]{1,0:T(8,128)(2,1)S(1)} pad(bf16[2048,2]{1,0:T(8,128)(2,1)} %copy.13, bf16[]{:T(256)} %constant.2.clone.1), padding=0_0x0_126 | pad | bytes 532482 | tf_op jit(solution)/shard_map/jit(_pad)/pad | solution.py:545
  11.2 0.9 %prepare.1 = (bf16[4,128,128]{2,1,0:T(8,128)(2,1)S(1)}, bf16[4,128,8]{2,1,0:T(8,128)(2,1)S(1)}, bf16[8,128]{1,0:T(8,128)(2,1)S(1)}, bf16[2,128,128]{2,1,0:T(8,12...) custom-call(s32[1,16]{1,0:T(1,128)S(1)} %copy-done.8, ...), custom_call_target="tpu_custom_call" | custom-call | bytes 539648 | tf_op jit(solution)/shard_map/prepare/pallas_call | solution.py:486
  12.1 0.0 copy-start.5
  12.1 0.6 %copy-done.5 = bf16[2,128,8]{2,1,0:T(8,128)(2,1)} copy-done((bf16[2,128,8]{2,1,0:T(8,128)(2,1)}, bf16[2,128,8]{2,1,0:T(8,128)(2,1)S(1)}, u32[]{:S(2)}) %copy-start.5) | copy-done | bytes 4120
  12.8 5.4 %all-to-all-done = bf16[16,8,1024]{2,1,0:T(8,128)(2,1)S(1)} async-done(((bf16[16,8,1024]{2,1,0:T(8,128)(2,1)}), bf16[16,8,1024]{2,1,0:T(8,128)(2,1)S(1)}, u32[]{:S(2)}, u32[]{:S(2)}) %all-to-all-start) | async-done | bytes 262176 | tf_op jit(solution)/shard_map/all_to_all | solution.py:548
  18.2 1.5 %collective-permute-start.1 = (bf16[128,1024]{1,0:T(8,128)(2,1)S(1)}, bf16[128,1024]{1,0:T(8,128)(2,1)S(1)}, u32[]{:S(2)}, u32[]{:S(2)}) collective-permute-start(bf16[128,1024]{1,0:T(8,128)(2,1)S(1)} %bitcast.5), channel_id=1, source_target_pairs={{0,1},{1,0},{2,3},{3,2},{4,5},{5,4},{6,7},{7,6},{8,9},{9,8},{10,11... | collective-permute-start | bytes 786440 | tf_op jit(solution)/shard_map/ppermute | solution.py:529
  19.7 0.1 convolution_convert_fusion
  19.9 0.0 collective-permute-start
  19.9 0.0 copy-start.2
  19.9 1.2 %copy-done.2 = bf16[2048,256]{1,0:T(8,128)(2,1)S(1)} copy-done((bf16[2048,256]{1,0:T(8,128)(2,1)S(1)}, bf16[2048,256]{1,0:T(8,128)(2,1)}, u32[]{:S(2)}) %copy-start.2) | copy-done | bytes 1048600
  21.2 1.1 %flip.1 = (bf16[256,2048]{1,0:T(8,128)(2,1)S(1)}, bf16[256,2048]{1,0:T(8,128)(2,1)S(1)}, bf16[256,2048]{1,0:T(8,128)(2,1)S(1)}, bf16[128,2048]{1,0:T(8,128)(2,1)S(1)}) custom-call(bf16[2048,256]{1,0:T(8,128)(2,1)S(1)} %copy-done, bf16[2048,256]{1,0:T(8,128)(2,1)S(1)} %copy-done.1, bf16[2048,256]{1,0:T(8,128)(2,1)S(1)} %copy-done.2, ...), custom_call_target="tpu_custom_call" | custom-call | bytes 7340032 | tf_op jit(solution)/shard_map/flip/pallas_call | solution.py:486
  22.2 0.2 copy-done.3
  22.4 0.6 %project_own.1 = (f32[128,256]{1,0:T(8,128)S(1)}, f32[128,256]{1,0:T(8,128)S(1)}, f32[128,256]{1,0:T(8,128)S(1)}, f32[128,128]{1,0:T(8,128)S(1)}) custom-call(bf16[128,1024]{1,0:T(8,128)(2,1)S(1)} %bitcast.7, bf16[4,128,128]{2,1,0:T(8,128)(2,1)S(1)} %get-tuple-element.115.pick_ref.refs_10_, bf16[4,128,8]{2,1,0:T(8,128)(2,1)S(1)} %get-tuple-element.116.edge_ref.refs_11_, ...), custom_call_target="tpu_custom_call" | custom-call | flops 234881024 | bytes 4530176 | tf_op jit(solution)/shard_map/project_own/pallas_call | solution.py:486
  23.0 2.8 %collective-permute-done.halo_ref = bf16[8,1024]{1,0:T(8,128)(2,1)S(1)} collective-permute-done((bf16[8,1024]{1,0:T(8,128)(2,1)S(1)}, bf16[8,1024]{1,0:T(8,128)(2,1)S(1)}, u32[]{:S(2)}, u32[]{:S(2)}) %collective-permute-start) | collective-permute-done | bytes 16416 | tf_op jit(solution)/shard_map/ppermute | solution.py:525
  25.8 0.4 project_halo.1
  26.3 0.3 collective-permute-done.2.refs_9_
  26.6 2.9 %project.1 = (bf16[2,128,256]{2,1,0:T(8,128)(2,1)S(1)}, f32[2,128,128]{2,1,0:T(8,128)S(1)}, f32[2,128,128]{2,1,0:T(8,128)S(1)}, f32[2,128,128]{2,1,0:T(8,128)S(1...) custom-call(f32[5,128,128]{2,1,0:T(8,128)S(1)} %get-tuple-element.112.mask_ref, ...), custom_call_target="tpu_custom_call" | custom-call | flops 234881024 | bytes 5915648 | tf_op jit(solution)/shard_map/project/pallas_call | solution.py:486
  29.5 0.1 collective-permute-start.3
  29.6 1.3 %collective-permute-done.3.other_ref = bf16[2,128,256]{2,1,0:T(8,128)(2,1)S(1)} collective-permute-done((bf16[2,128,256]{2,1,0:T(8,128)(2,1)S(1)}, bf16[2,128,256]{2,1,0:T(8,128)(2,1)S(1)}, u32[]{:S(2)}, u32[]{:S(2)}) %collective-permute-start.3) | collective-permute-done | bytes 131104 | tf_op jit(solution)/shard_map/ppermute | solution.py:517
  30.9 0.2 join.1
  31.1 0.3 collective-permute-start.4
  31.4 0.3 collective-permute-start.5
  31.7 0.7 %copy-done.7 = f32[128]{0:T(128)S(1)} copy-done((f32[128]{0:T(128)S(1)}, f32[128]{0:T(128)}, u32[]{:S(2)}) %copy-start.7) | copy-done | bytes 536
  32.4 0.9 %local_terms.1 = (f32[2,128,128]{2,1,0:T(8,128)S(1)}, f32[2,128,128]{2,1,0:T(8,128)S(1)}, f32[2,128,128]{2,1,0:T(8,128)S(1)}, f32[2,128,128]{2,1,0:T(8,128)S(1)}...) custom-call(f32[5,128,128]{2,1,0:T(8,128)S(1)} %get-tuple-element.11, ...), custom_call_target="tpu_custom_call" | custom-call | flops 200000000 | bytes 2622464 | tf_op jit(solution)/shard_map/local_terms/pallas_call | solution.py:486
  33.3 2.5 %collective-permute-done.5.odd_ref.refs_1_ = bf16[2,128,128]{2,1,0:T(8,128)(2,1)S(1)} collective-permute-done((bf16[2,128,128]{2,1,0:T(8,128)(2,1)S(1)}, bf16[2,128,128]{2,1,0:T(8,128)(2,1)S(1)}, u32[]{:S(2)}, u32[]{:S(2)}) %collective-permute-start.5) | collective-permute-done | bytes 65568 | tf_op jit(solution)/shard_map/ppermute | solution.py:509
  35.8 0.1 collective-permute-start.6
  35.9 1.3 %collective-permute-done.6.refs_2_ = bf16[2,128,256]{2,1,0:T(8,128)(2,1)S(1)} collective-permute-done((bf16[2,128,256]{2,1,0:T(8,128)(2,1)S(1)}, bf16[2,128,256]{2,1,0:T(8,128)(2,1)S(1)}, u32[]{:S(2)}, u32[]{:S(2)}) %collective-permute-start.6) | collective-permute-done | bytes 131104 | tf_op jit(solution)/shard_map/ppermute | solution.py:517
  37.2 1.1 %outputs.1 = (f32[2,128,128]{2,1,0:T(8,128)S(1)}, f32[2,128,128]{2,1,0:T(8,128)S(1)}, f32[2,128,128]{2,1,0:T(8,128)S(1)}, f32[2,128,128]{2,1,0:T(8,128)S(1)}, bf...) custom-call(bf16[2,128,256]{2,1,0:T(8,128)(2,1)S(1)} %collective-permute-done.4.even_ref.refs_0_, ...), custom_call_target="tpu_custom_call" | custom-call | flops 200000000 | bytes 1703936 | tf_op jit(solution)/shard_map/outputs/pallas_call | solution.py:486
  38.3 0.2 collective-permute-start.7
  38.5 1.1 %collective-permute-done.7.other_ref = bf16[2,128,128]{2,1,0:T(8,128)(2,1)S(1)} collective-permute-done((bf16[2,128,128]{2,1,0:T(8,128)(2,1)S(1)}, bf16[2,128,128]{2,1,0:T(8,128)(2,1)S(1)}, u32[]{:S(2)}, u32[]{:S(2)}) %collective-permute-start.7) | collective-permute-done | bytes 65568 | tf_op jit(solution)/shard_map/ppermute | solution.py:517
  39.6 0.4 join_back.1
  40.0 2.2 %collective-permute-start.8 = (bf16[2,128,128]{2,1,0:T(8,128)(2,1)S(1)}, bf16[2,128,128]{2,1,0:T(8,128)(2,1)S(1)}, u32[]{:S(2)}, u32[]{:S(2)}) collective-permute-start(bf16[2,128,128]{2,1,0:T(8,128)(2,1)S(1)} %get-tuple-element.170), channel_id=1, source_target_pairs={{0,8},{2,0},{4,12},{6,4},{8,16},{10,2},{12,20},{14,6},{16,24},{18,... | collective-permute-start | bytes 196616 | tf_op jit(solution)/shard_map/ppermute | solution.py:509
  42.2 0.1 collective-permute-start.9
  42.3 1.6 %query_grad.1 = (bf16[128,256]{1,0:T(8,128)(2,1)}, bf16[128,256]{1,0:T(8,128)(2,1)S(1)}, f32[2,128,128]{2,1,0:T(8,128)S(1)}, f32[2,128,128]{2,1,0:T(8,128)S(1)},...) custom-call(f32[5,128,128]{2,1,0:T(8,128)S(1)} %get-tuple-element.112.mask_ref, ...), custom_call_target="tpu_custom_call" | custom-call | flops 200000000 | bytes 2621952 | tf_op jit(solution)/shard_map/query_grad/pallas_call | solution.py:486
  44.0 0.1 collective-permute-done.8.refs_1_
  44.1 1.1 %collective-permute-start.10 = (bf16[2,128,128]{2,1,0:T(8,128)(2,1)S(1)}, bf16[2,128,128]{2,1,0:T(8,128)(2,1)S(1)}, u32[]{:S(2)}, u32[]{:S(2)}) collective-permute-start(bf16[2,128,128]{2,1,0:T(8,128)(2,1)S(1)} %collective-permute-done.8.refs_1_), channel_id=1, source_target_pairs={{0,2},{2,0},{4,6},{6,4},{8,10},{10,8},{12,14},{14,12},{16,18},{18,... | collective-permute-start | bytes 196616 | tf_op jit(solution)/shard_map/ppermute | solution.py:517
  45.2 1.2 %collective-permute-done.9.refs_0_ = bf16[2,128,128]{2,1,0:T(8,128)(2,1)S(1)} collective-permute-done((bf16[2,128,128]{2,1,0:T(8,128)(2,1)S(1)}, bf16[2,128,128]{2,1,0:T(8,128)(2,1)S(1)}, u32[]{:S(2)}, u32[]{:S(2)}) %collective-permute-start.9) | collective-permute-done | bytes 65568 | tf_op jit(solution)/shard_map/ppermute | solution.py:513
  46.4 1.6 %key_grad.1 = (bf16[128,1024]{1,0:T(8,128)(2,1)S(1)}, bf16[8,1024]{1,0:T(8,128)(2,1)S(1)}, bf16[128,896]{1,0:T(8,128)(2,1)S(1)}) custom-call(f32[5,128,128]{2,1,0:T(8,128)S(1)} %get-tuple-element.112.mask_ref, bf16[2,128,128]{2,1,0:T(8,128)(2,1)S(1)} %collective-permute-done.9.refs_0_, bf16[2,128,128]{2,1,0:T(8,128)(2,1)S(1)} %collective-permute-done.8.refs_1_, ...), custom_call_target="tpu_custom_call" | custom-call | flops 200000000 | bytes 6012928 | tf_op jit(solution)/shard_map/key_grad/pallas_call | solution.py:486
  48.0 1.6 %collective-permute-start.11 = (bf16[128,1024]{1,0:T(8,128)(2,1)S(1)}, bf16[128,1024]{1,0:T(8,128)(2,1)S(1)}, u32[]{:S(2)}, u32[]{:S(2)}) collective-permute-start(bf16[128,1024]{1,0:T(8,128)(2,1)S(1)} %get-tuple-element.205), channel_id=1, source_target_pairs={{0,1},{1,0},{2,3},{3,2},{4,5},{5,4},{6,7},{7,6},{8,9},{9,8},{10,11... | collective-permute-start | bytes 786440 | tf_op jit(solution)/shard_map/ppermute | solution.py:529
  49.6 0.5 own_back.1
  50.1 3.5 %collective-permute-start.12 = (bf16[8,1024]{1,0:T(8,128)(2,1)S(1)}, bf16[8,1024]{1,0:T(8,128)(2,1)S(1)}, u32[]{:S(2)}, u32[]{:S(2)}) collective-permute-start(bf16[8,1024]{1,0:T(8,128)(2,1)S(1)} %get-tuple-element.206), channel_id=1, source_target_pairs={{0,30},{1,31},{2,0},{3,1},{4,2},{5,3},{6,4},{7,5},{8,6},{9,7},{10,... | collective-permute-start | bytes 49160 | tf_op jit(solution)/shard_map/ppermute | solution.py:525
  53.6 0.7 %collective-permute-start.13 = (bf16[8,1024]{1,0:T(8,128)(2,1)S(1)}, bf16[8,1024]{1,0:T(8,128)(2,1)S(1)}, u32[]{:S(2)}, u32[]{:S(2)}) collective-permute-start(bf16[8,1024]{1,0:T(8,128)(2,1)S(1)} %get-tuple-element.207), channel_id=1, source_target_pairs={{0,31},{1,30},{2,1},{3,0},{4,3},{5,2},{6,5},{7,4},{8,7},{9,6},{10,... | collective-permute-start | bytes 49160 | tf_op jit(solution)/shard_map/ppermute | solution.py:525
  54.3 0.8 %collective-permute-done.12.refs_1_ = bf16[8,1024]{1,0:T(8,128)(2,1)S(1)} collective-permute-done((bf16[8,1024]{1,0:T(8,128)(2,1)S(1)}, bf16[8,1024]{1,0:T(8,128)(2,1)S(1)}, u32[]{:S(2)}, u32[]{:S(2)}) %collective-permute-start.12) | collective-permute-done | bytes 16416 | tf_op jit(solution)/shard_map/ppermute | solution.py:525
  55.0 1.7 %collective-permute-done.13.refs_2_ = bf16[8,1024]{1,0:T(8,128)(2,1)S(1)} collective-permute-done((bf16[8,1024]{1,0:T(8,128)(2,1)S(1)}, bf16[8,1024]{1,0:T(8,128)(2,1)S(1)}, u32[]{:S(2)}, u32[]{:S(2)}) %collective-permute-start.13) | collective-permute-done | bytes 16416 | tf_op jit(solution)/shard_map/ppermute | solution.py:525
  56.8 1.0 %finish.1 = bf16[128,1024]{1,0:T(8,128)(2,1)} custom-call(bf16[2,128,128]{2,1,0:T(8,128)(2,1)S(1)} %get-tuple-element.188.pick_ref, bf16[2,128,8]{2,1,0:T(8,128)(2,1)S(1)} %copy-done.6, f32[128,1024]{1,0:T(8,128)S(1)} %get-tuple-element.204.mine_ref, bf16[128,1024]{1,0:T(8,128)(2,1)S(1)} %collective-permute-done.11.refs_0_, ...), custom_call_target="tpu_custom_call" | custom-call | flops 100000000 | bytes 1150976 | tf_op jit(solution)/shard_map/finish/pallas_call | solution.py:486
  (23 shorter events, 0.1 us)
Async XLA Ops:
  0.6 19.3 %copy-start.1 = (bf16[2048,256]{1,0:T(8,128)(2,1)S(1)}, bf16[2048,256]{1,0:T(8,128)(2,1)}, u32[]{:S(2)}) copy-start(bf16[2048,256]{1,0:T(8,128)(2,1)} %refs_13_.1) | copy-start | bytes 3145732
  0.6 17.6 %all-to-all-start = ((bf16[16,8,1024]{2,1,0:T(8,128)(2,1)}), bf16[16,8,1024]{2,1,0:T(8,128)(2,1)S(1)}, u32[]{:S(2)}, u32[]{:S(2)}) async-start(bf16[16,8,1024]{2,1,0:T(8,128)(2,1)} %bitcast.9), calls=%async_computation | async-start | bytes 524288 | tf_op jit(solution)/shard_map/all_to_all | solution.py:548
  8.1 11.8 %copy-start = (bf16[2048,256]{1,0:T(8,128)(2,1)S(1)}, bf16[2048,256]{1,0:T(8,128)(2,1)}, u32[]{:S(2)}) copy-start(bf16[2048,256]{1,0:T(8,128)(2,1)} %refs_12_.1) | copy-start | bytes 3145732
  10.0 1.2 %copy-start.8 = (s32[1,16]{1,0:T(1,128)S(1)}, s32[1,16]{1,0:T(1,128)}, u32[]{:S(2)}) copy-start(s32[1,16]{1,0:T(1,128)} %order_ref.1) | copy-start | bytes 196
  10.0 1.2 %copy-start.9 = (s32[16]{0:T(128)S(1)}, s32[16]{0:T(128)}, u32[]{:S(2)}) copy-start(s32[16]{0:T(128)} %clips_ref.1) | copy-start | bytes 196
  10.0 1.2 %copy-start.10 = (s32[4]{0:T(128)S(1)}, s32[4]{0:T(128)}, u32[]{:S(2)}) copy-start(s32[4]{0:T(128)} %delays_ref.1) | copy-start | bytes 52
  10.0 1.2 %copy-start.11 = (f32[2]{0:T(128)S(1)}, f32[2]{0:T(128)}, u32[]{:S(2)}) copy-start(f32[2]{0:T(128)} %cap_ref.1) | copy-start | bytes 28
  12.1 0.6 %copy-start.5 = (bf16[2,128,8]{2,1,0:T(8,128)(2,1)}, bf16[2,128,8]{2,1,0:T(8,128)(2,1)S(1)}, u32[]{:S(2)}) copy-start(bf16[2,128,8]{2,1,0:T(8,128)(2,1)S(1)} %get-tuple-element.189.edge_ref) | copy-start | bytes 12292
  18.2 8.4 %collective-permute-start.1 = (bf16[128,1024]{1,0:T(8,128)(2,1)S(1)}, bf16[128,1024]{1,0:T(8,128)(2,1)S(1)}, u32[]{:S(2)}, u32[]{:S(2)}) collective-permute-start(bf16[128,1024]{1,0:T(8,128)(2,1)S(1)} %bitcast.5), channel_id=1, source_target_pairs={{0,1},{1,0},{2,3},{3,2},{4,5},{5,4},{6,7},{7,6},{8,9},{9,8},{10,11... | collective-permute-start | bytes 786440 | tf_op jit(solution)/shard_map/ppermute | solution.py:529
  19.9 6.8 %collective-permute-start.2 = (bf16[8,1024]{1,0:T(8,128)(2,1)S(1)}, bf16[8,1024]{1,0:T(8,128)(2,1)S(1)}, u32[]{:S(2)}, u32[]{:S(2)}) collective-permute-start(bf16[8,1024]{1,0:T(8,128)(2,1)S(1)} %convolution_convert_fusion), channel_id=1, source_target_pairs={{0,3},{1,2},{2,5},{3,4},{4,7},{5,6},{6,9},{7,8},{8,11},{9,10},{10,... | collective-permute-start | bytes 49160 | tf_op jit(solution)/shard_map/ppermute | solution.py:525
  19.9 6.0 %collective-permute-start = (bf16[8,1024]{1,0:T(8,128)(2,1)S(1)}, bf16[8,1024]{1,0:T(8,128)(2,1)S(1)}, u32[]{:S(2)}, u32[]{:S(2)}) collective-permute-start(bf16[8,1024]{1,0:T(8,128)(2,1)S(1)} %convolution_convert_fusion), channel_id=1, source_target_pairs={{0,2},{1,3},{2,4},{3,5},{4,6},{5,7},{6,8},{7,9},{8,10},{9,11},{10,... | collective-permute-start | bytes 49160 | tf_op jit(solution)/shard_map/ppermute | solution.py:525
  19.9 1.2 %copy-start.2 = (bf16[2048,256]{1,0:T(8,128)(2,1)S(1)}, bf16[2048,256]{1,0:T(8,128)(2,1)}, u32[]{:S(2)}) copy-start(bf16[2048,256]{1,0:T(8,128)(2,1)} %refs_14_.1) | copy-start | bytes 3145732
  21.2 1.2 %copy-start.3 = (bf16[2048,256]{1,0:T(8,128)(2,1)S(1)}, bf16[2048,256]{1,0:T(8,128)(2,1)}, u32[]{:S(2)}) copy-start(bf16[2048,256]{1,0:T(8,128)(2,1)} %refs_14_.1) | copy-start | bytes 3145732
  29.5 2.2 %copy-start.4 = (bf16[128,256]{1,0:T(8,128)(2,1)S(1)}, bf16[128,256]{1,0:T(8,128)(2,1)}, u32[]{:S(2)}) copy-start(bf16[128,256]{1,0:T(8,128)(2,1)} %grad_ref.1) | copy-start | bytes 196612
  29.5 1.4 %collective-permute-start.3 = (bf16[2,128,256]{2,1,0:T(8,128)(2,1)S(1)}, bf16[2,128,256]{2,1,0:T(8,128)(2,1)S(1)}, u32[]{:S(2)}, u32[]{:S(2)}) collective-permute-start(bf16[2,128,256]{2,1,0:T(8,128)(2,1)S(1)} %get-tuple-element.139.own_ref), channel_id=1, source_target_pairs={{0,2},{2,0},{4,6},{6,4},{8,10},{10,8},{12,14},{14,12},{16,18},{18,... | collective-permute-start | bytes 393224 | tf_op jit(solution)/shard_map/ppermute | solution.py:517
  31.1 4.6 %collective-permute-start.4 = (bf16[2,128,256]{2,1,0:T(8,128)(2,1)S(1)}, bf16[2,128,256]{2,1,0:T(8,128)(2,1)S(1)}, u32[]{:S(2)}, u32[]{:S(2)}) collective-permute-start(bf16[2,128,256]{2,1,0:T(8,128)(2,1)S(1)} %get-tuple-element.140), channel_id=1, source_target_pairs={{0,4},{2,0},{4,8},{6,2},{8,12},{10,6},{12,16},{14,10},{16,20},{18,... | collective-permute-start | bytes 393224 | tf_op jit(solution)/shard_map/ppermute | solution.py:509
  31.4 4.3 %collective-permute-start.5 = (bf16[2,128,128]{2,1,0:T(8,128)(2,1)S(1)}, bf16[2,128,128]{2,1,0:T(8,128)(2,1)S(1)}, u32[]{:S(2)}, u32[]{:S(2)}) collective-permute-start(bf16[2,128,128]{2,1,0:T(8,128)(2,1)S(1)} %get-tuple-element.141), channel_id=1, source_target_pairs={{2,10},{0,2},{6,14},{4,6},{10,18},{8,0},{14,22},{12,4},{18,26},{16... | collective-permute-start | bytes 196616 | tf_op jit(solution)/shard_map/ppermute | solution.py:509
  31.7 0.7 %copy-start.7 = (f32[128]{0:T(128)S(1)}, f32[128]{0:T(128)}, u32[]{:S(2)}) copy-start(f32[128]{0:T(128)} %param.18) | copy-start | bytes 1540
  35.8 1.4 %collective-permute-start.6 = (bf16[2,128,256]{2,1,0:T(8,128)(2,1)S(1)}, bf16[2,128,256]{2,1,0:T(8,128)(2,1)S(1)}, u32[]{:S(2)}, u32[]{:S(2)}) collective-permute-start(bf16[2,128,256]{2,1,0:T(8,128)(2,1)S(1)} %give.1), channel_id=1, source_target_pairs={{0,2},{2,0},{4,6},{6,4},{8,10},{10,8},{12,14},{14,12},{16,18},{18,... | collective-permute-start | bytes 393224 | tf_op jit(solution)/shard_map/ppermute | solution.py:517
  38.3 1.3 %collective-permute-start.7 = (bf16[2,128,128]{2,1,0:T(8,128)(2,1)S(1)}, bf16[2,128,128]{2,1,0:T(8,128)(2,1)S(1)}, u32[]{:S(2)}, u32[]{:S(2)}) collective-permute-start(bf16[2,128,128]{2,1,0:T(8,128)(2,1)S(1)} %get-tuple-element.167), channel_id=1, source_target_pairs={{0,2},{2,0},{4,6},{6,4},{8,10},{10,8},{12,14},{14,12},{16,18},{18,... | collective-permute-start | bytes 196616 | tf_op jit(solution)/shard_map/ppermute | solution.py:517
  40.0 4.1 %collective-permute-start.8 = (bf16[2,128,128]{2,1,0:T(8,128)(2,1)S(1)}, bf16[2,128,128]{2,1,0:T(8,128)(2,1)S(1)}, u32[]{:S(2)}, u32[]{:S(2)}) collective-permute-start(bf16[2,128,128]{2,1,0:T(8,128)(2,1)S(1)} %get-tuple-element.170), channel_id=1, source_target_pairs={{0,8},{2,0},{4,12},{6,4},{8,16},{10,2},{12,20},{14,6},{16,24},{18,... | collective-permute-start | bytes 196616 | tf_op jit(solution)/shard_map/ppermute | solution.py:509
  42.2 4.3 %collective-permute-start.9 = (bf16[2,128,128]{2,1,0:T(8,128)(2,1)S(1)}, bf16[2,128,128]{2,1,0:T(8,128)(2,1)S(1)}, u32[]{:S(2)}, u32[]{:S(2)}) collective-permute-start(bf16[2,128,128]{2,1,0:T(8,128)(2,1)S(1)} %get-tuple-element.190), channel_id=1, source_target_pairs={{0,28},{2,30},{4,0},{6,2},{8,4},{10,6},{12,8},{14,10},{16,12},{18,... | collective-permute-start | bytes 196616 | tf_op jit(solution)/shard_map/ppermute | solution.py:513
  44.1 2.4 %collective-permute-start.10 = (bf16[2,128,128]{2,1,0:T(8,128)(2,1)S(1)}, bf16[2,128,128]{2,1,0:T(8,128)(2,1)S(1)}, u32[]{:S(2)}, u32[]{:S(2)}) collective-permute-start(bf16[2,128,128]{2,1,0:T(8,128)(2,1)S(1)} %collective-permute-done.8.refs_1_), channel_id=1, source_target_pairs={{0,2},{2,0},{4,6},{6,4},{8,10},{10,8},{12,14},{14,12},{16,18},{18,... | collective-permute-start | bytes 196616 | tf_op jit(solution)/shard_map/ppermute | solution.py:517
  48.0 8.8 %collective-permute-start.11 = (bf16[128,1024]{1,0:T(8,128)(2,1)S(1)}, bf16[128,1024]{1,0:T(8,128)(2,1)S(1)}, u32[]{:S(2)}, u32[]{:S(2)}) collective-permute-start(bf16[128,1024]{1,0:T(8,128)(2,1)S(1)} %get-tuple-element.205), channel_id=1, source_target_pairs={{0,1},{1,0},{2,3},{3,2},{4,5},{5,4},{6,7},{7,6},{8,9},{9,8},{10,11... | collective-permute-start | bytes 786440 | tf_op jit(solution)/shard_map/ppermute | solution.py:529
  49.6 7.2 %copy-start.6 = (bf16[2,128,8]{2,1,0:T(8,128)(2,1)S(1)}, bf16[2,128,8]{2,1,0:T(8,128)(2,1)}, u32[]{:S(2)}) copy-start(bf16[2,128,8]{2,1,0:T(8,128)(2,1)} %copy-done.5) | copy-start | bytes 12292
  50.1 5.0 %collective-permute-start.12 = (bf16[8,1024]{1,0:T(8,128)(2,1)S(1)}, bf16[8,1024]{1,0:T(8,128)(2,1)S(1)}, u32[]{:S(2)}, u32[]{:S(2)}) collective-permute-start(bf16[8,1024]{1,0:T(8,128)(2,1)S(1)} %get-tuple-element.206), channel_id=1, source_target_pairs={{0,30},{1,31},{2,0},{3,1},{4,2},{5,3},{6,4},{7,5},{8,6},{9,7},{10,... | collective-permute-start | bytes 49160 | tf_op jit(solution)/shard_map/ppermute | solution.py:525
  53.6 3.2 %collective-permute-start.13 = (bf16[8,1024]{1,0:T(8,128)(2,1)S(1)}, bf16[8,1024]{1,0:T(8,128)(2,1)S(1)}, u32[]{:S(2)}, u32[]{:S(2)}) collective-permute-start(bf16[8,1024]{1,0:T(8,128)(2,1)S(1)} %get-tuple-element.207), channel_id=1, source_target_pairs={{0,31},{1,30},{2,1},{3,0},{4,3},{5,2},{6,5},{7,4},{8,7},{9,6},{10,... | collective-permute-start | bytes 49160 | tf_op jit(solution)/shard_map/ppermute | solution.py:525

commit v3 on v1

--- a/solution.py
+++ b/solution.py
@@ -47,6 +47,14 @@
     right = jnp.concatenate(halves(b), axis=0)
     both = dot_nt(left, jnp.concatenate([right, right], axis=1))
     return both[:, :width] + both[:, width:]
+
+
+def rough(a, b):
+    return dot(a.astype(BF16), b.astype(BF16))
+
+
+def rough_nt(a, b):
+    return dot_nt(a.astype(BF16), b.astype(BF16))
 
 
 def begins(clips_ref, position):
@@ -330,7 +338,8 @@
         state = jnp.where(seq >= 2 * chips, maps[-1][head], 0.0)
         for index in range(chips - 2, -1, -1):
             earlier = maps[index][head]
-            state = earlier[:, dk:] + mm(earlier[:, :dk].astype(BF16), state)
+            step = rough if index == chips - 2 else mm
+            state = earlier[:, dk:] + step(earlier[:, :dk].astype(BF16), state)
             state = jnp.where(seq >= 2 * index + 2, state, 0.0)
         raw = local_ref[head] + mm(reach_ref[head], state)
         state_ref[head] = prefix_ref[head, :, dk:].astype(F32) + mm(prefix_ref[head, :, :dk], state)
@@ -340,7 +349,7 @@
         weighted = weighted_ref[head]
         dout = scale * (weighted - unit * jnp.mean(unit * weighted, axis=1, keepdims=True))
         dout_ref[head] = dout
-        back = mm(reach_t_ref[head], dout)
+        back = rough(reach_t_ref[head], dout)
         back_ref[head] = back
         send_ref[head] = back.astype(BF16)
         product = None
@@ -356,11 +365,11 @@
     for head in range(heads):
         own, other = own_ref[head], other_ref[head].astype(F32)
         late = jnp.where(upper, own, other)
-        joined = jnp.where(upper, other, own) + mm(early_t_ref[head], late)
+        joined = jnp.where(upper, other, own) + mm(early_t_ref[head].astype(BF16), late)
         later_ref[head] = jnp.where(upper, 0.0, other)
         sends[0][head] = joined.astype(BF16)
         for flip_ref, send in zip(flipped, sends[1:]):
-            send[head] = mm(flip_ref[head], joined).astype(BF16)
+            send[head] = rough(flip_ref[head], joined).astype(BF16)
 
 
 def query_kernel(heads, mask_ref, dout_ref, state_ref, w_ref, score_t_ref, q_ref, k_ref, solve_t_ref,
@@ -409,13 +418,13 @@
         k_scale = aux_ref[:, 4 * head + 1 : 4 * head + 2]
         rate = aux_ref[:, 4 * head + 2 : 4 * head + 3]
         slope = aux_ref[:, 4 * head + 3 : 4 * head + 4]
-        y = y_ref[head] + mm(reach_ref[head], after)
-        both = mm_nt(y, jnp.concatenate([state_ref[head], fresh], axis=0))
+        y = y_ref[head] + rough(reach_ref[head], after)
+        both = rough_nt(y, jnp.concatenate([state_ref[head], fresh], axis=0))
         from_state = -carried * both[:, :dk]
         system = strict * -both[:, dk:]
         scaled = rate * system
-        dkey = dk0_ref[head] + mm_nt(mm_nt(final * fresh, after), suffix_t_ref[head])
-        dkey = dkey + mm(scaled + scaled.T, key) + rate * from_state
+        dkey = dk0_ref[head] + rough_nt(rough_nt(final * fresh, after), suffix_t_ref[head])
+        dkey = dkey + rough(scaled + scaled.T, key) + rate * from_state
         drate = jnp.sum(
             system * gram_ref[head] + from_state * key + y * v_ref[head], axis=1, keepdims=True
         )

time: 57.6 us -> 57.3 us (level)
  no operation moved by 1% of the time
where the time goes in v3:
time: 57.3 us; the launch traced here: 56.9 us
  starting transfers between devices  19 us (33%)
  waiting for transfers between devices  18.5 us (32%)
  Pallas kernels  12.7 us (22%)
  local copies, waits for them, and re-layouts  5.73 us (10%)
  between operations  0.85 us (1%)
    pallas_call x14, Pallas kernels, call(): pl.pallas_call(body, name=name, out_shape=tuple(outs), in_specs=[SMEM] *...  12.7 us
    all_to_all x1, starting transfers between devices, on_device(): lax.all_to_all(loaded.reshape(count, rows_each, local), 'seq', split_axis...  7.5 us
    all_to_all x1, waiting for transfers between devices, on_device(): lax.all_to_all(loaded.reshape(count, rows_each, local), 'seq', split_axis...  5.43 us
    ppermute x4, waiting for transfers between devices, corner_shift(): return lax.ppermute(x, ('seq', 'head'), pairs)  4.92 us
    unnamed x25, local copies, waits for them, and re-layouts  4.54 us
    ppermute x2, starting transfers between devices, seq_shift(): return lax.ppermute(x, 'seq', [(i, (i + by) % count) for i in range(count)])  4.01 us
    ppermute x3, waiting for transfers between devices, core_swap(): return lax.ppermute(x, 'seq', [(i, i ^ 1) for i in range(count)])  3.78 us
    ppermute x4, starting transfers between devices, corner_shift(): return lax.ppermute(x, ('seq', 'head'), pairs)  3.46 us
  transfers between devices with their start and end apart: 14, of which 10 were waited for; matrix products, arithmetic and copies ran while one was open for 6% of the time, Pallas kernels for 10%

profile of v3, /device:TPU:0, one launch (start us, length us, event | category | flops | bytes accessed | tf_op | source)
XLA Modules:
  0.0 56.9 jit_solution(9228595672337139520)
XLA Ops:
  0.6 7.5 %all-to-all-start = ((bf16[16,8,1024]{2,1,0:T(8,128)(2,1)}), bf16[16,8,1024]{2,1,0:T(8,128)(2,1)S(1)}, u32[]{:S(2)}, u32[]{:S(2)}) async-start(bf16[16,8,1024]{2,1,0:T(8,128)(2,1)} %bitcast.9), calls=%async_computation | async-start | bytes 524288 | tf_op jit(solution)/shard_map/all_to_all | solution.py:555
  8.1 0.0 copy-start
  8.2 1.8 %copy.13 = bf16[2048,2]{1,0:T(8,128)(2,1)} copy(bf16[2048,2]{0,1:T(2,128)(2,1)} %param.16) | data formatting | bytes 16384 | tf_op args[5]
  10.0 1.2 %pad.4.refs_3_.refs_15_ = bf16[2048,128]{1,0:T(8,128)(2,1)S(1)} pad(bf16[2048,2]{1,0:T(8,128)(2,1)} %copy.13, bf16[]{:T(256)} %constant.2.clone.1), padding=0_0x0_126 | pad | bytes 532482 | tf_op jit(solution)/shard_map/jit(_pad)/pad | solution.py:552
  11.3 0.9 %prepare.1 = (bf16[4,128,128]{2,1,0:T(8,128)(2,1)S(1)}, bf16[4,128,8]{2,1,0:T(8,128)(2,1)S(1)}, bf16[8,128]{1,0:T(8,128)(2,1)S(1)}, bf16[2,128,128]{2,1,0:T(8,12...) custom-call(s32[1,16]{1,0:T(1,128)S(1)} %copy-done.8, ...), custom_call_target="tpu_custom_call" | custom-call | bytes 539648 | tf_op jit(solution)/shard_map/prepare/pallas_call | solution.py:493
  12.1 0.0 copy-start.5
  12.1 0.6 %copy-done.5 = bf16[2,128,8]{2,1,0:T(8,128)(2,1)} copy-done((bf16[2,128,8]{2,1,0:T(8,128)(2,1)}, bf16[2,128,8]{2,1,0:T(8,128)(2,1)S(1)}, u32[]{:S(2)}) %copy-start.5) | copy-done | bytes 4120
  12.8 5.4 %all-to-all-done = bf16[16,8,1024]{2,1,0:T(8,128)(2,1)S(1)} async-done(((bf16[16,8,1024]{2,1,0:T(8,128)(2,1)}), bf16[16,8,1024]{2,1,0:T(8,128)(2,1)S(1)}, u32[]{:S(2)}, u32[]{:S(2)}) %all-to-all-start) | async-done | bytes 262176 | tf_op jit(solution)/shard_map/all_to_all | solution.py:555
  18.2 1.5 %collective-permute-start.1 = (bf16[128,1024]{1,0:T(8,128)(2,1)S(1)}, bf16[128,1024]{1,0:T(8,128)(2,1)S(1)}, u32[]{:S(2)}, u32[]{:S(2)}) collective-permute-start(bf16[128,1024]{1,0:T(8,128)(2,1)S(1)} %bitcast.5), channel_id=1, source_target_pairs={{0,1},{1,0},{2,3},{3,2},{4,5},{5,4},{6,7},{7,6},{8,9},{9,8},{10,11... | collective-permute-start | bytes 786440 | tf_op jit(solution)/shard_map/ppermute | solution.py:536
  19.7 0.1 convolution_convert_fusion
  19.9 0.0 collective-permute-start.2
  19.9 0.0 collective-permute-start
  19.9 0.0 copy-start.2
  19.9 1.2 %copy-done.2 = bf16[2048,256]{1,0:T(8,128)(2,1)S(1)} copy-done((bf16[2048,256]{1,0:T(8,128)(2,1)S(1)}, bf16[2048,256]{1,0:T(8,128)(2,1)}, u32[]{:S(2)}) %copy-start.2) | copy-done | bytes 1048600
  21.2 1.1 %flip.1 = (bf16[256,2048]{1,0:T(8,128)(2,1)S(1)}, bf16[256,2048]{1,0:T(8,128)(2,1)S(1)}, bf16[256,2048]{1,0:T(8,128)(2,1)S(1)}, bf16[128,2048]{1,0:T(8,128)(2,1)S(1)}) custom-call(bf16[2048,256]{1,0:T(8,128)(2,1)S(1)} %copy-done, bf16[2048,256]{1,0:T(8,128)(2,1)S(1)} %copy-done.1, bf16[2048,256]{1,0:T(8,128)(2,1)S(1)} %copy-done.2, ...), custom_call_target="tpu_custom_call" | custom-call | bytes 7340032 | tf_op jit(solution)/shard_map/flip/pallas_call | solution.py:493
  22.2 0.2 copy-done.3
  22.4 0.6 %project_own.1 = (f32[128,256]{1,0:T(8,128)S(1)}, f32[128,256]{1,0:T(8,128)S(1)}, f32[128,256]{1,0:T(8,128)S(1)}, f32[128,128]{1,0:T(8,128)S(1)}) custom-call(bf16[128,1024]{1,0:T(8,128)(2,1)S(1)} %bitcast.7, bf16[4,128,128]{2,1,0:T(8,128)(2,1)S(1)} %get-tuple-element.108.pick_ref.refs_10_, bf16[4,128,8]{2,1,0:T(8,128)(2,1)S(1)} %get-tuple-element.109.edge_ref.refs_11_, ...), custom_call_target="tpu_custom_call" | custom-call | flops 234881024 | bytes 4530176 | tf_op jit(solution)/shard_map/project_own/pallas_call | solution.py:493
  23.0 2.8 %collective-permute-done.halo_ref = bf16[8,1024]{1,0:T(8,128)(2,1)S(1)} collective-permute-done((bf16[8,1024]{1,0:T(8,128)(2,1)S(1)}, bf16[8,1024]{1,0:T(8,128)(2,1)S(1)}, u32[]{:S(2)}, u32[]{:S(2)}) %collective-permute-start) | collective-permute-done | bytes 16416 | tf_op jit(solution)/shard_map/ppermute | solution.py:532
  25.8 0.4 project_halo.1
  26.3 0.3 collective-permute-done.2.refs_9_
  26.6 2.9 %project.1 = (bf16[2,128,256]{2,1,0:T(8,128)(2,1)S(1)}, f32[2,128,128]{2,1,0:T(8,128)S(1)}, f32[2,128,128]{2,1,0:T(8,128)S(1)}, f32[2,128,128]{2,1,0:T(8,128)S(1...) custom-call(f32[5,128,128]{2,1,0:T(8,128)S(1)} %get-tuple-element.105.mask_ref, ...), custom_call_target="tpu_custom_call" | custom-call | flops 234881024 | bytes 5915648 | tf_op jit(solution)/shard_map/project/pallas_call | solution.py:493
  29.5 0.0 copy-start.4
  29.5 0.1 collective-permute-start.3
  29.6 1.3 %collective-permute-done.3.other_ref = bf16[2,128,256]{2,1,0:T(8,128)(2,1)S(1)} collective-permute-done((bf16[2,128,256]{2,1,0:T(8,128)(2,1)S(1)}, bf16[2,128,256]{2,1,0:T(8,128)(2,1)S(1)}, u32[]{:S(2)}, u32[]{:S(2)}) %collective-permute-start.3) | collective-permute-done | bytes 131104 | tf_op jit(solution)/shard_map/ppermute | solution.py:524
  30.9 0.2 join.1
  31.2 0.3 collective-permute-start.4
  31.4 0.3 collective-permute-start.5
  31.7 0.7 %copy-done.7 = f32[128]{0:T(128)S(1)} copy-done((f32[128]{0:T(128)S(1)}, f32[128]{0:T(128)}, u32[]{:S(2)}) %copy-start.7) | copy-done | bytes 536
  32.4 0.9 %local_terms.1 = (f32[2,128,128]{2,1,0:T(8,128)S(1)}, f32[2,128,128]{2,1,0:T(8,128)S(1)}, f32[2,128,128]{2,1,0:T(8,128)S(1)}, f32[2,128,128]{2,1,0:T(8,128)S(1)}...) custom-call(f32[5,128,128]{2,1,0:T(8,128)S(1)} %get-tuple-element.10, ...), custom_call_target="tpu_custom_call" | custom-call | flops 200000000 | bytes 2622464 | tf_op jit(solution)/shard_map/local_terms/pallas_call | solution.py:493
  33.3 2.5 %collective-permute-done.5.odd_ref.refs_1_ = bf16[2,128,128]{2,1,0:T(8,128)(2,1)S(1)} collective-permute-done((bf16[2,128,128]{2,1,0:T(8,128)(2,1)S(1)}, bf16[2,128,128]{2,1,0:T(8,128)(2,1)S(1)}, u32[]{:S(2)}, u32[]{:S(2)}) %collective-permute-start.5) | collective-permute-done | bytes 65568 | tf_op jit(solution)/shard_map/ppermute | solution.py:516
  35.8 0.1 collective-permute-start.6
  35.9 1.3 %collective-permute-done.6.refs_2_ = bf16[2,128,256]{2,1,0:T(8,128)(2,1)S(1)} collective-permute-done((bf16[2,128,256]{2,1,0:T(8,128)(2,1)S(1)}, bf16[2,128,256]{2,1,0:T(8,128)(2,1)S(1)}, u32[]{:S(2)}, u32[]{:S(2)}) %collective-permute-start.6) | collective-permute-done | bytes 131104 | tf_op jit(solution)/shard_map/ppermute | solution.py:524
  37.2 1.0 %outputs.1 = (f32[2,128,128]{2,1,0:T(8,128)S(1)}, f32[2,128,128]{2,1,0:T(8,128)S(1)}, f32[2,128,128]{2,1,0:T(8,128)S(1)}, f32[2,128,128]{2,1,0:T(8,128)S(1)}, bf...) custom-call(bf16[2,128,256]{2,1,0:T(8,128)(2,1)S(1)} %collective-permute-done.4.even_ref.refs_0_, ...), custom_call_target="tpu_custom_call" | custom-call | flops 200000000 | bytes 1703936 | tf_op jit(solution)/shard_map/outputs/pallas_call | solution.py:493
  38.2 0.2 collective-permute-start.7
  38.4 1.1 %collective-permute-done.7.other_ref = bf16[2,128,128]{2,1,0:T(8,128)(2,1)S(1)} collective-permute-done((bf16[2,128,128]{2,1,0:T(8,128)(2,1)S(1)}, bf16[2,128,128]{2,1,0:T(8,128)(2,1)S(1)}, u32[]{:S(2)}, u32[]{:S(2)}) %collective-permute-start.7) | collective-permute-done | bytes 65568 | tf_op jit(solution)/shard_map/ppermute | solution.py:524
  39.5 0.5 join_back.1
  40.0 2.2 %collective-permute-start.8 = (bf16[2,128,128]{2,1,0:T(8,128)(2,1)S(1)}, bf16[2,128,128]{2,1,0:T(8,128)(2,1)S(1)}, u32[]{:S(2)}, u32[]{:S(2)}) collective-permute-start(bf16[2,128,128]{2,1,0:T(8,128)(2,1)S(1)} %get-tuple-element.176), channel_id=1, source_target_pairs={{0,28},{2,30},{4,0},{6,2},{8,4},{10,6},{12,8},{14,10},{16,12},{18,... | collective-permute-start | bytes 196616 | tf_op jit(solution)/shard_map/ppermute | solution.py:520
  42.2 1.8 %collective-permute-start.9 = (bf16[2,128,128]{2,1,0:T(8,128)(2,1)S(1)}, bf16[2,128,128]{2,1,0:T(8,128)(2,1)S(1)}, u32[]{:S(2)}, u32[]{:S(2)}) collective-permute-start(bf16[2,128,128]{2,1,0:T(8,128)(2,1)S(1)} %get-tuple-element.177), channel_id=1, source_target_pairs={{0,24},{2,26},{4,28},{6,30},{8,0},{10,2},{12,4},{14,6},{16,8},{18,... | collective-permute-start | bytes 196616 | tf_op jit(solution)/shard_map/ppermute | solution.py:520
  44.0 1.7 %query_grad.1 = (bf16[128,256]{1,0:T(8,128)(2,1)}, bf16[128,256]{1,0:T(8,128)(2,1)S(1)}, f32[2,128,128]{2,1,0:T(8,128)S(1)}, f32[2,128,128]{2,1,0:T(8,128)S(1)},...) custom-call(f32[5,128,128]{2,1,0:T(8,128)S(1)} %get-tuple-element.105.mask_ref, ...), custom_call_target="tpu_custom_call" | custom-call | flops 200000000 | bytes 2621952 | tf_op jit(solution)/shard_map/query_grad/pallas_call | solution.py:493
  45.7 1.4 %collective-permute-done.9.refs_1_ = bf16[2,128,128]{2,1,0:T(8,128)(2,1)S(1)} collective-permute-done((bf16[2,128,128]{2,1,0:T(8,128)(2,1)S(1)}, bf16[2,128,128]{2,1,0:T(8,128)(2,1)S(1)}, u32[]{:S(2)}, u32[]{:S(2)}) %collective-permute-start.9) | collective-permute-done | bytes 65568 | tf_op jit(solution)/shard_map/ppermute | solution.py:520
  47.1 1.2 %key_grad.1 = (bf16[128,1024]{1,0:T(8,128)(2,1)S(1)}, bf16[8,1024]{1,0:T(8,128)(2,1)S(1)}, bf16[128,896]{1,0:T(8,128)(2,1)S(1)}) custom-call(f32[5,128,128]{2,1,0:T(8,128)S(1)} %get-tuple-element.105.mask_ref, bf16[2,128,128]{2,1,0:T(8,128)(2,1)S(1)} %collective-permute-done.8.refs_0_, bf16[2,128,128]{2,1,0:T(8,128)(2,1)S(1)} %collective-permute-done.9.refs_1_, ...), custom_call_target="tpu_custom_call" | custom-call | flops 200000000 | bytes 5947392 | tf_op jit(solution)/shard_map/key_grad/pallas_call | solution.py:493
  48.3 1.6 %collective-permute-start.10 = (bf16[128,1024]{1,0:T(8,128)(2,1)S(1)}, bf16[128,1024]{1,0:T(8,128)(2,1)S(1)}, u32[]{:S(2)}, u32[]{:S(2)}) collective-permute-start(bf16[128,1024]{1,0:T(8,128)(2,1)S(1)} %get-tuple-element.191), channel_id=1, source_target_pairs={{0,1},{1,0},{2,3},{3,2},{4,5},{5,4},{6,7},{7,6},{8,9},{9,8},{10,11... | collective-permute-start | bytes 786440 | tf_op jit(solution)/shard_map/ppermute | solution.py:536
  49.9 0.4 own_back.1
  50.3 1.6 %collective-permute-start.11 = (bf16[8,1024]{1,0:T(8,128)(2,1)S(1)}, bf16[8,1024]{1,0:T(8,128)(2,1)S(1)}, u32[]{:S(2)}, u32[]{:S(2)}) collective-permute-start(bf16[8,1024]{1,0:T(8,128)(2,1)S(1)} %get-tuple-element.192), channel_id=1, source_target_pairs={{0,30},{1,31},{2,0},{3,1},{4,2},{5,3},{6,4},{7,5},{8,6},{9,7},{10,... | collective-permute-start | bytes 49160 | tf_op jit(solution)/shard_map/ppermute | solution.py:532
  51.9 1.8 %collective-permute-start.12 = (bf16[8,1024]{1,0:T(8,128)(2,1)S(1)}, bf16[8,1024]{1,0:T(8,128)(2,1)S(1)}, u32[]{:S(2)}, u32[]{:S(2)}) collective-permute-start(bf16[8,1024]{1,0:T(8,128)(2,1)S(1)} %get-tuple-element.193), channel_id=1, source_target_pairs={{0,31},{1,30},{2,1},{3,0},{4,3},{5,2},{6,5},{7,4},{8,7},{9,6},{10,... | collective-permute-start | bytes 49160 | tf_op jit(solution)/shard_map/ppermute | solution.py:532
  53.8 1.7 %collective-permute-done.12.refs_2_ = bf16[8,1024]{1,0:T(8,128)(2,1)S(1)} collective-permute-done((bf16[8,1024]{1,0:T(8,128)(2,1)S(1)}, bf16[8,1024]{1,0:T(8,128)(2,1)S(1)}, u32[]{:S(2)}, u32[]{:S(2)}) %collective-permute-start.12) | collective-permute-done | bytes 16416 | tf_op jit(solution)/shard_map/ppermute | solution.py:532
  55.5 0.5 collective-permute-done.10.refs_0_
  56.0 0.9 %finish.1 = bf16[128,1024]{1,0:T(8,128)(2,1)} custom-call(bf16[2,128,128]{2,1,0:T(8,128)(2,1)S(1)} %get-tuple-element.174.pick_ref, bf16[2,128,8]{2,1,0:T(8,128)(2,1)S(1)} %copy-done.6, f32[128,1024]{1,0:T(8,128)S(1)} %get-tuple-element.190.mine_ref, bf16[128,1024]{1,0:T(8,128)(2,1)S(1)} %collective-permute-done.10.refs_0_, ...), custom_call_target="tpu_custom_call" | custom-call | flops 100000000 | bytes 1150976 | tf_op jit(solution)/shard_map/finish/pallas_call | solution.py:493
  (21 shorter events, 0.1 us)
Async XLA Ops:
  0.6 19.3 %copy-start.1 = (bf16[2048,256]{1,0:T(8,128)(2,1)S(1)}, bf16[2048,256]{1,0:T(8,128)(2,1)}, u32[]{:S(2)}) copy-start(bf16[2048,256]{1,0:T(8,128)(2,1)} %refs_13_.1) | copy-start | bytes 3145732
  0.6 17.6 %all-to-all-start = ((bf16[16,8,1024]{2,1,0:T(8,128)(2,1)}), bf16[16,8,1024]{2,1,0:T(8,128)(2,1)S(1)}, u32[]{:S(2)}, u32[]{:S(2)}) async-start(bf16[16,8,1024]{2,1,0:T(8,128)(2,1)} %bitcast.9), calls=%async_computation | async-start | bytes 524288 | tf_op jit(solution)/shard_map/all_to_all | solution.py:555
  8.1 11.8 %copy-start = (bf16[2048,256]{1,0:T(8,128)(2,1)S(1)}, bf16[2048,256]{1,0:T(8,128)(2,1)}, u32[]{:S(2)}) copy-start(bf16[2048,256]{1,0:T(8,128)(2,1)} %refs_12_.1) | copy-start | bytes 3145732
  10.0 1.2 %copy-start.8 = (s32[1,16]{1,0:T(1,128)S(1)}, s32[1,16]{1,0:T(1,128)}, u32[]{:S(2)}) copy-start(s32[1,16]{1,0:T(1,128)} %order_ref.1) | copy-start | bytes 196
  10.0 1.2 %copy-start.9 = (s32[16]{0:T(128)S(1)}, s32[16]{0:T(128)}, u32[]{:S(2)}) copy-start(s32[16]{0:T(128)} %clips_ref.1) | copy-start | bytes 196
  10.0 1.2 %copy-start.10 = (s32[4]{0:T(128)S(1)}, s32[4]{0:T(128)}, u32[]{:S(2)}) copy-start(s32[4]{0:T(128)} %delays_ref.1) | copy-start | bytes 52
  10.0 1.2 %copy-start.11 = (f32[2]{0:T(128)S(1)}, f32[2]{0:T(128)}, u32[]{:S(2)}) copy-start(f32[2]{0:T(128)} %cap_ref.1) | copy-start | bytes 28
  12.1 0.6 %copy-start.5 = (bf16[2,128,8]{2,1,0:T(8,128)(2,1)}, bf16[2,128,8]{2,1,0:T(8,128)(2,1)S(1)}, u32[]{:S(2)}) copy-start(bf16[2,128,8]{2,1,0:T(8,128)(2,1)S(1)} %get-tuple-element.175.edge_ref) | copy-start | bytes 12292
  18.2 8.4 %collective-permute-start.1 = (bf16[128,1024]{1,0:T(8,128)(2,1)S(1)}, bf16[128,1024]{1,0:T(8,128)(2,1)S(1)}, u32[]{:S(2)}, u32[]{:S(2)}) collective-permute-start(bf16[128,1024]{1,0:T(8,128)(2,1)S(1)} %bitcast.5), channel_id=1, source_target_pairs={{0,1},{1,0},{2,3},{3,2},{4,5},{5,4},{6,7},{7,6},{8,9},{9,8},{10,11... | collective-permute-start | bytes 786440 | tf_op jit(solution)/shard_map/ppermute | solution.py:536
  19.9 6.8 %collective-permute-start.2 = (bf16[8,1024]{1,0:T(8,128)(2,1)S(1)}, bf16[8,1024]{1,0:T(8,128)(2,1)S(1)}, u32[]{:S(2)}, u32[]{:S(2)}) collective-permute-start(bf16[8,1024]{1,0:T(8,128)(2,1)S(1)} %convolution_convert_fusion), channel_id=1, source_target_pairs={{0,3},{1,2},{2,5},{3,4},{4,7},{5,6},{6,9},{7,8},{8,11},{9,10},{10,... | collective-permute-start | bytes 49160 | tf_op jit(solution)/shard_map/ppermute | solution.py:532
  19.9 6.0 %collective-permute-start = (bf16[8,1024]{1,0:T(8,128)(2,1)S(1)}, bf16[8,1024]{1,0:T(8,128)(2,1)S(1)}, u32[]{:S(2)}, u32[]{:S(2)}) collective-permute-start(bf16[8,1024]{1,0:T(8,128)(2,1)S(1)} %convolution_convert_fusion), channel_id=1, source_target_pairs={{0,2},{1,3},{2,4},{3,5},{4,6},{5,7},{6,8},{7,9},{8,10},{9,11},{10,... | collective-permute-start | bytes 49160 | tf_op jit(solution)/shard_map/ppermute | solution.py:532
  19.9 1.2 %copy-start.2 = (bf16[2048,256]{1,0:T(8,128)(2,1)S(1)}, bf16[2048,256]{1,0:T(8,128)(2,1)}, u32[]{:S(2)}) copy-start(bf16[2048,256]{1,0:T(8,128)(2,1)} %refs_14_.1) | copy-start | bytes 3145732
  21.2 1.2 %copy-start.3 = (bf16[2048,256]{1,0:T(8,128)(2,1)S(1)}, bf16[2048,256]{1,0:T(8,128)(2,1)}, u32[]{:S(2)}) copy-start(bf16[2048,256]{1,0:T(8,128)(2,1)} %refs_14_.1) | copy-start | bytes 3145732
  29.5 2.2 %copy-start.4 = (bf16[128,256]{1,0:T(8,128)(2,1)S(1)}, bf16[128,256]{1,0:T(8,128)(2,1)}, u32[]{:S(2)}) copy-start(bf16[128,256]{1,0:T(8,128)(2,1)} %grad_ref.1) | copy-start | bytes 196612
  29.5 1.4 %collective-permute-start.3 = (bf16[2,128,256]{2,1,0:T(8,128)(2,1)S(1)}, bf16[2,128,256]{2,1,0:T(8,128)(2,1)S(1)}, u32[]{:S(2)}, u32[]{:S(2)}) collective-permute-start(bf16[2,128,256]{2,1,0:T(8,128)(2,1)S(1)} %get-tuple-element.132.own_ref), channel_id=1, source_target_pairs={{0,2},{2,0},{4,6},{6,4},{8,10},{10,8},{12,14},{14,12},{16,18},{18,... | collective-permute-start | bytes 393224 | tf_op jit(solution)/shard_map/ppermute | solution.py:524
  31.2 4.6 %collective-permute-start.4 = (bf16[2,128,256]{2,1,0:T(8,128)(2,1)S(1)}, bf16[2,128,256]{2,1,0:T(8,128)(2,1)S(1)}, u32[]{:S(2)}, u32[]{:S(2)}) collective-permute-start(bf16[2,128,256]{2,1,0:T(8,128)(2,1)S(1)} %get-tuple-element.133), channel_id=1, source_target_pairs={{0,4},{2,0},{4,8},{6,2},{8,12},{10,6},{12,16},{14,10},{16,20},{18,... | collective-permute-start | bytes 393224 | tf_op jit(solution)/shard_map/ppermute | solution.py:516
  31.4 4.3 %collective-permute-start.5 = (bf16[2,128,128]{2,1,0:T(8,128)(2,1)S(1)}, bf16[2,128,128]{2,1,0:T(8,128)(2,1)S(1)}, u32[]{:S(2)}, u32[]{:S(2)}) collective-permute-start(bf16[2,128,128]{2,1,0:T(8,128)(2,1)S(1)} %get-tuple-element.134), channel_id=1, source_target_pairs={{2,10},{0,2},{6,14},{4,6},{10,18},{8,0},{14,22},{12,4},{18,26},{16... | collective-permute-start | bytes 196616 | tf_op jit(solution)/shard_map/ppermute | solution.py:516
  31.7 0.7 %copy-start.7 = (f32[128]{0:T(128)S(1)}, f32[128]{0:T(128)}, u32[]{:S(2)}) copy-start(f32[128]{0:T(128)} %param.18) | copy-start | bytes 1540
  35.8 1.4 %collective-permute-start.6 = (bf16[2,128,256]{2,1,0:T(8,128)(2,1)S(1)}, bf16[2,128,256]{2,1,0:T(8,128)(2,1)S(1)}, u32[]{:S(2)}, u32[]{:S(2)}) collective-permute-start(bf16[2,128,256]{2,1,0:T(8,128)(2,1)S(1)} %give.1), channel_id=1, source_target_pairs={{0,2},{2,0},{4,6},{6,4},{8,10},{10,8},{12,14},{14,12},{16,18},{18,... | collective-permute-start | bytes 393224 | tf_op jit(solution)/shard_map/ppermute | solution.py:524
  38.2 1.3 %collective-permute-start.7 = (bf16[2,128,128]{2,1,0:T(8,128)(2,1)S(1)}, bf16[2,128,128]{2,1,0:T(8,128)(2,1)S(1)}, u32[]{:S(2)}, u32[]{:S(2)}) collective-permute-start(bf16[2,128,128]{2,1,0:T(8,128)(2,1)S(1)} %get-tuple-element.169), channel_id=1, source_target_pairs={{0,2},{2,0},{4,6},{6,4},{8,10},{10,8},{12,14},{14,12},{16,18},{18,... | collective-permute-start | bytes 196616 | tf_op jit(solution)/shard_map/ppermute | solution.py:524
  40.0 5.7 %collective-permute-start.8 = (bf16[2,128,128]{2,1,0:T(8,128)(2,1)S(1)}, bf16[2,128,128]{2,1,0:T(8,128)(2,1)S(1)}, u32[]{:S(2)}, u32[]{:S(2)}) collective-permute-start(bf16[2,128,128]{2,1,0:T(8,128)(2,1)S(1)} %get-tuple-element.176), channel_id=1, source_target_pairs={{0,28},{2,30},{4,0},{6,2},{8,4},{10,6},{12,8},{14,10},{16,12},{18,... | collective-permute-start | bytes 196616 | tf_op jit(solution)/shard_map/ppermute | solution.py:520
  42.2 4.9 %collective-permute-start.9 = (bf16[2,128,128]{2,1,0:T(8,128)(2,1)S(1)}, bf16[2,128,128]{2,1,0:T(8,128)(2,1)S(1)}, u32[]{:S(2)}, u32[]{:S(2)}) collective-permute-start(bf16[2,128,128]{2,1,0:T(8,128)(2,1)S(1)} %get-tuple-element.177), channel_id=1, source_target_pairs={{0,24},{2,26},{4,28},{6,30},{8,0},{10,2},{12,4},{14,6},{16,8},{18,... | collective-permute-start | bytes 196616 | tf_op jit(solution)/shard_map/ppermute | solution.py:520
  48.3 7.7 %collective-permute-start.10 = (bf16[128,1024]{1,0:T(8,128)(2,1)S(1)}, bf16[128,1024]{1,0:T(8,128)(2,1)S(1)}, u32[]{:S(2)}, u32[]{:S(2)}) collective-permute-start(bf16[128,1024]{1,0:T(8,128)(2,1)S(1)} %get-tuple-element.191), channel_id=1, source_target_pairs={{0,1},{1,0},{2,3},{3,2},{4,5},{5,4},{6,7},{7,6},{8,9},{9,8},{10,11... | collective-permute-start | bytes 786440 | tf_op jit(solution)/shard_map/ppermute | solution.py:536
  49.9 6.1 %copy-start.6 = (bf16[2,128,8]{2,1,0:T(8,128)(2,1)S(1)}, bf16[2,128,8]{2,1,0:T(8,128)(2,1)}, u32[]{:S(2)}) copy-start(bf16[2,128,8]{2,1,0:T(8,128)(2,1)} %copy-done.5) | copy-start | bytes 12292
  50.3 3.4 %collective-permute-start.11 = (bf16[8,1024]{1,0:T(8,128)(2,1)S(1)}, bf16[8,1024]{1,0:T(8,128)(2,1)S(1)}, u32[]{:S(2)}, u32[]{:S(2)}) collective-permute-start(bf16[8,1024]{1,0:T(8,128)(2,1)S(1)} %get-tuple-element.192), channel_id=1, source_target_pairs={{0,30},{1,31},{2,0},{3,1},{4,2},{5,3},{6,4},{7,5},{8,6},{9,7},{10,... | collective-permute-start | bytes 49160 | tf_op jit(solution)/shard_map/ppermute | solution.py:532
  51.9 3.6 %collective-permute-start.12 = (bf16[8,1024]{1,0:T(8,128)(2,1)S(1)}, bf16[8,1024]{1,0:T(8,128)(2,1)S(1)}, u32[]{:S(2)}, u32[]{:S(2)}) collective-permute-start(bf16[8,1024]{1,0:T(8,128)(2,1)S(1)} %get-tuple-element.193), channel_id=1, source_target_pairs={{0,31},{1,30},{2,1},{3,0},{4,3},{5,2},{6,5},{7,4},{8,7},{9,6},{10,... | collective-permute-start | bytes 49160 | tf_op jit(solution)/shard_map/ppermute | solution.py:532

commit v4 on v3

--- a/solution.py
+++ b/solution.py
@@ -245,7 +245,7 @@
         ended = jnp.concatenate(
             [-(final * carried) * solved[:, :dk], final * solved[:, dk:]], axis=1
         )
-        affine = mm(keys[head].T, ended)
+        affine = rough(keys[head].T, ended)
         map_ref[head, :, :dk] = (affine[:, :dk] + eye).astype(BF16)
         map_ref[head, :, dk:] = affine[:, dk:].astype(BF16)
 
@@ -317,8 +317,7 @@
             give_ref[head, :, :-width] = even_ref[head, :, :-width]
 
 
-def output_kernel(heads, chips, *refs):
-    rows, swapped, refs = refs[:chips], refs[chips : chips + chips // 2], refs[chips + chips // 2 :]
+def shared_maps(heads, rows, swapped):
     maps = []
     upper = is_upper()
     for index, row in enumerate(rows):
@@ -329,9 +328,29 @@
             jnp.where(mine, row[head].astype(F32), other[head, :, -width:].astype(F32))
             for head in range(heads)
         ])
+    return maps
+
+
+def chain_kernel(heads, chips, *refs):
+    rows, swapped, refs = refs[:chips], refs[chips : chips + chips // 2], refs[chips + chips // 2 :]
+    maps = shared_maps(heads, rows[:-1], swapped)
+    early_t_ref, flipped, chained = refs[0], refs[1:chips], refs[chips:]
+    dk = early_t_ref.shape[1]
+    for head in range(heads):
+        product = None
+        for earlier, flip_ref, chain_ref in zip(maps, flipped, chained):
+            move = earlier[head][:, :dk]
+            product = move if product is None else mm(product, move)
+            flip = product.T
+            flip_ref[head] = flip
+            chain_ref[head] = rough(flip, early_t_ref[head])
+
+
+def output_kernel(heads, chips, *refs):
+    rows, swapped, refs = refs[:chips], refs[chips : chips + chips // 2], refs[chips + chips // 2 :]
+    maps = shared_maps(heads, rows, swapped)
     (prefix_ref, reach_ref, reach_t_ref, local_ref, weighted_ref,
-     state_ref, unit_ref, dout_ref, back_ref, send_ref) = refs[:10]
-    flipped = refs[10:]
+     state_ref, unit_ref, dout_ref, back_ref, send_ref) = refs
     seq = here()[0]
     dk = reach_ref.shape[2]
     for head in range(heads):
@@ -352,24 +371,20 @@
         back = rough(reach_t_ref[head], dout)
         back_ref[head] = back
         send_ref[head] = back.astype(BF16)
-        product = None
-        for earlier, flip_ref in zip(maps, flipped):
-            move = earlier[head][:, :dk]
-            product = move if product is None else mm(product, move)
-            flip_ref[head] = product.T
 
 
 def join_back_kernel(heads, chips, own_ref, other_ref, early_t_ref, *refs):
-    flipped, later_ref, sends = refs[: chips - 1], refs[chips - 1], refs[chips:]
+    flipped, chained = refs[: chips - 1], refs[chips - 1 : 2 * chips - 2]
+    later_ref, sends = refs[2 * chips - 2], refs[2 * chips - 1 :]
     upper = is_upper()
     for head in range(heads):
         own, other = own_ref[head], other_ref[head].astype(F32)
         late = jnp.where(upper, own, other)
-        joined = jnp.where(upper, other, own) + mm(early_t_ref[head].astype(BF16), late)
+        first = jnp.where(upper, other, own)
         later_ref[head] = jnp.where(upper, 0.0, other)
-        sends[0][head] = joined.astype(BF16)
-        for flip_ref, send in zip(flipped, sends[1:]):
-            send[head] = rough(flip_ref[head], joined).astype(BF16)
+        sends[0][head] = (first + rough(early_t_ref[head], late)).astype(BF16)
+        for flip_ref, chain_ref, send in zip(flipped, chained, sends[1:]):
+            send[head] = (rough(flip_ref[head], first) + rough(chain_ref[head], late)).astype(BF16)
 
 
 def query_kernel(heads, mask_ref, dout_ref, state_ref, w_ref, score_t_ref, q_ref, k_ref, solve_t_ref,
@@ -648,15 +663,23 @@
         "outputs",
         [],
         arrived + swapped + [prefix, reach, reach_t, local_out, weighted],
-        [states, values, values, states, offsets] + [moves] * (chips - 1),
+        [states, values, values, states, offsets],
         flops=2 * 10**8,
     )
-    state, unit, dout, back, send = results[:5]
+    state, unit, dout, back, send = results
+    chained = call(
+        functools.partial(chain_kernel, heads, chips),
+        "chain",
+        [],
+        arrived + swapped + [early_t],
+        [moves] * (2 * chips - 2),
+        flops=10**7,
+    )
     results = call(
         functools.partial(join_back_kernel, heads, chips),
         "join_back",
         [],
-        [back, core_swap(send, count), early_t] + list(results[5:]),
+        [back, core_swap(send, count), early_t] + list(chained),
         [states] + [offsets] * chips,
         flops=10**7,
     )

time: 57.3 us -> 57 us (level)
    pallas_call x14 -> x15, Pallas kernels: 12.7 us -> 12.6 us  [call(): pl.pallas_call(body, name=name, out_shape=tuple(outs), in_specs=[SMEM] *...]
  transfers between devices with their start and end apart: 14 -> 14, of which waited for: 10 -> 10; matrix products, arithmetic and copies ran while one was open for 6% -> 6% of each run, Pallas kernels for 10% -> 11%
where the time goes in v4:
time: 57 us; the launch traced here: 56.6 us
  starting transfers between devices  19 us (33%)
  waiting for transfers between devices  18.3 us (32%)
  Pallas kernels  12.6 us (22%)
  local copies, waits for them, and re-layouts  5.73 us (10%)
  between operations  0.85 us (1%)
    pallas_call x15, Pallas kernels, call(): pl.pallas_call(body, name=name, out_shape=tuple(outs), in_specs=[SMEM] *...  12.6 us
    all_to_all x1, starting transfers between devices, on_device(): lax.all_to_all(loaded.reshape(count, rows_each, local), 'seq', split_axis...  7.5 us
    all_to_all x1, waiting for transfers between devices, on_device(): lax.all_to_all(loaded.reshape(count, rows_each, local), 'seq', split_axis...  5.43 us
    ppermute x4, waiting for transfers between devices, corner_shift(): return lax.ppermute(x, ('seq', 'head'), pairs)  4.94 us
    unnamed x25, local copies, waits for them, and re-layouts  4.53 us
    ppermute x2, starting transfers between devices, seq_shift(): return lax.ppermute(x, 'seq', [(i, (i + by) % count) for i in range(count)])  4.01 us
    ppermute x3, waiting for transfers between devices, core_swap(): return lax.ppermute(x, 'seq', [(i, i ^ 1) for i in range(count)])  3.55 us
    ppermute x4, starting transfers between devices, corner_shift(): return lax.ppermute(x, ('seq', 'head'), pairs)  3.46 us
  transfers between devices with their start and end apart: 14, of which 10 were waited for; matrix products, arithmetic and copies ran while one was open for 6% of the time, Pallas kernels for 11%

profile of v4, /device:TPU:0, one launch (start us, length us, event | category | flops | bytes accessed | tf_op | source)
XLA Modules:
  0.0 56.6 jit_solution(4717462990670880004)
XLA Ops:
  0.6 7.5 %all-to-all-start = ((bf16[16,8,1024]{2,1,0:T(8,128)(2,1)}), bf16[16,8,1024]{2,1,0:T(8,128)(2,1)S(1)}, u32[]{:S(2)}, u32[]{:S(2)}) async-start(bf16[16,8,1024]{2,1,0:T(8,128)(2,1)} %bitcast.9), calls=%async_computation | async-start | bytes 524288 | tf_op jit(solution)/shard_map/all_to_all | solution.py:570
  8.1 0.0 copy-start
  8.2 1.8 %copy.13 = bf16[2048,2]{1,0:T(8,128)(2,1)} copy(bf16[2048,2]{0,1:T(2,128)(2,1)} %param.16) | data formatting | bytes 16384 | tf_op args[5]
  10.0 1.2 %pad.4.refs_3_.refs_15_ = bf16[2048,128]{1,0:T(8,128)(2,1)S(1)} pad(bf16[2048,2]{1,0:T(8,128)(2,1)} %copy.13, bf16[]{:T(256)} %constant.2.clone.1), padding=0_0x0_126 | pad | bytes 532482 | tf_op jit(solution)/shard_map/jit(_pad)/pad | solution.py:567
  11.2 0.9 %prepare.1 = (bf16[4,128,128]{2,1,0:T(8,128)(2,1)S(1)}, bf16[4,128,8]{2,1,0:T(8,128)(2,1)S(1)}, bf16[8,128]{1,0:T(8,128)(2,1)S(1)}, bf16[2,128,128]{2,1,0:T(8,12...) custom-call(s32[1,16]{1,0:T(1,128)S(1)} %copy-done.8, ...), custom_call_target="tpu_custom_call" | custom-call | bytes 539648 | tf_op jit(solution)/shard_map/prepare/pallas_call | solution.py:508
  12.1 0.0 copy-start.5
  12.1 0.6 %copy-done.5 = bf16[2,128,8]{2,1,0:T(8,128)(2,1)} copy-done((bf16[2,128,8]{2,1,0:T(8,128)(2,1)}, bf16[2,128,8]{2,1,0:T(8,128)(2,1)S(1)}, u32[]{:S(2)}) %copy-start.5) | copy-done | bytes 4120
  12.8 5.4 %all-to-all-done = bf16[16,8,1024]{2,1,0:T(8,128)(2,1)S(1)} async-done(((bf16[16,8,1024]{2,1,0:T(8,128)(2,1)}), bf16[16,8,1024]{2,1,0:T(8,128)(2,1)S(1)}, u32[]{:S(2)}, u32[]{:S(2)}) %all-to-all-start) | async-done | bytes 262176 | tf_op jit(solution)/shard_map/all_to_all | solution.py:570
  18.2 1.5 %collective-permute-start.1 = (bf16[128,1024]{1,0:T(8,128)(2,1)S(1)}, bf16[128,1024]{1,0:T(8,128)(2,1)S(1)}, u32[]{:S(2)}, u32[]{:S(2)}) collective-permute-start(bf16[128,1024]{1,0:T(8,128)(2,1)S(1)} %bitcast.5), channel_id=1, source_target_pairs={{0,1},{1,0},{2,3},{3,2},{4,5},{5,4},{6,7},{7,6},{8,9},{9,8},{10,11... | collective-permute-start | bytes 786440 | tf_op jit(solution)/shard_map/ppermute | solution.py:551
  19.7 0.1 convolution_convert_fusion
  19.9 0.0 collective-permute-start
  19.9 0.0 copy-start.2
  19.9 1.2 %copy-done.2 = bf16[2048,256]{1,0:T(8,128)(2,1)S(1)} copy-done((bf16[2048,256]{1,0:T(8,128)(2,1)S(1)}, bf16[2048,256]{1,0:T(8,128)(2,1)}, u32[]{:S(2)}) %copy-start.2) | copy-done | bytes 1048600
  21.2 1.1 %flip.1 = (bf16[256,2048]{1,0:T(8,128)(2,1)S(1)}, bf16[256,2048]{1,0:T(8,128)(2,1)S(1)}, bf16[256,2048]{1,0:T(8,128)(2,1)S(1)}, bf16[128,2048]{1,0:T(8,128)(2,1)S(1)}) custom-call(bf16[2048,256]{1,0:T(8,128)(2,1)S(1)} %copy-done, bf16[2048,256]{1,0:T(8,128)(2,1)S(1)} %copy-done.1, bf16[2048,256]{1,0:T(8,128)(2,1)S(1)} %copy-done.2, ...), custom_call_target="tpu_custom_call" | custom-call | bytes 7340032 | tf_op jit(solution)/shard_map/flip/pallas_call | solution.py:508
  22.2 0.2 copy-done.3
  22.4 0.6 %project_own.1 = (f32[128,256]{1,0:T(8,128)S(1)}, f32[128,256]{1,0:T(8,128)S(1)}, f32[128,256]{1,0:T(8,128)S(1)}, f32[128,128]{1,0:T(8,128)S(1)}) custom-call(bf16[128,1024]{1,0:T(8,128)(2,1)S(1)} %bitcast.7, bf16[4,128,128]{2,1,0:T(8,128)(2,1)S(1)} %get-tuple-element.109.pick_ref.refs_10_, bf16[4,128,8]{2,1,0:T(8,128)(2,1)S(1)} %get-tuple-element.110.edge_ref.refs_11_, ...), custom_call_target="tpu_custom_call" | custom-call | flops 234881024 | bytes 4530176 | tf_op jit(solution)/shard_map/project_own/pallas_call | solution.py:508
  23.0 2.8 %collective-permute-done.halo_ref = bf16[8,1024]{1,0:T(8,128)(2,1)S(1)} collective-permute-done((bf16[8,1024]{1,0:T(8,128)(2,1)S(1)}, bf16[8,1024]{1,0:T(8,128)(2,1)S(1)}, u32[]{:S(2)}, u32[]{:S(2)}) %collective-permute-start) | collective-permute-done | bytes 16416 | tf_op jit(solution)/shard_map/ppermute | solution.py:547
  25.8 0.4 project_halo.1
  26.3 0.3 collective-permute-done.2.refs_9_
  26.6 2.8 %project.1 = (bf16[2,128,256]{2,1,0:T(8,128)(2,1)S(1)}, f32[2,128,128]{2,1,0:T(8,128)S(1)}, f32[2,128,128]{2,1,0:T(8,128)S(1)}, f32[2,128,128]{2,1,0:T(8,128)S(1...) custom-call(f32[5,128,128]{2,1,0:T(8,128)S(1)} %get-tuple-element.106.mask_ref, ...), custom_call_target="tpu_custom_call" | custom-call | flops 234881024 | bytes 5915648 | tf_op jit(solution)/shard_map/project/pallas_call | solution.py:508
  29.5 0.0 copy-start.4
  29.5 0.1 collective-permute-start.3
  29.5 1.3 %collective-permute-done.3.other_ref = bf16[2,128,256]{2,1,0:T(8,128)(2,1)S(1)} collective-permute-done((bf16[2,128,256]{2,1,0:T(8,128)(2,1)S(1)}, bf16[2,128,256]{2,1,0:T(8,128)(2,1)S(1)}, u32[]{:S(2)}, u32[]{:S(2)}) %collective-permute-start.3) | collective-permute-done | bytes 131104 | tf_op jit(solution)/shard_map/ppermute | solution.py:539
  30.9 0.2 join.1
  31.1 0.3 collective-permute-start.4
  31.4 0.3 collective-permute-start.5
  31.7 0.7 %copy-done.7 = f32[128]{0:T(128)S(1)} copy-done((f32[128]{0:T(128)S(1)}, f32[128]{0:T(128)}, u32[]{:S(2)}) %copy-start.7) | copy-done | bytes 536
  32.3 0.9 %local_terms.1 = (f32[2,128,128]{2,1,0:T(8,128)S(1)}, f32[2,128,128]{2,1,0:T(8,128)S(1)}, f32[2,128,128]{2,1,0:T(8,128)S(1)}, f32[2,128,128]{2,1,0:T(8,128)S(1)}...) custom-call(f32[5,128,128]{2,1,0:T(8,128)S(1)} %get-tuple-element.10, ...), custom_call_target="tpu_custom_call" | custom-call | flops 200000000 | bytes 2622464 | tf_op jit(solution)/shard_map/local_terms/pallas_call | solution.py:508
  33.2 2.5 %collective-permute-done.5.odd_ref.refs_1_ = bf16[2,128,128]{2,1,0:T(8,128)(2,1)S(1)} collective-permute-done((bf16[2,128,128]{2,1,0:T(8,128)(2,1)S(1)}, bf16[2,128,128]{2,1,0:T(8,128)(2,1)S(1)}, u32[]{:S(2)}, u32[]{:S(2)}) %collective-permute-start.5) | collective-permute-done | bytes 65568 | tf_op jit(solution)/shard_map/ppermute | solution.py:531
  35.7 0.1 collective-permute-start.6
  35.8 1.3 %collective-permute-done.6.refs_2_ = bf16[2,128,256]{2,1,0:T(8,128)(2,1)S(1)} collective-permute-done((bf16[2,128,256]{2,1,0:T(8,128)(2,1)S(1)}, bf16[2,128,256]{2,1,0:T(8,128)(2,1)S(1)}, u32[]{:S(2)}, u32[]{:S(2)}) %collective-permute-start.6) | collective-permute-done | bytes 131104 | tf_op jit(solution)/shard_map/ppermute | solution.py:539
  37.2 1.0 %outputs.1 = (f32[2,128,128]{2,1,0:T(8,128)S(1)}, f32[2,128,128]{2,1,0:T(8,128)S(1)}, f32[2,128,128]{2,1,0:T(8,128)S(1)}, f32[2,128,128]{2,1,0:T(8,128)S(1)}, bf16[2,128,128]{2,1,0:T(8,128)(2,1)S(1)}) custom-call(bf16[2,128,256]{2,1,0:T(8,128)(2,1)S(1)} %collective-permute-done.4.even_ref.refs_0_, ...), custom_call_target="tpu_custom_call" | custom-call | flops 200000000 | bytes 1572864 | tf_op jit(solution)/shard_map/outputs/pallas_call | solution.py:508
  38.1 0.2 collective-permute-start.7
  38.4 0.2 chain.1
  38.6 0.9 %collective-permute-done.7.other_ref = bf16[2,128,128]{2,1,0:T(8,128)(2,1)S(1)} collective-permute-done((bf16[2,128,128]{2,1,0:T(8,128)(2,1)S(1)}, bf16[2,128,128]{2,1,0:T(8,128)(2,1)S(1)}, u32[]{:S(2)}, u32[]{:S(2)}) %collective-permute-start.7) | collective-permute-done | bytes 65568 | tf_op jit(solution)/shard_map/ppermute | solution.py:539
  39.5 0.2 join_back.1
  39.7 2.2 %collective-permute-start.8 = (bf16[2,128,128]{2,1,0:T(8,128)(2,1)S(1)}, bf16[2,128,128]{2,1,0:T(8,128)(2,1)S(1)}, u32[]{:S(2)}, u32[]{:S(2)}) collective-permute-start(bf16[2,128,128]{2,1,0:T(8,128)(2,1)S(1)} %get-tuple-element.178), channel_id=1, source_target_pairs={{0,28},{2,30},{4,0},{6,2},{8,4},{10,6},{12,8},{14,10},{16,12},{18,... | collective-permute-start | bytes 196616 | tf_op jit(solution)/shard_map/ppermute | solution.py:535
  41.9 1.8 %collective-permute-start.9 = (bf16[2,128,128]{2,1,0:T(8,128)(2,1)S(1)}, bf16[2,128,128]{2,1,0:T(8,128)(2,1)S(1)}, u32[]{:S(2)}, u32[]{:S(2)}) collective-permute-start(bf16[2,128,128]{2,1,0:T(8,128)(2,1)S(1)} %get-tuple-element.179), channel_id=1, source_target_pairs={{0,24},{2,26},{4,28},{6,30},{8,0},{10,2},{12,4},{14,6},{16,8},{18,... | collective-permute-start | bytes 196616 | tf_op jit(solution)/shard_map/ppermute | solution.py:535
  43.7 1.6 %query_grad.1 = (bf16[128,256]{1,0:T(8,128)(2,1)}, bf16[128,256]{1,0:T(8,128)(2,1)S(1)}, f32[2,128,128]{2,1,0:T(8,128)S(1)}, f32[2,128,128]{2,1,0:T(8,128)S(1)},...) custom-call(f32[5,128,128]{2,1,0:T(8,128)S(1)} %get-tuple-element.106.mask_ref, ...), custom_call_target="tpu_custom_call" | custom-call | flops 200000000 | bytes 2621952 | tf_op jit(solution)/shard_map/query_grad/pallas_call | solution.py:508
  45.3 1.4 %collective-permute-done.9.refs_1_ = bf16[2,128,128]{2,1,0:T(8,128)(2,1)S(1)} collective-permute-done((bf16[2,128,128]{2,1,0:T(8,128)(2,1)S(1)}, bf16[2,128,128]{2,1,0:T(8,128)(2,1)S(1)}, u32[]{:S(2)}, u32[]{:S(2)}) %collective-permute-start.9) | collective-permute-done | bytes 65568 | tf_op jit(solution)/shard_map/ppermute | solution.py:535
  46.8 1.2 %key_grad.1 = (bf16[128,1024]{1,0:T(8,128)(2,1)S(1)}, bf16[8,1024]{1,0:T(8,128)(2,1)S(1)}, bf16[128,896]{1,0:T(8,128)(2,1)S(1)}) custom-call(f32[5,128,128]{2,1,0:T(8,128)S(1)} %get-tuple-element.106.mask_ref, bf16[2,128,128]{2,1,0:T(8,128)(2,1)S(1)} %collective-permute-done.8.refs_0_, bf16[2,128,128]{2,1,0:T(8,128)(2,1)S(1)} %collective-permute-done.9.refs_1_, ...), custom_call_target="tpu_custom_call" | custom-call | flops 200000000 | bytes 5947392 | tf_op jit(solution)/shard_map/key_grad/pallas_call | solution.py:508
  48.0 1.6 %collective-permute-start.10 = (bf16[128,1024]{1,0:T(8,128)(2,1)S(1)}, bf16[128,1024]{1,0:T(8,128)(2,1)S(1)}, u32[]{:S(2)}, u32[]{:S(2)}) collective-permute-start(bf16[128,1024]{1,0:T(8,128)(2,1)S(1)} %get-tuple-element.193), channel_id=1, source_target_pairs={{0,1},{1,0},{2,3},{3,2},{4,5},{5,4},{6,7},{7,6},{8,9},{9,8},{10,11... | collective-permute-start | bytes 786440 | tf_op jit(solution)/shard_map/ppermute | solution.py:551
  49.6 0.4 own_back.1
  50.0 1.6 %collective-permute-start.11 = (bf16[8,1024]{1,0:T(8,128)(2,1)S(1)}, bf16[8,1024]{1,0:T(8,128)(2,1)S(1)}, u32[]{:S(2)}, u32[]{:S(2)}) collective-permute-start(bf16[8,1024]{1,0:T(8,128)(2,1)S(1)} %get-tuple-element.194), channel_id=1, source_target_pairs={{0,30},{1,31},{2,0},{3,1},{4,2},{5,3},{6,4},{7,5},{8,6},{9,7},{10,... | collective-permute-start | bytes 49160 | tf_op jit(solution)/shard_map/ppermute | solution.py:547
  51.6 1.8 %collective-permute-start.12 = (bf16[8,1024]{1,0:T(8,128)(2,1)S(1)}, bf16[8,1024]{1,0:T(8,128)(2,1)S(1)}, u32[]{:S(2)}, u32[]{:S(2)}) collective-permute-start(bf16[8,1024]{1,0:T(8,128)(2,1)S(1)} %get-tuple-element.195), channel_id=1, source_target_pairs={{0,31},{1,30},{2,1},{3,0},{4,3},{5,2},{6,5},{7,4},{8,7},{9,6},{10,... | collective-permute-start | bytes 49160 | tf_op jit(solution)/shard_map/ppermute | solution.py:547
  53.4 1.7 %collective-permute-done.12.refs_2_ = bf16[8,1024]{1,0:T(8,128)(2,1)S(1)} collective-permute-done((bf16[8,1024]{1,0:T(8,128)(2,1)S(1)}, bf16[8,1024]{1,0:T(8,128)(2,1)S(1)}, u32[]{:S(2)}, u32[]{:S(2)}) %collective-permute-start.12) | collective-permute-done | bytes 16416 | tf_op jit(solution)/shard_map/ppermute | solution.py:547
  55.2 0.5 collective-permute-done.10.refs_0_
  55.7 0.9 %finish.1 = bf16[128,1024]{1,0:T(8,128)(2,1)} custom-call(bf16[2,128,128]{2,1,0:T(8,128)(2,1)S(1)} %get-tuple-element.176.pick_ref, bf16[2,128,8]{2,1,0:T(8,128)(2,1)S(1)} %copy-done.6, f32[128,1024]{1,0:T(8,128)S(1)} %get-tuple-element.192.mine_ref, bf16[128,1024]{1,0:T(8,128)(2,1)S(1)} %collective-permute-done.10.refs_0_, ...), custom_call_target="tpu_custom_call" | custom-call | flops 100000000 | bytes 1150976 | tf_op jit(solution)/shard_map/finish/pallas_call | solution.py:508
  (22 shorter events, 0.1 us)
Async XLA Ops:
  0.6 19.3 %copy-start.1 = (bf16[2048,256]{1,0:T(8,128)(2,1)S(1)}, bf16[2048,256]{1,0:T(8,128)(2,1)}, u32[]{:S(2)}) copy-start(bf16[2048,256]{1,0:T(8,128)(2,1)} %refs_13_.1) | copy-start | bytes 3145732
  0.6 17.6 %all-to-all-start = ((bf16[16,8,1024]{2,1,0:T(8,128)(2,1)}), bf16[16,8,1024]{2,1,0:T(8,128)(2,1)S(1)}, u32[]{:S(2)}, u32[]{:S(2)}) async-start(bf16[16,8,1024]{2,1,0:T(8,128)(2,1)} %bitcast.9), calls=%async_computation | async-start | bytes 524288 | tf_op jit(solution)/shard_map/all_to_all | solution.py:570
  8.1 11.8 %copy-start = (bf16[2048,256]{1,0:T(8,128)(2,1)S(1)}, bf16[2048,256]{1,0:T(8,128)(2,1)}, u32[]{:S(2)}) copy-start(bf16[2048,256]{1,0:T(8,128)(2,1)} %refs_12_.1) | copy-start | bytes 3145732
  10.0 1.2 %copy-start.8 = (s32[1,16]{1,0:T(1,128)S(1)}, s32[1,16]{1,0:T(1,128)}, u32[]{:S(2)}) copy-start(s32[1,16]{1,0:T(1,128)} %order_ref.1) | copy-start | bytes 196
  10.0 1.2 %copy-start.9 = (s32[16]{0:T(128)S(1)}, s32[16]{0:T(128)}, u32[]{:S(2)}) copy-start(s32[16]{0:T(128)} %clips_ref.1) | copy-start | bytes 196
  10.0 1.2 %copy-start.10 = (s32[4]{0:T(128)S(1)}, s32[4]{0:T(128)}, u32[]{:S(2)}) copy-start(s32[4]{0:T(128)} %delays_ref.1) | copy-start | bytes 52
  10.0 1.2 %copy-start.11 = (f32[2]{0:T(128)S(1)}, f32[2]{0:T(128)}, u32[]{:S(2)}) copy-start(f32[2]{0:T(128)} %cap_ref.1) | copy-start | bytes 28
  12.1 0.6 %copy-start.5 = (bf16[2,128,8]{2,1,0:T(8,128)(2,1)}, bf16[2,128,8]{2,1,0:T(8,128)(2,1)S(1)}, u32[]{:S(2)}) copy-start(bf16[2,128,8]{2,1,0:T(8,128)(2,1)S(1)} %get-tuple-element.177.edge_ref) | copy-start | bytes 12292
  18.2 8.4 %collective-permute-start.1 = (bf16[128,1024]{1,0:T(8,128)(2,1)S(1)}, bf16[128,1024]{1,0:T(8,128)(2,1)S(1)}, u32[]{:S(2)}, u32[]{:S(2)}) collective-permute-start(bf16[128,1024]{1,0:T(8,128)(2,1)S(1)} %bitcast.5), channel_id=1, source_target_pairs={{0,1},{1,0},{2,3},{3,2},{4,5},{5,4},{6,7},{7,6},{8,9},{9,8},{10,11... | collective-permute-start | bytes 786440 | tf_op jit(solution)/shard_map/ppermute | solution.py:551
  19.9 6.8 %collective-permute-start.2 = (bf16[8,1024]{1,0:T(8,128)(2,1)S(1)}, bf16[8,1024]{1,0:T(8,128)(2,1)S(1)}, u32[]{:S(2)}, u32[]{:S(2)}) collective-permute-start(bf16[8,1024]{1,0:T(8,128)(2,1)S(1)} %convolution_convert_fusion), channel_id=1, source_target_pairs={{0,3},{1,2},{2,5},{3,4},{4,7},{5,6},{6,9},{7,8},{8,11},{9,10},{10,... | collective-permute-start | bytes 49160 | tf_op jit(solution)/shard_map/ppermute | solution.py:547
  19.9 6.0 %collective-permute-start = (bf16[8,1024]{1,0:T(8,128)(2,1)S(1)}, bf16[8,1024]{1,0:T(8,128)(2,1)S(1)}, u32[]{:S(2)}, u32[]{:S(2)}) collective-permute-start(bf16[8,1024]{1,0:T(8,128)(2,1)S(1)} %convolution_convert_fusion), channel_id=1, source_target_pairs={{0,2},{1,3},{2,4},{3,5},{4,6},{5,7},{6,8},{7,9},{8,10},{9,11},{10,... | collective-permute-start | bytes 49160 | tf_op jit(solution)/shard_map/ppermute | solution.py:547
  19.9 1.2 %copy-start.2 = (bf16[2048,256]{1,0:T(8,128)(2,1)S(1)}, bf16[2048,256]{1,0:T(8,128)(2,1)}, u32[]{:S(2)}) copy-start(bf16[2048,256]{1,0:T(8,128)(2,1)} %refs_14_.1) | copy-start | bytes 3145732
  21.2 1.2 %copy-start.3 = (bf16[2048,256]{1,0:T(8,128)(2,1)S(1)}, bf16[2048,256]{1,0:T(8,128)(2,1)}, u32[]{:S(2)}) copy-start(bf16[2048,256]{1,0:T(8,128)(2,1)} %refs_14_.1) | copy-start | bytes 3145732
  29.5 2.2 %copy-start.4 = (bf16[128,256]{1,0:T(8,128)(2,1)S(1)}, bf16[128,256]{1,0:T(8,128)(2,1)}, u32[]{:S(2)}) copy-start(bf16[128,256]{1,0:T(8,128)(2,1)} %grad_ref.1) | copy-start | bytes 196612
  29.5 1.4 %collective-permute-start.3 = (bf16[2,128,256]{2,1,0:T(8,128)(2,1)S(1)}, bf16[2,128,256]{2,1,0:T(8,128)(2,1)S(1)}, u32[]{:S(2)}, u32[]{:S(2)}) collective-permute-start(bf16[2,128,256]{2,1,0:T(8,128)(2,1)S(1)} %get-tuple-element.133.own_ref), channel_id=1, source_target_pairs={{0,2},{2,0},{4,6},{6,4},{8,10},{10,8},{12,14},{14,12},{16,18},{18,... | collective-permute-start | bytes 393224 | tf_op jit(solution)/shard_map/ppermute | solution.py:539
  31.1 4.6 %collective-permute-start.4 = (bf16[2,128,256]{2,1,0:T(8,128)(2,1)S(1)}, bf16[2,128,256]{2,1,0:T(8,128)(2,1)S(1)}, u32[]{:S(2)}, u32[]{:S(2)}) collective-permute-start(bf16[2,128,256]{2,1,0:T(8,128)(2,1)S(1)} %get-tuple-element.134), channel_id=1, source_target_pairs={{0,4},{2,0},{4,8},{6,2},{8,12},{10,6},{12,16},{14,10},{16,20},{18,... | collective-permute-start | bytes 393224 | tf_op jit(solution)/shard_map/ppermute | solution.py:531
  31.4 4.3 %collective-permute-start.5 = (bf16[2,128,128]{2,1,0:T(8,128)(2,1)S(1)}, bf16[2,128,128]{2,1,0:T(8,128)(2,1)S(1)}, u32[]{:S(2)}, u32[]{:S(2)}) collective-permute-start(bf16[2,128,128]{2,1,0:T(8,128)(2,1)S(1)} %get-tuple-element.135), channel_id=1, source_target_pairs={{2,10},{0,2},{6,14},{4,6},{10,18},{8,0},{14,22},{12,4},{18,26},{16... | collective-permute-start | bytes 196616 | tf_op jit(solution)/shard_map/ppermute | solution.py:531
  31.7 0.7 %copy-start.7 = (f32[128]{0:T(128)S(1)}, f32[128]{0:T(128)}, u32[]{:S(2)}) copy-start(f32[128]{0:T(128)} %param.18) | copy-start | bytes 1540
  35.7 1.4 %collective-permute-start.6 = (bf16[2,128,256]{2,1,0:T(8,128)(2,1)S(1)}, bf16[2,128,256]{2,1,0:T(8,128)(2,1)S(1)}, u32[]{:S(2)}, u32[]{:S(2)}) collective-permute-start(bf16[2,128,256]{2,1,0:T(8,128)(2,1)S(1)} %give.1), channel_id=1, source_target_pairs={{0,2},{2,0},{4,6},{6,4},{8,10},{10,8},{12,14},{14,12},{16,18},{18,... | collective-permute-start | bytes 393224 | tf_op jit(solution)/shard_map/ppermute | solution.py:539
  38.1 1.3 %collective-permute-start.7 = (bf16[2,128,128]{2,1,0:T(8,128)(2,1)S(1)}, bf16[2,128,128]{2,1,0:T(8,128)(2,1)S(1)}, u32[]{:S(2)}, u32[]{:S(2)}) collective-permute-start(bf16[2,128,128]{2,1,0:T(8,128)(2,1)S(1)} %get-tuple-element.170), channel_id=1, source_target_pairs={{0,2},{2,0},{4,6},{6,4},{8,10},{10,8},{12,14},{14,12},{16,18},{18,... | collective-permute-start | bytes 196616 | tf_op jit(solution)/shard_map/ppermute | solution.py:539
  39.7 5.7 %collective-permute-start.8 = (bf16[2,128,128]{2,1,0:T(8,128)(2,1)S(1)}, bf16[2,128,128]{2,1,0:T(8,128)(2,1)S(1)}, u32[]{:S(2)}, u32[]{:S(2)}) collective-permute-start(bf16[2,128,128]{2,1,0:T(8,128)(2,1)S(1)} %get-tuple-element.178), channel_id=1, source_target_pairs={{0,28},{2,30},{4,0},{6,2},{8,4},{10,6},{12,8},{14,10},{16,12},{18,... | collective-permute-start | bytes 196616 | tf_op jit(solution)/shard_map/ppermute | solution.py:535
  41.9 4.9 %collective-permute-start.9 = (bf16[2,128,128]{2,1,0:T(8,128)(2,1)S(1)}, bf16[2,128,128]{2,1,0:T(8,128)(2,1)S(1)}, u32[]{:S(2)}, u32[]{:S(2)}) collective-permute-start(bf16[2,128,128]{2,1,0:T(8,128)(2,1)S(1)} %get-tuple-element.179), channel_id=1, source_target_pairs={{0,24},{2,26},{4,28},{6,30},{8,0},{10,2},{12,4},{14,6},{16,8},{18,... | collective-permute-start | bytes 196616 | tf_op jit(solution)/shard_map/ppermute | solution.py:535
  48.0 7.7 %collective-permute-start.10 = (bf16[128,1024]{1,0:T(8,128)(2,1)S(1)}, bf16[128,1024]{1,0:T(8,128)(2,1)S(1)}, u32[]{:S(2)}, u32[]{:S(2)}) collective-permute-start(bf16[128,1024]{1,0:T(8,128)(2,1)S(1)} %get-tuple-element.193), channel_id=1, source_target_pairs={{0,1},{1,0},{2,3},{3,2},{4,5},{5,4},{6,7},{7,6},{8,9},{9,8},{10,11... | collective-permute-start | bytes 786440 | tf_op jit(solution)/shard_map/ppermute | solution.py:551
  49.6 6.1 %copy-start.6 = (bf16[2,128,8]{2,1,0:T(8,128)(2,1)S(1)}, bf16[2,128,8]{2,1,0:T(8,128)(2,1)}, u32[]{:S(2)}) copy-start(bf16[2,128,8]{2,1,0:T(8,128)(2,1)} %copy-done.5) | copy-start | bytes 12292
  50.0 3.4 %collective-permute-start.11 = (bf16[8,1024]{1,0:T(8,128)(2,1)S(1)}, bf16[8,1024]{1,0:T(8,128)(2,1)S(1)}, u32[]{:S(2)}, u32[]{:S(2)}) collective-permute-start(bf16[8,1024]{1,0:T(8,128)(2,1)S(1)} %get-tuple-element.194), channel_id=1, source_target_pairs={{0,30},{1,31},{2,0},{3,1},{4,2},{5,3},{6,4},{7,5},{8,6},{9,7},{10,... | collective-permute-start | bytes 49160 | tf_op jit(solution)/shard_map/ppermute | solution.py:547
  51.6 3.6 %collective-permute-start.12 = (bf16[8,1024]{1,0:T(8,128)(2,1)S(1)}, bf16[8,1024]{1,0:T(8,128)(2,1)S(1)}, u32[]{:S(2)}, u32[]{:S(2)}) collective-permute-start(bf16[8,1024]{1,0:T(8,128)(2,1)S(1)} %get-tuple-element.195), channel_id=1, source_target_pairs={{0,31},{1,30},{2,1},{3,0},{4,3},{5,2},{6,5},{7,4},{8,7},{9,6},{10,... | collective-permute-start | bytes 49160 | tf_op jit(solution)/shard_map/ppermute | solution.py:547

commit v5 on v4

--- a/solution.py
+++ b/solution.py
@@ -360,13 +360,14 @@
             step = rough if index == chips - 2 else mm
             state = earlier[:, dk:] + step(earlier[:, :dk].astype(BF16), state)
             state = jnp.where(seq >= 2 * index + 2, state, 0.0)
-        raw = local_ref[head] + mm(reach_ref[head], state)
+        raw = local_ref[head] + rough(reach_ref[head], state)
         state_ref[head] = prefix_ref[head, :, dk:].astype(F32) + mm(prefix_ref[head, :, :dk], state)
         scale = lax.rsqrt(jnp.mean(raw * raw, axis=1, keepdims=True) + EPSILON)
         unit = raw * scale
         unit_ref[head] = unit
         weighted = weighted_ref[head]
-        dout = scale * (weighted - unit * jnp.mean(unit * weighted, axis=1, keepdims=True))
+        along = scale * jnp.mean(raw * weighted, axis=1, keepdims=True)
+        dout = scale * (weighted - unit * along)
         dout_ref[head] = dout
         back = rough(reach_t_ref[head], dout)
         back_ref[head] = back
@@ -389,7 +390,7 @@
 
 def query_kernel(heads, mask_ref, dout_ref, state_ref, w_ref, score_t_ref, q_ref, k_ref, solve_t_ref,
                  aux_ref, unit_ref, gain_ref, spread_ref, suffix_t_ref, later_ref,
-                 out_ref, gq_ref, u_ref, y_ref, dk_ref, reach_ref):
+                 weight_ref, out_ref, gq_ref, u_ref, y_ref, dk_ref, reach_ref, *sums):
     frames, dk = q_ref.shape[1:]
     lower, carried, final = mask_ref[1], mask_ref[2], mask_ref[3]
     for head in range(heads):
@@ -410,6 +411,10 @@
         scale = aux_ref[:, 4 * head : 4 * head + 1]
         along = jnp.sum(query * dquery, axis=1, keepdims=True)
         gq_ref[:, head * dk : (head + 1) * dk] = (scale * (dquery - query * along)).astype(BF16)
+    local = sums[0].shape[1]
+    for turn, sum_ref in enumerate(sums, 1):
+        first = lax.rem(here()[1] + turn, len(sums) + 1) * local
+        sum_ref[...] = dot(gq_ref[...], weight_ref[:, pl.ds(pl.multiple_of(first, local), local)])
 
 
 def key_kernel(heads, kinds, chips, count, mask_ref, *refs):
@@ -417,7 +422,7 @@
     (suffix_t_ref, reach_ref, gq_ref, u_ref, y_ref, dk0_ref, state_ref, k_ref, v_ref, gram_ref,
      aux_ref), refs = refs[:11], refs[11:]
     seq = here()[0]
-    weights, refs = refs[:4], refs[4:]
+    weights, sums, refs = refs[:4], refs[4 : 3 + kinds], refs[3 + kinds :]
     outs, grads_ref = refs[:-1], refs[-1]
     frames, dk = k_ref.shape[1:]
     strict, carried, final = mask_ref[0], mask_ref[2], mask_ref[3]
@@ -452,20 +457,25 @@
     )
     others, halos = outs[: kinds - 1], outs[kinds - 1 :]
     for turn in range(1, kinds):
-        back_products(grads_ref, weights, turn, kinds, others[turn - 1], halos[turn - 1])
-
-
-def back_products(grads_ref, weights, turn, kinds, sum_ref, halo_ref):
+        back_products(
+            grads_ref, weights, turn, kinds, others[turn - 1], halos[turn - 1], sums[turn - 1]
+        )
+
+
+def back_products(grads_ref, weights, turn, kinds, sum_ref, halo_ref, query_ref=None):
     local = sum_ref.shape[1]
     width = min(512, local)
     for part in range(local // width):
         first = lax.rem(here()[1] + turn, kinds) * local + part * width
         at = pl.ds(pl.multiple_of(first, width), width)
+        span = slice(part * width, (part + 1) * width)
         row, total = 0, 0.0
-        for weight in weights:
-            total = total + dot(grads_ref[:, row : row + weight.shape[0]], weight[:, at])
+        for index, weight in enumerate(weights):
+            if index == 0 and query_ref is not None:
+                total = query_ref[:, span]
+            else:
+                total = total + dot(grads_ref[:, row : row + weight.shape[0]], weight[:, at])
             row += weight.shape[0]
-        span = slice(part * width, (part + 1) * width)
         halo_ref[:, span] = total[:HALO].astype(BF16)
         sum_ref[:, span] = total.astype(sum_ref.dtype)
 
@@ -690,17 +700,18 @@
         "query_grad",
         [],
         [masks, dout, state, solved, score_t, q, k, solve_t, aux, unit, gains, spread, suffix_t,
-         later],
+         later, flipped[0]],
         [shape((frames, heads * dv), BF16), shape((frames, heads * dk), BF16), values, values,
-         square, square],
+         square, square] + [shape((frames, local))] * (kinds - 1),
         flops=2 * 10**8,
     )
-    head_out, gq, fresh, y, dkey, reach = query_terms
+    head_out, gq, fresh, y, dkey, reach = query_terms[:6]
     results = call(
         functools.partial(key_kernel, heads, kinds, chips, count),
         "key_grad",
         [],
-        [masks] + arrived + [suffix_t, reach, gq, fresh, y, dkey, state, k, v, gram, aux] + list(flipped),
+        [masks] + arrived + [suffix_t, reach, gq, fresh, y, dkey, state, k, v, gram, aux] + list(flipped)
+        + list(query_terms[6:]),
         [shape((frames, local), BF16)] * (kinds - 1)
         + [shape((HALO, local), BF16)] * (kinds - 1)
         + [shape((frames, columns), BF16)],

time: 57 us -> 56.8 us (level)
  no operation moved by 1% of the time
where the time goes in v5:
time: 56.8 us; the launch traced here: 56.5 us
  starting transfers between devices  19 us (33%)
  waiting for transfers between devices  18.1 us (32%)
  Pallas kernels  12.7 us (22%)
  local copies, waits for them, and re-layouts  5.73 us (10%)
  between operations  0.85 us (1%)
    pallas_call x15, Pallas kernels, call(): pl.pallas_call(body, name=name, out_shape=tuple(outs), in_specs=[SMEM] *...  12.7 us
    all_to_all x1, starting transfers between devices, on_device(): lax.all_to_all(loaded.reshape(count, rows_each, local), 'seq', split_axis...  7.5 us
    all_to_all x1, waiting for transfers between devices, on_device(): lax.all_to_all(loaded.reshape(count, rows_each, local), 'seq', split_axis...  5.43 us
    ppermute x4, waiting for transfers between devices, corner_shift(): return lax.ppermute(x, ('seq', 'head'), pairs)  4.94 us
    unnamed x25, local copies, waits for them, and re-layouts  4.53 us
    ppermute x2, starting transfers between devices, seq_shift(): return lax.ppermute(x, 'seq', [(i, (i + by) % count) for i in range(count)])  4.01 us
    ppermute x3, waiting for transfers between devices, core_swap(): return lax.ppermute(x, 'seq', [(i, i ^ 1) for i in range(count)])  3.55 us
    ppermute x4, starting transfers between devices, corner_shift(): return lax.ppermute(x, ('seq', 'head'), pairs)  3.43 us
  transfers between devices with their start and end apart: 14, of which 10 were waited for; matrix products, arithmetic and copies ran while one was open for 6% of the time, Pallas kernels for 11%

profile of v5, /device:TPU:0, one launch (start us, length us, event | category | flops | bytes accessed | tf_op | source)
XLA Modules:
  0.0 56.5 jit_solution(15137809484396687242)
XLA Ops:
  0.6 7.5 %all-to-all-start = ((bf16[16,8,1024]{2,1,0:T(8,128)(2,1)}), bf16[16,8,1024]{2,1,0:T(8,128)(2,1)S(1)}, u32[]{:S(2)}, u32[]{:S(2)}) async-start(bf16[16,8,1024]{2,1,0:T(8,128)(2,1)} %bitcast.9), calls=%async_computation | async-start | bytes 524288 | tf_op jit(solution)/shard_map/all_to_all | solution.py:580
  8.1 0.0 copy-start
  8.2 1.8 %copy.13 = bf16[2048,2]{1,0:T(8,128)(2,1)} copy(bf16[2048,2]{0,1:T(2,128)(2,1)} %param.16) | data formatting | bytes 16384 | tf_op args[5]
  10.0 1.2 %pad.4.refs_3_.refs_15_ = bf16[2048,128]{1,0:T(8,128)(2,1)S(1)} pad(bf16[2048,2]{1,0:T(8,128)(2,1)} %copy.13, bf16[]{:T(256)} %constant.2.clone.1), padding=0_0x0_126 | pad | bytes 532482 | tf_op jit(solution)/shard_map/jit(_pad)/pad | solution.py:577
  11.2 0.9 %prepare.1 = (bf16[4,128,128]{2,1,0:T(8,128)(2,1)S(1)}, bf16[4,128,8]{2,1,0:T(8,128)(2,1)S(1)}, bf16[8,128]{1,0:T(8,128)(2,1)S(1)}, bf16[2,128,128]{2,1,0:T(8,12...) custom-call(s32[1,16]{1,0:T(1,128)S(1)} %copy-done.8, ...), custom_call_target="tpu_custom_call" | custom-call | bytes 539648 | tf_op jit(solution)/shard_map/prepare/pallas_call | solution.py:518
  12.1 0.0 copy-start.5
  12.1 0.6 %copy-done.5 = bf16[2,128,8]{2,1,0:T(8,128)(2,1)} copy-done((bf16[2,128,8]{2,1,0:T(8,128)(2,1)}, bf16[2,128,8]{2,1,0:T(8,128)(2,1)S(1)}, u32[]{:S(2)}) %copy-start.5) | copy-done | bytes 4120
  12.8 5.4 %all-to-all-done = bf16[16,8,1024]{2,1,0:T(8,128)(2,1)S(1)} async-done(((bf16[16,8,1024]{2,1,0:T(8,128)(2,1)}), bf16[16,8,1024]{2,1,0:T(8,128)(2,1)S(1)}, u32[]{:S(2)}, u32[]{:S(2)}) %all-to-all-start) | async-done | bytes 262176 | tf_op jit(solution)/shard_map/all_to_all | solution.py:580
  18.2 1.5 %collective-permute-start.1 = (bf16[128,1024]{1,0:T(8,128)(2,1)S(1)}, bf16[128,1024]{1,0:T(8,128)(2,1)S(1)}, u32[]{:S(2)}, u32[]{:S(2)}) collective-permute-start(bf16[128,1024]{1,0:T(8,128)(2,1)S(1)} %bitcast.5), channel_id=1, source_target_pairs={{0,1},{1,0},{2,3},{3,2},{4,5},{5,4},{6,7},{7,6},{8,9},{9,8},{10,11... | collective-permute-start | bytes 786440 | tf_op jit(solution)/shard_map/ppermute | solution.py:561
  19.7 0.1 convolution_convert_fusion
  19.9 0.0 collective-permute-start
  19.9 0.0 copy-start.2
  19.9 1.2 %copy-done.2 = bf16[2048,256]{1,0:T(8,128)(2,1)S(1)} copy-done((bf16[2048,256]{1,0:T(8,128)(2,1)S(1)}, bf16[2048,256]{1,0:T(8,128)(2,1)}, u32[]{:S(2)}) %copy-start.2) | copy-done | bytes 1048600
  21.2 1.1 %flip.1 = (bf16[256,2048]{1,0:T(8,128)(2,1)S(1)}, bf16[256,2048]{1,0:T(8,128)(2,1)S(1)}, bf16[256,2048]{1,0:T(8,128)(2,1)S(1)}, bf16[128,2048]{1,0:T(8,128)(2,1)S(1)}) custom-call(bf16[2048,256]{1,0:T(8,128)(2,1)S(1)} %copy-done, bf16[2048,256]{1,0:T(8,128)(2,1)S(1)} %copy-done.1, bf16[2048,256]{1,0:T(8,128)(2,1)S(1)} %copy-done.2, ...), custom_call_target="tpu_custom_call" | custom-call | bytes 7340032 | tf_op jit(solution)/shard_map/flip/pallas_call | solution.py:518
  22.2 0.2 copy-done.3
  22.4 0.6 %project_own.1 = (f32[128,256]{1,0:T(8,128)S(1)}, f32[128,256]{1,0:T(8,128)S(1)}, f32[128,256]{1,0:T(8,128)S(1)}, f32[128,128]{1,0:T(8,128)S(1)}) custom-call(bf16[128,1024]{1,0:T(8,128)(2,1)S(1)} %bitcast.7, bf16[4,128,128]{2,1,0:T(8,128)(2,1)S(1)} %get-tuple-element.110.pick_ref.refs_10_, bf16[4,128,8]{2,1,0:T(8,128)(2,1)S(1)} %get-tuple-element.111.edge_ref.refs_11_, ...), custom_call_target="tpu_custom_call" | custom-call | flops 234881024 | bytes 4530176 | tf_op jit(solution)/shard_map/project_own/pallas_call | solution.py:518
  23.0 2.8 %collective-permute-done.halo_ref = bf16[8,1024]{1,0:T(8,128)(2,1)S(1)} collective-permute-done((bf16[8,1024]{1,0:T(8,128)(2,1)S(1)}, bf16[8,1024]{1,0:T(8,128)(2,1)S(1)}, u32[]{:S(2)}, u32[]{:S(2)}) %collective-permute-start) | collective-permute-done | bytes 16416 | tf_op jit(solution)/shard_map/ppermute | solution.py:557
  25.8 0.4 project_halo.1
  26.3 0.3 collective-permute-done.2.refs_9_
  26.6 2.8 %project.1 = (bf16[2,128,256]{2,1,0:T(8,128)(2,1)S(1)}, f32[2,128,128]{2,1,0:T(8,128)S(1)}, f32[2,128,128]{2,1,0:T(8,128)S(1)}, f32[2,128,128]{2,1,0:T(8,128)S(1...) custom-call(f32[5,128,128]{2,1,0:T(8,128)S(1)} %get-tuple-element.107.mask_ref, ...), custom_call_target="tpu_custom_call" | custom-call | flops 234881024 | bytes 5915648 | tf_op jit(solution)/shard_map/project/pallas_call | solution.py:518
  29.5 0.0 copy-start.4
  29.5 0.1 collective-permute-start.3
  29.5 1.3 %collective-permute-done.3.other_ref = bf16[2,128,256]{2,1,0:T(8,128)(2,1)S(1)} collective-permute-done((bf16[2,128,256]{2,1,0:T(8,128)(2,1)S(1)}, bf16[2,128,256]{2,1,0:T(8,128)(2,1)S(1)}, u32[]{:S(2)}, u32[]{:S(2)}) %collective-permute-start.3) | collective-permute-done | bytes 131104 | tf_op jit(solution)/shard_map/ppermute | solution.py:549
  30.9 0.2 join.1
  31.1 0.3 collective-permute-start.4
  31.4 0.3 collective-permute-start.5
  31.7 0.7 %copy-done.7 = f32[128]{0:T(128)S(1)} copy-done((f32[128]{0:T(128)S(1)}, f32[128]{0:T(128)}, u32[]{:S(2)}) %copy-start.7) | copy-done | bytes 536
  32.3 0.9 %local_terms.1 = (f32[2,128,128]{2,1,0:T(8,128)S(1)}, f32[2,128,128]{2,1,0:T(8,128)S(1)}, f32[2,128,128]{2,1,0:T(8,128)S(1)}, f32[2,128,128]{2,1,0:T(8,128)S(1)}...) custom-call(f32[5,128,128]{2,1,0:T(8,128)S(1)} %get-tuple-element.10, ...), custom_call_target="tpu_custom_call" | custom-call | flops 200000000 | bytes 2622464 | tf_op jit(solution)/shard_map/local_terms/pallas_call | solution.py:518
  33.2 2.5 %collective-permute-done.5.odd_ref.refs_1_ = bf16[2,128,128]{2,1,0:T(8,128)(2,1)S(1)} collective-permute-done((bf16[2,128,128]{2,1,0:T(8,128)(2,1)S(1)}, bf16[2,128,128]{2,1,0:T(8,128)(2,1)S(1)}, u32[]{:S(2)}, u32[]{:S(2)}) %collective-permute-start.5) | collective-permute-done | bytes 65568 | tf_op jit(solution)/shard_map/ppermute | solution.py:541
  35.7 0.1 collective-permute-start.6
  35.8 1.3 %collective-permute-done.6.refs_2_ = bf16[2,128,256]{2,1,0:T(8,128)(2,1)S(1)} collective-permute-done((bf16[2,128,256]{2,1,0:T(8,128)(2,1)S(1)}, bf16[2,128,256]{2,1,0:T(8,128)(2,1)S(1)}, u32[]{:S(2)}, u32[]{:S(2)}) %collective-permute-start.6) | collective-permute-done | bytes 131104 | tf_op jit(solution)/shard_map/ppermute | solution.py:549
  37.2 0.9 %outputs.1 = (f32[2,128,128]{2,1,0:T(8,128)S(1)}, f32[2,128,128]{2,1,0:T(8,128)S(1)}, f32[2,128,128]{2,1,0:T(8,128)S(1)}, f32[2,128,128]{2,1,0:T(8,128)S(1)}, bf16[2,128,128]{2,1,0:T(8,128)(2,1)S(1)}) custom-call(bf16[2,128,256]{2,1,0:T(8,128)(2,1)S(1)} %collective-permute-done.4.even_ref.refs_0_, ...), custom_call_target="tpu_custom_call" | custom-call | flops 200000000 | bytes 1572864 | tf_op jit(solution)/shard_map/outputs/pallas_call | solution.py:518
  38.1 0.2 collective-permute-start.7
  38.3 0.2 chain.1
  38.5 0.9 %collective-permute-done.7.other_ref = bf16[2,128,128]{2,1,0:T(8,128)(2,1)S(1)} collective-permute-done((bf16[2,128,128]{2,1,0:T(8,128)(2,1)S(1)}, bf16[2,128,128]{2,1,0:T(8,128)(2,1)S(1)}, u32[]{:S(2)}, u32[]{:S(2)}) %collective-permute-start.7) | collective-permute-done | bytes 65568 | tf_op jit(solution)/shard_map/ppermute | solution.py:549
  39.4 0.2 join_back.1
  39.6 2.2 %collective-permute-start.8 = (bf16[2,128,128]{2,1,0:T(8,128)(2,1)S(1)}, bf16[2,128,128]{2,1,0:T(8,128)(2,1)S(1)}, u32[]{:S(2)}, u32[]{:S(2)}) collective-permute-start(bf16[2,128,128]{2,1,0:T(8,128)(2,1)S(1)} %get-tuple-element.180), channel_id=1, source_target_pairs={{0,28},{2,30},{4,0},{6,2},{8,4},{10,6},{12,8},{14,10},{16,12},{18,... | collective-permute-start | bytes 196616 | tf_op jit(solution)/shard_map/ppermute | solution.py:545
  41.8 1.8 %collective-permute-start.9 = (bf16[2,128,128]{2,1,0:T(8,128)(2,1)S(1)}, bf16[2,128,128]{2,1,0:T(8,128)(2,1)S(1)}, u32[]{:S(2)}, u32[]{:S(2)}) collective-permute-start(bf16[2,128,128]{2,1,0:T(8,128)(2,1)S(1)} %get-tuple-element.181), channel_id=1, source_target_pairs={{0,24},{2,26},{4,28},{6,30},{8,0},{10,2},{12,4},{14,6},{16,8},{18,... | collective-permute-start | bytes 196616 | tf_op jit(solution)/shard_map/ppermute | solution.py:545
  43.6 1.9 %query_grad.1 = (bf16[128,256]{1,0:T(8,128)(2,1)}, bf16[128,256]{1,0:T(8,128)(2,1)S(1)}, f32[2,128,128]{2,1,0:T(8,128)S(1)}, f32[2,128,128]{2,1,0:T(8,128)S(1)},...) custom-call(f32[5,128,128]{2,1,0:T(8,128)S(1)} %get-tuple-element.107.mask_ref, ...), custom_call_target="tpu_custom_call" | custom-call | flops 200000000 | bytes 4194816 | tf_op jit(solution)/shard_map/query_grad/pallas_call | solution.py:518
  45.5 1.2 %collective-permute-done.9.refs_1_ = bf16[2,128,128]{2,1,0:T(8,128)(2,1)S(1)} collective-permute-done((bf16[2,128,128]{2,1,0:T(8,128)(2,1)S(1)}, bf16[2,128,128]{2,1,0:T(8,128)(2,1)S(1)}, u32[]{:S(2)}, u32[]{:S(2)}) %collective-permute-start.9) | collective-permute-done | bytes 65568 | tf_op jit(solution)/shard_map/ppermute | solution.py:545
  46.7 1.2 %key_grad.1 = (bf16[128,1024]{1,0:T(8,128)(2,1)S(1)}, bf16[8,1024]{1,0:T(8,128)(2,1)S(1)}, bf16[128,896]{1,0:T(8,128)(2,1)S(1)}) custom-call(f32[5,128,128]{2,1,0:T(8,128)S(1)} %get-tuple-element.107.mask_ref, bf16[2,128,128]{2,1,0:T(8,128)(2,1)S(1)} %collective-permute-done.8.refs_0_, bf16[2,128,128]{2,1,0:T(8,128)(2,1)S(1)} %collective-permute-done.9.refs_1_, ...), custom_call_target="tpu_custom_call" | custom-call | flops 200000000 | bytes 6471680 | tf_op jit(solution)/shard_map/key_grad/pallas_call | solution.py:518
  47.9 1.6 %collective-permute-start.10 = (bf16[128,1024]{1,0:T(8,128)(2,1)S(1)}, bf16[128,1024]{1,0:T(8,128)(2,1)S(1)}, u32[]{:S(2)}, u32[]{:S(2)}) collective-permute-start(bf16[128,1024]{1,0:T(8,128)(2,1)S(1)} %get-tuple-element.195), channel_id=1, source_target_pairs={{0,1},{1,0},{2,3},{3,2},{4,5},{5,4},{6,7},{7,6},{8,9},{9,8},{10,11... | collective-permute-start | bytes 786440 | tf_op jit(solution)/shard_map/ppermute | solution.py:561
  49.4 0.5 own_back.1
  49.9 1.6 %collective-permute-start.11 = (bf16[8,1024]{1,0:T(8,128)(2,1)S(1)}, bf16[8,1024]{1,0:T(8,128)(2,1)S(1)}, u32[]{:S(2)}, u32[]{:S(2)}) collective-permute-start(bf16[8,1024]{1,0:T(8,128)(2,1)S(1)} %get-tuple-element.196), channel_id=1, source_target_pairs={{0,30},{1,31},{2,0},{3,1},{4,2},{5,3},{6,4},{7,5},{8,6},{9,7},{10,... | collective-permute-start | bytes 49160 | tf_op jit(solution)/shard_map/ppermute | solution.py:557
  51.5 1.8 %collective-permute-start.12 = (bf16[8,1024]{1,0:T(8,128)(2,1)S(1)}, bf16[8,1024]{1,0:T(8,128)(2,1)S(1)}, u32[]{:S(2)}, u32[]{:S(2)}) collective-permute-start(bf16[8,1024]{1,0:T(8,128)(2,1)S(1)} %get-tuple-element.197), channel_id=1, source_target_pairs={{0,31},{1,30},{2,1},{3,0},{4,3},{5,2},{6,5},{7,4},{8,7},{9,6},{10,... | collective-permute-start | bytes 49160 | tf_op jit(solution)/shard_map/ppermute | solution.py:557
  53.3 1.7 %collective-permute-done.12.refs_2_ = bf16[8,1024]{1,0:T(8,128)(2,1)S(1)} collective-permute-done((bf16[8,1024]{1,0:T(8,128)(2,1)S(1)}, bf16[8,1024]{1,0:T(8,128)(2,1)S(1)}, u32[]{:S(2)}, u32[]{:S(2)}) %collective-permute-start.12) | collective-permute-done | bytes 16416 | tf_op jit(solution)/shard_map/ppermute | solution.py:557
  55.0 0.5 collective-permute-done.10.refs_0_
  55.5 1.0 %finish.1 = bf16[128,1024]{1,0:T(8,128)(2,1)} custom-call(bf16[2,128,128]{2,1,0:T(8,128)(2,1)S(1)} %get-tuple-element.178.pick_ref, bf16[2,128,8]{2,1,0:T(8,128)(2,1)S(1)} %copy-done.6, f32[128,1024]{1,0:T(8,128)S(1)} %get-tuple-element.194.mine_ref, bf16[128,1024]{1,0:T(8,128)(2,1)S(1)} %collective-permute-done.10.refs_0_, ...), custom_call_target="tpu_custom_call" | custom-call | flops 100000000 | bytes 1150976 | tf_op jit(solution)/shard_map/finish/pallas_call | solution.py:518
  (22 shorter events, 0.1 us)
Async XLA Ops:
  0.6 19.3 %copy-start.1 = (bf16[2048,256]{1,0:T(8,128)(2,1)S(1)}, bf16[2048,256]{1,0:T(8,128)(2,1)}, u32[]{:S(2)}) copy-start(bf16[2048,256]{1,0:T(8,128)(2,1)} %refs_13_.1) | copy-start | bytes 3145732
  0.6 17.6 %all-to-all-start = ((bf16[16,8,1024]{2,1,0:T(8,128)(2,1)}), bf16[16,8,1024]{2,1,0:T(8,128)(2,1)S(1)}, u32[]{:S(2)}, u32[]{:S(2)}) async-start(bf16[16,8,1024]{2,1,0:T(8,128)(2,1)} %bitcast.9), calls=%async_computation | async-start | bytes 524288 | tf_op jit(solution)/shard_map/all_to_all | solution.py:580
  8.1 11.8 %copy-start = (bf16[2048,256]{1,0:T(8,128)(2,1)S(1)}, bf16[2048,256]{1,0:T(8,128)(2,1)}, u32[]{:S(2)}) copy-start(bf16[2048,256]{1,0:T(8,128)(2,1)} %refs_12_.1) | copy-start | bytes 3145732
  10.0 1.2 %copy-start.8 = (s32[1,16]{1,0:T(1,128)S(1)}, s32[1,16]{1,0:T(1,128)}, u32[]{:S(2)}) copy-start(s32[1,16]{1,0:T(1,128)} %order_ref.1) | copy-start | bytes 196
  10.0 1.2 %copy-start.9 = (s32[16]{0:T(128)S(1)}, s32[16]{0:T(128)}, u32[]{:S(2)}) copy-start(s32[16]{0:T(128)} %clips_ref.1) | copy-start | bytes 196
  10.0 1.2 %copy-start.10 = (s32[4]{0:T(128)S(1)}, s32[4]{0:T(128)}, u32[]{:S(2)}) copy-start(s32[4]{0:T(128)} %delays_ref.1) | copy-start | bytes 52
  10.0 1.2 %copy-start.11 = (f32[2]{0:T(128)S(1)}, f32[2]{0:T(128)}, u32[]{:S(2)}) copy-start(f32[2]{0:T(128)} %cap_ref.1) | copy-start | bytes 28
  12.1 0.6 %copy-start.5 = (bf16[2,128,8]{2,1,0:T(8,128)(2,1)}, bf16[2,128,8]{2,1,0:T(8,128)(2,1)S(1)}, u32[]{:S(2)}) copy-start(bf16[2,128,8]{2,1,0:T(8,128)(2,1)S(1)} %get-tuple-element.179.edge_ref) | copy-start | bytes 12292
  18.2 8.4 %collective-permute-start.1 = (bf16[128,1024]{1,0:T(8,128)(2,1)S(1)}, bf16[128,1024]{1,0:T(8,128)(2,1)S(1)}, u32[]{:S(2)}, u32[]{:S(2)}) collective-permute-start(bf16[128,1024]{1,0:T(8,128)(2,1)S(1)} %bitcast.5), channel_id=1, source_target_pairs={{0,1},{1,0},{2,3},{3,2},{4,5},{5,4},{6,7},{7,6},{8,9},{9,8},{10,11... | collective-permute-start | bytes 786440 | tf_op jit(solution)/shard_map/ppermute | solution.py:561
  19.9 6.8 %collective-permute-start.2 = (bf16[8,1024]{1,0:T(8,128)(2,1)S(1)}, bf16[8,1024]{1,0:T(8,128)(2,1)S(1)}, u32[]{:S(2)}, u32[]{:S(2)}) collective-permute-start(bf16[8,1024]{1,0:T(8,128)(2,1)S(1)} %convolution_convert_fusion), channel_id=1, source_target_pairs={{0,3},{1,2},{2,5},{3,4},{4,7},{5,6},{6,9},{7,8},{8,11},{9,10},{10,... | collective-permute-start | bytes 49160 | tf_op jit(solution)/shard_map/ppermute | solution.py:557
  19.9 6.0 %collective-permute-start = (bf16[8,1024]{1,0:T(8,128)(2,1)S(1)}, bf16[8,1024]{1,0:T(8,128)(2,1)S(1)}, u32[]{:S(2)}, u32[]{:S(2)}) collective-permute-start(bf16[8,1024]{1,0:T(8,128)(2,1)S(1)} %convolution_convert_fusion), channel_id=1, source_target_pairs={{0,2},{1,3},{2,4},{3,5},{4,6},{5,7},{6,8},{7,9},{8,10},{9,11},{10,... | collective-permute-start | bytes 49160 | tf_op jit(solution)/shard_map/ppermute | solution.py:557
  19.9 1.2 %copy-start.2 = (bf16[2048,256]{1,0:T(8,128)(2,1)S(1)}, bf16[2048,256]{1,0:T(8,128)(2,1)}, u32[]{:S(2)}) copy-start(bf16[2048,256]{1,0:T(8,128)(2,1)} %refs_14_.1) | copy-start | bytes 3145732
  21.2 1.2 %copy-start.3 = (bf16[2048,256]{1,0:T(8,128)(2,1)S(1)}, bf16[2048,256]{1,0:T(8,128)(2,1)}, u32[]{:S(2)}) copy-start(bf16[2048,256]{1,0:T(8,128)(2,1)} %refs_14_.1) | copy-start | bytes 3145732
  29.5 2.2 %copy-start.4 = (bf16[128,256]{1,0:T(8,128)(2,1)S(1)}, bf16[128,256]{1,0:T(8,128)(2,1)}, u32[]{:S(2)}) copy-start(bf16[128,256]{1,0:T(8,128)(2,1)} %grad_ref.1) | copy-start | bytes 196612
  29.5 1.4 %collective-permute-start.3 = (bf16[2,128,256]{2,1,0:T(8,128)(2,1)S(1)}, bf16[2,128,256]{2,1,0:T(8,128)(2,1)S(1)}, u32[]{:S(2)}, u32[]{:S(2)}) collective-permute-start(bf16[2,128,256]{2,1,0:T(8,128)(2,1)S(1)} %get-tuple-element.134.own_ref), channel_id=1, source_target_pairs={{0,2},{2,0},{4,6},{6,4},{8,10},{10,8},{12,14},{14,12},{16,18},{18,... | collective-permute-start | bytes 393224 | tf_op jit(solution)/shard_map/ppermute | solution.py:549
  31.1 4.6 %collective-permute-start.4 = (bf16[2,128,256]{2,1,0:T(8,128)(2,1)S(1)}, bf16[2,128,256]{2,1,0:T(8,128)(2,1)S(1)}, u32[]{:S(2)}, u32[]{:S(2)}) collective-permute-start(bf16[2,128,256]{2,1,0:T(8,128)(2,1)S(1)} %get-tuple-element.135), channel_id=1, source_target_pairs={{0,4},{2,0},{4,8},{6,2},{8,12},{10,6},{12,16},{14,10},{16,20},{18,... | collective-permute-start | bytes 393224 | tf_op jit(solution)/shard_map/ppermute | solution.py:541
  31.4 4.3 %collective-permute-start.5 = (bf16[2,128,128]{2,1,0:T(8,128)(2,1)S(1)}, bf16[2,128,128]{2,1,0:T(8,128)(2,1)S(1)}, u32[]{:S(2)}, u32[]{:S(2)}) collective-permute-start(bf16[2,128,128]{2,1,0:T(8,128)(2,1)S(1)} %get-tuple-element.136), channel_id=1, source_target_pairs={{2,10},{0,2},{6,14},{4,6},{10,18},{8,0},{14,22},{12,4},{18,26},{16... | collective-permute-start | bytes 196616 | tf_op jit(solution)/shard_map/ppermute | solution.py:541
  31.7 0.7 %copy-start.7 = (f32[128]{0:T(128)S(1)}, f32[128]{0:T(128)}, u32[]{:S(2)}) copy-start(f32[128]{0:T(128)} %param.18) | copy-start | bytes 1540
  35.7 1.4 %collective-permute-start.6 = (bf16[2,128,256]{2,1,0:T(8,128)(2,1)S(1)}, bf16[2,128,256]{2,1,0:T(8,128)(2,1)S(1)}, u32[]{:S(2)}, u32[]{:S(2)}) collective-permute-start(bf16[2,128,256]{2,1,0:T(8,128)(2,1)S(1)} %give.1), channel_id=1, source_target_pairs={{0,2},{2,0},{4,6},{6,4},{8,10},{10,8},{12,14},{14,12},{16,18},{18,... | collective-permute-start | bytes 393224 | tf_op jit(solution)/shard_map/ppermute | solution.py:549
  38.1 1.3 %collective-permute-start.7 = (bf16[2,128,128]{2,1,0:T(8,128)(2,1)S(1)}, bf16[2,128,128]{2,1,0:T(8,128)(2,1)S(1)}, u32[]{:S(2)}, u32[]{:S(2)}) collective-permute-start(bf16[2,128,128]{2,1,0:T(8,128)(2,1)S(1)} %get-tuple-element.171), channel_id=1, source_target_pairs={{0,2},{2,0},{4,6},{6,4},{8,10},{10,8},{12,14},{14,12},{16,18},{18,... | collective-permute-start | bytes 196616 | tf_op jit(solution)/shard_map/ppermute | solution.py:549
  39.6 5.9 %collective-permute-start.8 = (bf16[2,128,128]{2,1,0:T(8,128)(2,1)S(1)}, bf16[2,128,128]{2,1,0:T(8,128)(2,1)S(1)}, u32[]{:S(2)}, u32[]{:S(2)}) collective-permute-start(bf16[2,128,128]{2,1,0:T(8,128)(2,1)S(1)} %get-tuple-element.180), channel_id=1, source_target_pairs={{0,28},{2,30},{4,0},{6,2},{8,4},{10,6},{12,8},{14,10},{16,12},{18,... | collective-permute-start | bytes 196616 | tf_op jit(solution)/shard_map/ppermute | solution.py:545
  41.8 4.9 %collective-permute-start.9 = (bf16[2,128,128]{2,1,0:T(8,128)(2,1)S(1)}, bf16[2,128,128]{2,1,0:T(8,128)(2,1)S(1)}, u32[]{:S(2)}, u32[]{:S(2)}) collective-permute-start(bf16[2,128,128]{2,1,0:T(8,128)(2,1)S(1)} %get-tuple-element.181), channel_id=1, source_target_pairs={{0,24},{2,26},{4,28},{6,30},{8,0},{10,2},{12,4},{14,6},{16,8},{18,... | collective-permute-start | bytes 196616 | tf_op jit(solution)/shard_map/ppermute | solution.py:545
  47.9 7.7 %collective-permute-start.10 = (bf16[128,1024]{1,0:T(8,128)(2,1)S(1)}, bf16[128,1024]{1,0:T(8,128)(2,1)S(1)}, u32[]{:S(2)}, u32[]{:S(2)}) collective-permute-start(bf16[128,1024]{1,0:T(8,128)(2,1)S(1)} %get-tuple-element.195), channel_id=1, source_target_pairs={{0,1},{1,0},{2,3},{3,2},{4,5},{5,4},{6,7},{7,6},{8,9},{9,8},{10,11... | collective-permute-start | bytes 786440 | tf_op jit(solution)/shard_map/ppermute | solution.py:561
  49.4 6.1 %copy-start.6 = (bf16[2,128,8]{2,1,0:T(8,128)(2,1)S(1)}, bf16[2,128,8]{2,1,0:T(8,128)(2,1)}, u32[]{:S(2)}) copy-start(bf16[2,128,8]{2,1,0:T(8,128)(2,1)} %copy-done.5) | copy-start | bytes 12292
  49.9 3.4 %collective-permute-start.11 = (bf16[8,1024]{1,0:T(8,128)(2,1)S(1)}, bf16[8,1024]{1,0:T(8,128)(2,1)S(1)}, u32[]{:S(2)}, u32[]{:S(2)}) collective-permute-start(bf16[8,1024]{1,0:T(8,128)(2,1)S(1)} %get-tuple-element.196), channel_id=1, source_target_pairs={{0,30},{1,31},{2,0},{3,1},{4,2},{5,3},{6,4},{7,5},{8,6},{9,7},{10,... | collective-permute-start | bytes 49160 | tf_op jit(solution)/shard_map/ppermute | solution.py:557
  51.5 3.6 %collective-permute-start.12 = (bf16[8,1024]{1,0:T(8,128)(2,1)S(1)}, bf16[8,1024]{1,0:T(8,128)(2,1)S(1)}, u32[]{:S(2)}, u32[]{:S(2)}) collective-permute-start(bf16[8,1024]{1,0:T(8,128)(2,1)S(1)} %get-tuple-element.197), channel_id=1, source_target_pairs={{0,31},{1,30},{2,1},{3,0},{4,3},{5,2},{6,5},{7,4},{8,7},{9,6},{10,... | collective-permute-start | bytes 49160 | tf_op jit(solution)/shard_map/ppermute | solution.py:557

commit v6 on v5

--- a/solution.py
+++ b/solution.py
@@ -361,13 +361,12 @@
             state = earlier[:, dk:] + step(earlier[:, :dk].astype(BF16), state)
             state = jnp.where(seq >= 2 * index + 2, state, 0.0)
         raw = local_ref[head] + rough(reach_ref[head], state)
-        state_ref[head] = prefix_ref[head, :, dk:].astype(F32) + mm(prefix_ref[head, :, :dk], state)
+        state_ref[head] = prefix_ref[head, :, dk:].astype(F32) + rough(prefix_ref[head, :, :dk], state)
         scale = lax.rsqrt(jnp.mean(raw * raw, axis=1, keepdims=True) + EPSILON)
         unit = raw * scale
         unit_ref[head] = unit
         weighted = weighted_ref[head]
-        along = scale * jnp.mean(raw * weighted, axis=1, keepdims=True)
-        dout = scale * (weighted - unit * along)
+        dout = scale * (weighted - unit * jnp.mean(unit * weighted, axis=1, keepdims=True))
         dout_ref[head] = dout
         back = rough(reach_t_ref[head], dout)
         back_ref[head] = back

time: 56.8 us -> 56.8 us (level)
  no operation moved by 1% of the time
where the time goes in v6:
time: 56.8 us; the launch traced here: 56.5 us
  starting transfers between devices  19 us (33%)
  waiting for transfers between devices  18.1 us (32%)
  Pallas kernels  12.7 us (22%)
  local copies, waits for them, and re-layouts  5.73 us (10%)
  between operations  0.85 us (1%)
    pallas_call x15, Pallas kernels, call(): pl.pallas_call(body, name=name, out_shape=tuple(outs), in_specs=[SMEM] *...  12.7 us
    all_to_all x1, starting transfers between devices, on_device(): lax.all_to_all(loaded.reshape(count, rows_each, local), 'seq', split_axis...  7.5 us
    all_to_all x1, waiting for transfers between devices, on_device(): lax.all_to_all(loaded.reshape(count, rows_each, local), 'seq', split_axis...  5.43 us
    ppermute x4, waiting for transfers between devices, corner_shift(): return lax.ppermute(x, ('seq', 'head'), pairs)  4.95 us
    unnamed x25, local copies, waits for them, and re-layouts  4.53 us
    ppermute x2, starting transfers between devices, seq_shift(): return lax.ppermute(x, 'seq', [(i, (i + by) % count) for i in range(count)])  4.01 us
    ppermute x3, waiting for transfers between devices, core_swap(): return lax.ppermute(x, 'seq', [(i, i ^ 1) for i in range(count)])  3.55 us
    ppermute x4, starting transfers between devices, corner_shift(): return lax.ppermute(x, ('seq', 'head'), pairs)  3.43 us
  transfers between devices with their start and end apart: 14, of which 10 were waited for; matrix products, arithmetic and copies ran while one was open for 6% of the time, Pallas kernels for 11%

profile of v6, /device:TPU:0, one launch (start us, length us, event | category | flops | bytes accessed | tf_op | source)
XLA Modules:
  0.0 56.5 jit_solution(30401401750322887)
XLA Ops:
  0.6 7.5 %all-to-all-start = ((bf16[16,8,1024]{2,1,0:T(8,128)(2,1)}), bf16[16,8,1024]{2,1,0:T(8,128)(2,1)S(1)}, u32[]{:S(2)}, u32[]{:S(2)}) async-start(bf16[16,8,1024]{2,1,0:T(8,128)(2,1)} %bitcast.9), calls=%async_computation | async-start | bytes 524288 | tf_op jit(solution)/shard_map/all_to_all | solution.py:579
  8.1 0.0 copy-start
  8.2 1.8 %copy.13 = bf16[2048,2]{1,0:T(8,128)(2,1)} copy(bf16[2048,2]{0,1:T(2,128)(2,1)} %param.16) | data formatting | bytes 16384 | tf_op args[5]
  10.0 1.2 %pad.4.refs_3_.refs_15_ = bf16[2048,128]{1,0:T(8,128)(2,1)S(1)} pad(bf16[2048,2]{1,0:T(8,128)(2,1)} %copy.13, bf16[]{:T(256)} %constant.2.clone.1), padding=0_0x0_126 | pad | bytes 532482 | tf_op jit(solution)/shard_map/jit(_pad)/pad | solution.py:576
  11.2 0.9 %prepare.1 = (bf16[4,128,128]{2,1,0:T(8,128)(2,1)S(1)}, bf16[4,128,8]{2,1,0:T(8,128)(2,1)S(1)}, bf16[8,128]{1,0:T(8,128)(2,1)S(1)}, bf16[2,128,128]{2,1,0:T(8,12...) custom-call(s32[1,16]{1,0:T(1,128)S(1)} %copy-done.8, ...), custom_call_target="tpu_custom_call" | custom-call | bytes 539648 | tf_op jit(solution)/shard_map/prepare/pallas_call | solution.py:517
  12.1 0.0 copy-start.5
  12.1 0.6 %copy-done.5 = bf16[2,128,8]{2,1,0:T(8,128)(2,1)} copy-done((bf16[2,128,8]{2,1,0:T(8,128)(2,1)}, bf16[2,128,8]{2,1,0:T(8,128)(2,1)S(1)}, u32[]{:S(2)}) %copy-start.5) | copy-done | bytes 4120
  12.8 5.4 %all-to-all-done = bf16[16,8,1024]{2,1,0:T(8,128)(2,1)S(1)} async-done(((bf16[16,8,1024]{2,1,0:T(8,128)(2,1)}), bf16[16,8,1024]{2,1,0:T(8,128)(2,1)S(1)}, u32[]{:S(2)}, u32[]{:S(2)}) %all-to-all-start) | async-done | bytes 262176 | tf_op jit(solution)/shard_map/all_to_all | solution.py:579
  18.2 1.5 %collective-permute-start.1 = (bf16[128,1024]{1,0:T(8,128)(2,1)S(1)}, bf16[128,1024]{1,0:T(8,128)(2,1)S(1)}, u32[]{:S(2)}, u32[]{:S(2)}) collective-permute-start(bf16[128,1024]{1,0:T(8,128)(2,1)S(1)} %bitcast.5), channel_id=1, source_target_pairs={{0,1},{1,0},{2,3},{3,2},{4,5},{5,4},{6,7},{7,6},{8,9},{9,8},{10,11... | collective-permute-start | bytes 786440 | tf_op jit(solution)/shard_map/ppermute | solution.py:560
  19.7 0.1 convolution_convert_fusion
  19.9 0.0 collective-permute-start
  19.9 0.0 copy-start.2
  19.9 1.2 %copy-done.2 = bf16[2048,256]{1,0:T(8,128)(2,1)S(1)} copy-done((bf16[2048,256]{1,0:T(8,128)(2,1)S(1)}, bf16[2048,256]{1,0:T(8,128)(2,1)}, u32[]{:S(2)}) %copy-start.2) | copy-done | bytes 1048600
  21.2 1.1 %flip.1 = (bf16[256,2048]{1,0:T(8,128)(2,1)S(1)}, bf16[256,2048]{1,0:T(8,128)(2,1)S(1)}, bf16[256,2048]{1,0:T(8,128)(2,1)S(1)}, bf16[128,2048]{1,0:T(8,128)(2,1)S(1)}) custom-call(bf16[2048,256]{1,0:T(8,128)(2,1)S(1)} %copy-done, bf16[2048,256]{1,0:T(8,128)(2,1)S(1)} %copy-done.1, bf16[2048,256]{1,0:T(8,128)(2,1)S(1)} %copy-done.2, ...), custom_call_target="tpu_custom_call" | custom-call | bytes 7340032 | tf_op jit(solution)/shard_map/flip/pallas_call | solution.py:517
  22.2 0.2 copy-done.3
  22.4 0.6 %project_own.1 = (f32[128,256]{1,0:T(8,128)S(1)}, f32[128,256]{1,0:T(8,128)S(1)}, f32[128,256]{1,0:T(8,128)S(1)}, f32[128,128]{1,0:T(8,128)S(1)}) custom-call(bf16[128,1024]{1,0:T(8,128)(2,1)S(1)} %bitcast.7, bf16[4,128,128]{2,1,0:T(8,128)(2,1)S(1)} %get-tuple-element.110.pick_ref.refs_10_, bf16[4,128,8]{2,1,0:T(8,128)(2,1)S(1)} %get-tuple-element.111.edge_ref.refs_11_, ...), custom_call_target="tpu_custom_call" | custom-call | flops 234881024 | bytes 4530176 | tf_op jit(solution)/shard_map/project_own/pallas_call | solution.py:517
  23.0 2.8 %collective-permute-done.halo_ref = bf16[8,1024]{1,0:T(8,128)(2,1)S(1)} collective-permute-done((bf16[8,1024]{1,0:T(8,128)(2,1)S(1)}, bf16[8,1024]{1,0:T(8,128)(2,1)S(1)}, u32[]{:S(2)}, u32[]{:S(2)}) %collective-permute-start) | collective-permute-done | bytes 16416 | tf_op jit(solution)/shard_map/ppermute | solution.py:556
  25.8 0.4 project_halo.1
  26.3 0.3 collective-permute-done.2.refs_9_
  26.6 2.8 %project.1 = (bf16[2,128,256]{2,1,0:T(8,128)(2,1)S(1)}, f32[2,128,128]{2,1,0:T(8,128)S(1)}, f32[2,128,128]{2,1,0:T(8,128)S(1)}, f32[2,128,128]{2,1,0:T(8,128)S(1...) custom-call(f32[5,128,128]{2,1,0:T(8,128)S(1)} %get-tuple-element.107.mask_ref, ...), custom_call_target="tpu_custom_call" | custom-call | flops 234881024 | bytes 5915648 | tf_op jit(solution)/shard_map/project/pallas_call | solution.py:517
  29.5 0.0 copy-start.4
  29.5 0.1 collective-permute-start.3
  29.5 1.3 %collective-permute-done.3.other_ref = bf16[2,128,256]{2,1,0:T(8,128)(2,1)S(1)} collective-permute-done((bf16[2,128,256]{2,1,0:T(8,128)(2,1)S(1)}, bf16[2,128,256]{2,1,0:T(8,128)(2,1)S(1)}, u32[]{:S(2)}, u32[]{:S(2)}) %collective-permute-start.3) | collective-permute-done | bytes 131104 | tf_op jit(solution)/shard_map/ppermute | solution.py:548
  30.9 0.2 join.1
  31.1 0.3 collective-permute-start.4
  31.4 0.3 collective-permute-start.5
  31.7 0.7 %copy-done.7 = f32[128]{0:T(128)S(1)} copy-done((f32[128]{0:T(128)S(1)}, f32[128]{0:T(128)}, u32[]{:S(2)}) %copy-start.7) | copy-done | bytes 536
  32.3 0.9 %local_terms.1 = (f32[2,128,128]{2,1,0:T(8,128)S(1)}, f32[2,128,128]{2,1,0:T(8,128)S(1)}, f32[2,128,128]{2,1,0:T(8,128)S(1)}, f32[2,128,128]{2,1,0:T(8,128)S(1)}...) custom-call(f32[5,128,128]{2,1,0:T(8,128)S(1)} %get-tuple-element.10, ...), custom_call_target="tpu_custom_call" | custom-call | flops 200000000 | bytes 2622464 | tf_op jit(solution)/shard_map/local_terms/pallas_call | solution.py:517
  33.2 2.5 %collective-permute-done.5.odd_ref.refs_1_ = bf16[2,128,128]{2,1,0:T(8,128)(2,1)S(1)} collective-permute-done((bf16[2,128,128]{2,1,0:T(8,128)(2,1)S(1)}, bf16[2,128,128]{2,1,0:T(8,128)(2,1)S(1)}, u32[]{:S(2)}, u32[]{:S(2)}) %collective-permute-start.5) | collective-permute-done | bytes 65568 | tf_op jit(solution)/shard_map/ppermute | solution.py:540
  35.7 0.1 collective-permute-start.6
  35.8 1.3 %collective-permute-done.6.refs_2_ = bf16[2,128,256]{2,1,0:T(8,128)(2,1)S(1)} collective-permute-done((bf16[2,128,256]{2,1,0:T(8,128)(2,1)S(1)}, bf16[2,128,256]{2,1,0:T(8,128)(2,1)S(1)}, u32[]{:S(2)}, u32[]{:S(2)}) %collective-permute-start.6) | collective-permute-done | bytes 131104 | tf_op jit(solution)/shard_map/ppermute | solution.py:548
  37.2 0.9 %outputs.1 = (f32[2,128,128]{2,1,0:T(8,128)S(1)}, f32[2,128,128]{2,1,0:T(8,128)S(1)}, f32[2,128,128]{2,1,0:T(8,128)S(1)}, f32[2,128,128]{2,1,0:T(8,128)S(1)}, bf16[2,128,128]{2,1,0:T(8,128)(2,1)S(1)}) custom-call(bf16[2,128,256]{2,1,0:T(8,128)(2,1)S(1)} %collective-permute-done.4.even_ref.refs_0_, ...), custom_call_target="tpu_custom_call" | custom-call | flops 200000000 | bytes 1572864 | tf_op jit(solution)/shard_map/outputs/pallas_call | solution.py:517
  38.1 0.2 collective-permute-start.7
  38.3 0.2 chain.1
  38.5 0.9 %collective-permute-done.7.other_ref = bf16[2,128,128]{2,1,0:T(8,128)(2,1)S(1)} collective-permute-done((bf16[2,128,128]{2,1,0:T(8,128)(2,1)S(1)}, bf16[2,128,128]{2,1,0:T(8,128)(2,1)S(1)}, u32[]{:S(2)}, u32[]{:S(2)}) %collective-permute-start.7) | collective-permute-done | bytes 65568 | tf_op jit(solution)/shard_map/ppermute | solution.py:548
  39.4 0.2 join_back.1
  39.6 2.2 %collective-permute-start.8 = (bf16[2,128,128]{2,1,0:T(8,128)(2,1)S(1)}, bf16[2,128,128]{2,1,0:T(8,128)(2,1)S(1)}, u32[]{:S(2)}, u32[]{:S(2)}) collective-permute-start(bf16[2,128,128]{2,1,0:T(8,128)(2,1)S(1)} %get-tuple-element.180), channel_id=1, source_target_pairs={{0,28},{2,30},{4,0},{6,2},{8,4},{10,6},{12,8},{14,10},{16,12},{18,... | collective-permute-start | bytes 196616 | tf_op jit(solution)/shard_map/ppermute | solution.py:544
  41.8 1.8 %collective-permute-start.9 = (bf16[2,128,128]{2,1,0:T(8,128)(2,1)S(1)}, bf16[2,128,128]{2,1,0:T(8,128)(2,1)S(1)}, u32[]{:S(2)}, u32[]{:S(2)}) collective-permute-start(bf16[2,128,128]{2,1,0:T(8,128)(2,1)S(1)} %get-tuple-element.181), channel_id=1, source_target_pairs={{0,24},{2,26},{4,28},{6,30},{8,0},{10,2},{12,4},{14,6},{16,8},{18,... | collective-permute-start | bytes 196616 | tf_op jit(solution)/shard_map/ppermute | solution.py:544
  43.6 1.9 %query_grad.1 = (bf16[128,256]{1,0:T(8,128)(2,1)}, bf16[128,256]{1,0:T(8,128)(2,1)S(1)}, f32[2,128,128]{2,1,0:T(8,128)S(1)}, f32[2,128,128]{2,1,0:T(8,128)S(1)},...) custom-call(f32[5,128,128]{2,1,0:T(8,128)S(1)} %get-tuple-element.107.mask_ref, ...), custom_call_target="tpu_custom_call" | custom-call | flops 200000000 | bytes 4194816 | tf_op jit(solution)/shard_map/query_grad/pallas_call | solution.py:517
  45.5 1.2 %collective-permute-done.9.refs_1_ = bf16[2,128,128]{2,1,0:T(8,128)(2,1)S(1)} collective-permute-done((bf16[2,128,128]{2,1,0:T(8,128)(2,1)S(1)}, bf16[2,128,128]{2,1,0:T(8,128)(2,1)S(1)}, u32[]{:S(2)}, u32[]{:S(2)}) %collective-permute-start.9) | collective-permute-done | bytes 65568 | tf_op jit(solution)/shard_map/ppermute | solution.py:544
  46.7 1.2 %key_grad.1 = (bf16[128,1024]{1,0:T(8,128)(2,1)S(1)}, bf16[8,1024]{1,0:T(8,128)(2,1)S(1)}, bf16[128,896]{1,0:T(8,128)(2,1)S(1)}) custom-call(f32[5,128,128]{2,1,0:T(8,128)S(1)} %get-tuple-element.107.mask_ref, bf16[2,128,128]{2,1,0:T(8,128)(2,1)S(1)} %collective-permute-done.8.refs_0_, bf16[2,128,128]{2,1,0:T(8,128)(2,1)S(1)} %collective-permute-done.9.refs_1_, ...), custom_call_target="tpu_custom_call" | custom-call | flops 200000000 | bytes 6471680 | tf_op jit(solution)/shard_map/key_grad/pallas_call | solution.py:517
  47.9 1.6 %collective-permute-start.10 = (bf16[128,1024]{1,0:T(8,128)(2,1)S(1)}, bf16[128,1024]{1,0:T(8,128)(2,1)S(1)}, u32[]{:S(2)}, u32[]{:S(2)}) collective-permute-start(bf16[128,1024]{1,0:T(8,128)(2,1)S(1)} %get-tuple-element.195), channel_id=1, source_target_pairs={{0,1},{1,0},{2,3},{3,2},{4,5},{5,4},{6,7},{7,6},{8,9},{9,8},{10,11... | collective-permute-start | bytes 786440 | tf_op jit(solution)/shard_map/ppermute | solution.py:560
  49.4 0.5 own_back.1
  49.9 1.6 %collective-permute-start.11 = (bf16[8,1024]{1,0:T(8,128)(2,1)S(1)}, bf16[8,1024]{1,0:T(8,128)(2,1)S(1)}, u32[]{:S(2)}, u32[]{:S(2)}) collective-permute-start(bf16[8,1024]{1,0:T(8,128)(2,1)S(1)} %get-tuple-element.196), channel_id=1, source_target_pairs={{0,30},{1,31},{2,0},{3,1},{4,2},{5,3},{6,4},{7,5},{8,6},{9,7},{10,... | collective-permute-start | bytes 49160 | tf_op jit(solution)/shard_map/ppermute | solution.py:556
  51.5 1.8 %collective-permute-start.12 = (bf16[8,1024]{1,0:T(8,128)(2,1)S(1)}, bf16[8,1024]{1,0:T(8,128)(2,1)S(1)}, u32[]{:S(2)}, u32[]{:S(2)}) collective-permute-start(bf16[8,1024]{1,0:T(8,128)(2,1)S(1)} %get-tuple-element.197), channel_id=1, source_target_pairs={{0,31},{1,30},{2,1},{3,0},{4,3},{5,2},{6,5},{7,4},{8,7},{9,6},{10,... | collective-permute-start | bytes 49160 | tf_op jit(solution)/shard_map/ppermute | solution.py:556
  53.3 1.8 %collective-permute-done.12.refs_2_ = bf16[8,1024]{1,0:T(8,128)(2,1)S(1)} collective-permute-done((bf16[8,1024]{1,0:T(8,128)(2,1)S(1)}, bf16[8,1024]{1,0:T(8,128)(2,1)S(1)}, u32[]{:S(2)}, u32[]{:S(2)}) %collective-permute-start.12) | collective-permute-done | bytes 16416 | tf_op jit(solution)/shard_map/ppermute | solution.py:556
  55.1 0.5 collective-permute-done.10.refs_0_
  55.5 0.9 %finish.1 = bf16[128,1024]{1,0:T(8,128)(2,1)} custom-call(bf16[2,128,128]{2,1,0:T(8,128)(2,1)S(1)} %get-tuple-element.178.pick_ref, bf16[2,128,8]{2,1,0:T(8,128)(2,1)S(1)} %copy-done.6, f32[128,1024]{1,0:T(8,128)S(1)} %get-tuple-element.194.mine_ref, bf16[128,1024]{1,0:T(8,128)(2,1)S(1)} %collective-permute-done.10.refs_0_, ...), custom_call_target="tpu_custom_call" | custom-call | flops 100000000 | bytes 1150976 | tf_op jit(solution)/shard_map/finish/pallas_call | solution.py:517
  (22 shorter events, 0.1 us)
Async XLA Ops:
  0.6 19.3 %copy-start.1 = (bf16[2048,256]{1,0:T(8,128)(2,1)S(1)}, bf16[2048,256]{1,0:T(8,128)(2,1)}, u32[]{:S(2)}) copy-start(bf16[2048,256]{1,0:T(8,128)(2,1)} %refs_13_.1) | copy-start | bytes 3145732
  0.6 17.6 %all-to-all-start = ((bf16[16,8,1024]{2,1,0:T(8,128)(2,1)}), bf16[16,8,1024]{2,1,0:T(8,128)(2,1)S(1)}, u32[]{:S(2)}, u32[]{:S(2)}) async-start(bf16[16,8,1024]{2,1,0:T(8,128)(2,1)} %bitcast.9), calls=%async_computation | async-start | bytes 524288 | tf_op jit(solution)/shard_map/all_to_all | solution.py:579
  8.1 11.8 %copy-start = (bf16[2048,256]{1,0:T(8,128)(2,1)S(1)}, bf16[2048,256]{1,0:T(8,128)(2,1)}, u32[]{:S(2)}) copy-start(bf16[2048,256]{1,0:T(8,128)(2,1)} %refs_12_.1) | copy-start | bytes 3145732
  10.0 1.2 %copy-start.8 = (s32[1,16]{1,0:T(1,128)S(1)}, s32[1,16]{1,0:T(1,128)}, u32[]{:S(2)}) copy-start(s32[1,16]{1,0:T(1,128)} %order_ref.1) | copy-start | bytes 196
  10.0 1.2 %copy-start.9 = (s32[16]{0:T(128)S(1)}, s32[16]{0:T(128)}, u32[]{:S(2)}) copy-start(s32[16]{0:T(128)} %clips_ref.1) | copy-start | bytes 196
  10.0 1.2 %copy-start.10 = (s32[4]{0:T(128)S(1)}, s32[4]{0:T(128)}, u32[]{:S(2)}) copy-start(s32[4]{0:T(128)} %delays_ref.1) | copy-start | bytes 52
  10.0 1.2 %copy-start.11 = (f32[2]{0:T(128)S(1)}, f32[2]{0:T(128)}, u32[]{:S(2)}) copy-start(f32[2]{0:T(128)} %cap_ref.1) | copy-start | bytes 28
  12.1 0.6 %copy-start.5 = (bf16[2,128,8]{2,1,0:T(8,128)(2,1)}, bf16[2,128,8]{2,1,0:T(8,128)(2,1)S(1)}, u32[]{:S(2)}) copy-start(bf16[2,128,8]{2,1,0:T(8,128)(2,1)S(1)} %get-tuple-element.179.edge_ref) | copy-start | bytes 12292
  18.2 8.4 %collective-permute-start.1 = (bf16[128,1024]{1,0:T(8,128)(2,1)S(1)}, bf16[128,1024]{1,0:T(8,128)(2,1)S(1)}, u32[]{:S(2)}, u32[]{:S(2)}) collective-permute-start(bf16[128,1024]{1,0:T(8,128)(2,1)S(1)} %bitcast.5), channel_id=1, source_target_pairs={{0,1},{1,0},{2,3},{3,2},{4,5},{5,4},{6,7},{7,6},{8,9},{9,8},{10,11... | collective-permute-start | bytes 786440 | tf_op jit(solution)/shard_map/ppermute | solution.py:560
  19.9 6.8 %collective-permute-start.2 = (bf16[8,1024]{1,0:T(8,128)(2,1)S(1)}, bf16[8,1024]{1,0:T(8,128)(2,1)S(1)}, u32[]{:S(2)}, u32[]{:S(2)}) collective-permute-start(bf16[8,1024]{1,0:T(8,128)(2,1)S(1)} %convolution_convert_fusion), channel_id=1, source_target_pairs={{0,3},{1,2},{2,5},{3,4},{4,7},{5,6},{6,9},{7,8},{8,11},{9,10},{10,... | collective-permute-start | bytes 49160 | tf_op jit(solution)/shard_map/ppermute | solution.py:556
  19.9 6.0 %collective-permute-start = (bf16[8,1024]{1,0:T(8,128)(2,1)S(1)}, bf16[8,1024]{1,0:T(8,128)(2,1)S(1)}, u32[]{:S(2)}, u32[]{:S(2)}) collective-permute-start(bf16[8,1024]{1,0:T(8,128)(2,1)S(1)} %convolution_convert_fusion), channel_id=1, source_target_pairs={{0,2},{1,3},{2,4},{3,5},{4,6},{5,7},{6,8},{7,9},{8,10},{9,11},{10,... | collective-permute-start | bytes 49160 | tf_op jit(solution)/shard_map/ppermute | solution.py:556
  19.9 1.2 %copy-start.2 = (bf16[2048,256]{1,0:T(8,128)(2,1)S(1)}, bf16[2048,256]{1,0:T(8,128)(2,1)}, u32[]{:S(2)}) copy-start(bf16[2048,256]{1,0:T(8,128)(2,1)} %refs_14_.1) | copy-start | bytes 3145732
  21.2 1.2 %copy-start.3 = (bf16[2048,256]{1,0:T(8,128)(2,1)S(1)}, bf16[2048,256]{1,0:T(8,128)(2,1)}, u32[]{:S(2)}) copy-start(bf16[2048,256]{1,0:T(8,128)(2,1)} %refs_14_.1) | copy-start | bytes 3145732
  29.5 2.2 %copy-start.4 = (bf16[128,256]{1,0:T(8,128)(2,1)S(1)}, bf16[128,256]{1,0:T(8,128)(2,1)}, u32[]{:S(2)}) copy-start(bf16[128,256]{1,0:T(8,128)(2,1)} %grad_ref.1) | copy-start | bytes 196612
  29.5 1.4 %collective-permute-start.3 = (bf16[2,128,256]{2,1,0:T(8,128)(2,1)S(1)}, bf16[2,128,256]{2,1,0:T(8,128)(2,1)S(1)}, u32[]{:S(2)}, u32[]{:S(2)}) collective-permute-start(bf16[2,128,256]{2,1,0:T(8,128)(2,1)S(1)} %get-tuple-element.134.own_ref), channel_id=1, source_target_pairs={{0,2},{2,0},{4,6},{6,4},{8,10},{10,8},{12,14},{14,12},{16,18},{18,... | collective-permute-start | bytes 393224 | tf_op jit(solution)/shard_map/ppermute | solution.py:548
  31.1 4.6 %collective-permute-start.4 = (bf16[2,128,256]{2,1,0:T(8,128)(2,1)S(1)}, bf16[2,128,256]{2,1,0:T(8,128)(2,1)S(1)}, u32[]{:S(2)}, u32[]{:S(2)}) collective-permute-start(bf16[2,128,256]{2,1,0:T(8,128)(2,1)S(1)} %get-tuple-element.135), channel_id=1, source_target_pairs={{0,4},{2,0},{4,8},{6,2},{8,12},{10,6},{12,16},{14,10},{16,20},{18,... | collective-permute-start | bytes 393224 | tf_op jit(solution)/shard_map/ppermute | solution.py:540
  31.4 4.3 %collective-permute-start.5 = (bf16[2,128,128]{2,1,0:T(8,128)(2,1)S(1)}, bf16[2,128,128]{2,1,0:T(8,128)(2,1)S(1)}, u32[]{:S(2)}, u32[]{:S(2)}) collective-permute-start(bf16[2,128,128]{2,1,0:T(8,128)(2,1)S(1)} %get-tuple-element.136), channel_id=1, source_target_pairs={{2,10},{0,2},{6,14},{4,6},{10,18},{8,0},{14,22},{12,4},{18,26},{16... | collective-permute-start | bytes 196616 | tf_op jit(solution)/shard_map/ppermute | solution.py:540
  31.7 0.7 %copy-start.7 = (f32[128]{0:T(128)S(1)}, f32[128]{0:T(128)}, u32[]{:S(2)}) copy-start(f32[128]{0:T(128)} %param.18) | copy-start | bytes 1540
  35.7 1.4 %collective-permute-start.6 = (bf16[2,128,256]{2,1,0:T(8,128)(2,1)S(1)}, bf16[2,128,256]{2,1,0:T(8,128)(2,1)S(1)}, u32[]{:S(2)}, u32[]{:S(2)}) collective-permute-start(bf16[2,128,256]{2,1,0:T(8,128)(2,1)S(1)} %give.1), channel_id=1, source_target_pairs={{0,2},{2,0},{4,6},{6,4},{8,10},{10,8},{12,14},{14,12},{16,18},{18,... | collective-permute-start | bytes 393224 | tf_op jit(solution)/shard_map/ppermute | solution.py:548
  38.1 1.3 %collective-permute-start.7 = (bf16[2,128,128]{2,1,0:T(8,128)(2,1)S(1)}, bf16[2,128,128]{2,1,0:T(8,128)(2,1)S(1)}, u32[]{:S(2)}, u32[]{:S(2)}) collective-permute-start(bf16[2,128,128]{2,1,0:T(8,128)(2,1)S(1)} %get-tuple-element.171), channel_id=1, source_target_pairs={{0,2},{2,0},{4,6},{6,4},{8,10},{10,8},{12,14},{14,12},{16,18},{18,... | collective-permute-start | bytes 196616 | tf_op jit(solution)/shard_map/ppermute | solution.py:548
  39.6 5.9 %collective-permute-start.8 = (bf16[2,128,128]{2,1,0:T(8,128)(2,1)S(1)}, bf16[2,128,128]{2,1,0:T(8,128)(2,1)S(1)}, u32[]{:S(2)}, u32[]{:S(2)}) collective-permute-start(bf16[2,128,128]{2,1,0:T(8,128)(2,1)S(1)} %get-tuple-element.180), channel_id=1, source_target_pairs={{0,28},{2,30},{4,0},{6,2},{8,4},{10,6},{12,8},{14,10},{16,12},{18,... | collective-permute-start | bytes 196616 | tf_op jit(solution)/shard_map/ppermute | solution.py:544
  41.8 4.9 %collective-permute-start.9 = (bf16[2,128,128]{2,1,0:T(8,128)(2,1)S(1)}, bf16[2,128,128]{2,1,0:T(8,128)(2,1)S(1)}, u32[]{:S(2)}, u32[]{:S(2)}) collective-permute-start(bf16[2,128,128]{2,1,0:T(8,128)(2,1)S(1)} %get-tuple-element.181), channel_id=1, source_target_pairs={{0,24},{2,26},{4,28},{6,30},{8,0},{10,2},{12,4},{14,6},{16,8},{18,... | collective-permute-start | bytes 196616 | tf_op jit(solution)/shard_map/ppermute | solution.py:544
  47.9 7.6 %collective-permute-start.10 = (bf16[128,1024]{1,0:T(8,128)(2,1)S(1)}, bf16[128,1024]{1,0:T(8,128)(2,1)S(1)}, u32[]{:S(2)}, u32[]{:S(2)}) collective-permute-start(bf16[128,1024]{1,0:T(8,128)(2,1)S(1)} %get-tuple-element.195), channel_id=1, source_target_pairs={{0,1},{1,0},{2,3},{3,2},{4,5},{5,4},{6,7},{7,6},{8,9},{9,8},{10,11... | collective-permute-start | bytes 786440 | tf_op jit(solution)/shard_map/ppermute | solution.py:560
  49.4 6.1 %copy-start.6 = (bf16[2,128,8]{2,1,0:T(8,128)(2,1)S(1)}, bf16[2,128,8]{2,1,0:T(8,128)(2,1)}, u32[]{:S(2)}) copy-start(bf16[2,128,8]{2,1,0:T(8,128)(2,1)} %copy-done.5) | copy-start | bytes 12292
  49.9 3.4 %collective-permute-start.11 = (bf16[8,1024]{1,0:T(8,128)(2,1)S(1)}, bf16[8,1024]{1,0:T(8,128)(2,1)S(1)}, u32[]{:S(2)}, u32[]{:S(2)}) collective-permute-start(bf16[8,1024]{1,0:T(8,128)(2,1)S(1)} %get-tuple-element.196), channel_id=1, source_target_pairs={{0,30},{1,31},{2,0},{3,1},{4,2},{5,3},{6,4},{7,5},{8,6},{9,7},{10,... | collective-permute-start | bytes 49160 | tf_op jit(solution)/shard_map/ppermute | solution.py:556
  51.5 3.6 %collective-permute-start.12 = (bf16[8,1024]{1,0:T(8,128)(2,1)S(1)}, bf16[8,1024]{1,0:T(8,128)(2,1)S(1)}, u32[]{:S(2)}, u32[]{:S(2)}) collective-permute-start(bf16[8,1024]{1,0:T(8,128)(2,1)S(1)} %get-tuple-element.197), channel_id=1, source_target_pairs={{0,31},{1,30},{2,1},{3,0},{4,3},{5,2},{6,5},{7,4},{8,7},{9,6},{10,... | collective-permute-start | bytes 49160 | tf_op jit(solution)/shard_map/ppermute | solution.py:556
